TPU v7x, 32 devices: a whole 2x2x4 slice. The times are simulated.
32 devices in a mesh: dp: 2 (over y), row: 4 (over z), col: 4 (over x, core).
Axes of the slice: x: 2, y: 2, z: 4, core: 2. Of those that a mesh axis runs over, the one named last changes fastest.
Arguments:
- tokens: bfloat16 [4728, 768], P(('dp', 'row')), may hold values from -6 to 6
- attn_gain: float32 [768], replicated, may hold values from 0.5 to 1.5
- attn_shift: float32 [768], replicated, may hold values from -3 to 3
- query_weight: bfloat16 [768, 768], P('col', 'row'), may hold values from -0.21875 to 0.21875
- key_weight: bfloat16 [768, 768], P('col', 'row'), may hold values from -0.21875 to 0.21875
- value_weight: bfloat16 [768, 768], P('col', 'row'), may hold values from -0.21875 to 0.21875
- query_bias: float32 [768], P('row'), may hold values from -3 to 3
- value_bias: float32 [768], P('row'), may hold values from -3 to 3
- proj_weight: bfloat16 [768, 768], P('row', 'col'), may hold values from -0.625 to 0.625
- proj_bias: float32 [768], P('col'), may hold values from -3 to 3
- mlp_gain: float32 [768], replicated, may hold values from 0.5 to 1.5
- mlp_shift: float32 [768], replicated, may hold values from -3 to 3
- expand_weight: bfloat16 [768, 3072], P('col', 'row'), may hold values from -0.21875 to 0.21875
- expand_bias: float32 [3072], P('row'), may hold values from -3 to 3
- shrink_weight: bfloat16 [768, 3072], P('col', 'row'), may hold values from -0.109375 to 0.109375
- shrink_bias: float32 [768], P('col'), may hold values from -3 to 3
- cotangent: bfloat16 [4728, 768], P(('dp', 'row')), may hold values from -6 to 6
Outputs:
- output: bfloat16 [4728, 768], P(('dp', 'row'))
- grad_tokens: bfloat16 [4728, 768], P(('dp', 'row'))
- grad_attn_gain: float32 [768], replicated
- grad_attn_shift: float32 [768], replicated
- grad_query_weight: float32 [768, 768], P('col', 'row')
- grad_key_weight: float32 [768, 768], P('col', 'row')
- grad_value_weight: float32 [768, 768], P('col', 'row')
- grad_query_bias: float32 [768], P('row')
- grad_value_bias: float32 [768], P('row')
- grad_proj_weight: float32 [768, 768], P('row', 'col')
- grad_proj_bias: float32 [768], P('col')
- grad_mlp_gain: float32 [768], replicated
- grad_mlp_shift: float32 [768], replicated
- grad_expand_weight: float32 [768, 3072], P('col', 'row')
- grad_expand_bias: float32 [3072], P('row')
- grad_shrink_weight: float32 [768, 3072], P('col', 'row')
- grad_shrink_bias: float32 [768], P('col')
All inputs are finite; a program needn't handle non-finite values.
Results may differ from a plain program's by a relative error of at most 0.015.
Values may be sent and summed in bfloat16 or wider, within the bound.
No kernel may reach another device: no remote copies, remote signals or barrier semaphores. Data moves between devices by JAX's collectives and lax.ppermute only.
A program may use at most 128 MiB of HBM per device.

v0:
```python
import jax
import jax.numpy as jnp
from jax import lax
from jax.experimental import pallas as pl
from jax.experimental.pallas import tpu as pltpu
from jax.sharding import PartitionSpec as P

HD = 64
SEQ = 197
PAD = 208
LANES = 128
EPS = 1e-06
BF = jnp.bfloat16
F32 = jnp.float32


def mirrored(index, size):
    out, step = 0, 1
    while step < size:
        out = out * 2 + (index // step) % 2
        step *= 2
    return out


class Grid:
    def __init__(self):
        self.rows = lax.axis_size("row")
        self.cols = lax.axis_size("col")
        self.dps = lax.axis_size("dp")
        assert self.rows == self.cols
        self.row = lax.axis_index("row")
        self.col = lax.axis_index("col")
        self.dp = lax.axis_index("dp")
        self.mirror = [mirrored(c, self.cols) for c in range(self.cols)]
        self.block = self.row ^ jnp.array(self.mirror, jnp.int32)[self.col]
        self.ids = jnp.stack([self.col, self.dp % 2]).astype(jnp.int32)

    def fetch(self, array, flip):
        pairs = []
        for r in range(self.rows):
            for c in range(self.cols):
                source = (r ^ self.mirror[c]) * self.cols + (c ^ flip)
                pairs.append((source, r * self.cols + c))
        return lax.ppermute(array, ("row", "col"), pairs)

    def give(self, array, flip):
        pairs = []
        for r in range(self.rows):
            for c in range(self.cols):
                target = (r ^ self.mirror[c]) * self.cols + (c ^ flip)
                pairs.append((r * self.cols + c, target))
        return lax.ppermute(array, ("row", "col"), pairs)

    def swap(self, array, axis, flip):
        size = lax.axis_size(axis)
        return lax.ppermute(array, axis, [(i, i ^ flip) for i in range(size)])


def after(value, *others):
    return lax.optimization_barrier((value, *others))[0]


def gather_block(grid, shard, first=None):
    half = shard.shape[0] // 2
    mine = lax.dynamic_slice_in_dim(shard, (grid.dp % 2) * half, half, 0)
    if first is not None:
        mine = after(mine, first)
    here = [grid.fetch(mine, flip) for flip in range(grid.cols)]
    there = [grid.swap(jnp.stack(here[i : i + 2]), "dp", 1) for i in range(0, grid.cols, 2)]
    return here, there


def reduce_block(grid, stay, away):
    got = grid.swap(away, "dp", 1)
    pair = (stay.astype(F32) + got.astype(F32)).astype(BF)
    total = None
    for flip in range(grid.cols):
        part = grid.give(pair[flip], flip).astype(F32)
        total = part if total is None else total + part
    step = 2
    while step < grid.dps:
        total = total + grid.swap(total.astype(BF), "dp", step).astype(F32)
        step *= 2
    total = total.astype(BF)
    back = grid.swap(total, "dp", 1)
    first = grid.dp % 2 == 0
    return jnp.concatenate([jnp.where(first, total, back), jnp.where(first, back, total)], 0).astype(F32)


def sum_cols(grid, mine, away):
    mine = mine + grid.swap(away, "col", 1)
    step = 2
    while step < grid.cols:
        mine = mine + grid.swap(mine, "col", step)
        step *= 2
    return mine, grid.swap(mine, "col", 1)


def sum_all(grid, array):
    for axis in ("col", "row", "dp"):
        step = 1
        while step < lax.axis_size(axis):
            array = array + grid.swap(array, axis, step)
            step *= 2
    return array


def sum_tokens(grid, array):
    for axis in ("row", "dp"):
        step = 1
        while step < lax.axis_size(axis):
            array = array + grid.swap(array, axis, step)
            step *= 2
    return array


def dot(left, right, contract):
    return lax.dot_general(left, right, ((contract[:1], contract[1:]), ((), ())), preferred_element_type=F32)


def normalize(values):
    mean_part = jnp.mean(values, axis=-1, keepdims=True)
    square_part = jnp.mean(values * values, axis=-1, keepdims=True)
    inverse = lax.rsqrt(square_part - mean_part * mean_part + EPS)
    return (values - mean_part) * inverse, inverse


def norm_back(grad_normed, centred, inverse, norm_gain):
    scaled = grad_normed * norm_gain
    first_mean = jnp.mean(scaled, axis=-1, keepdims=True)
    second_mean = jnp.mean(scaled * centred, axis=-1, keepdims=True)
    return inverse * (scaled - first_mean - centred * second_mean)


def gelu_parts(pre_act):
    cdf_value = 0.5 * (1.0 + lax.erf(pre_act * 0.7071067811865476))
    density = jnp.exp(-0.5 * pre_act * pre_act) * 0.3989422804014327
    return (pre_act * cdf_value, cdf_value + pre_act * density)


def columns_sum(values):
    return jnp.sum(values, axis=0, keepdims=True)


def low_lanes(shape):
    return lax.broadcasted_iota(jnp.int32, shape, len(shape) - 1) % LANES < HD


def low(values):
    return jnp.where(low_lanes(values.shape), values, jnp.zeros_like(values))


def high(values):
    return jnp.where(low_lanes(values.shape), jnp.zeros_like(values), values)


def place(ids, here, there, full):
    half = here[0].shape[0]
    pairs = [(ref, flip, ids[1]) for flip, ref in enumerate(here)]
    for i, ref in enumerate(there):
        pairs += [(ref.at[j], 2 * i + j, 1 - ids[1]) for j in range(2)]
    for ref, flip, side in pairs:
        start = pl.multiple_of(((ids[0] ^ flip) * 2 + side) * half, half)
        full[pl.ds(start, half), :] = ref[...]


def split_halves(ids, values, mine, away):
    half = values.shape[1] // 2
    left, right = values[:, :half], values[:, half:]
    first = ids[0] % 2 == 0
    mine[...] = jnp.where(first, left, right)
    away[...] = jnp.where(first, right, left)


def join_halves(ids, mine, other):
    first = ids[0] % 2 == 0
    a, b = mine[...].astype(F32), other[...].astype(F32)
    return jnp.concatenate([jnp.where(first, a, b), jnp.where(first, b, a)], axis=1)


def enter_kernel(tokens, cot, gain, shift, tokens_out, first_out, cot_out, sums):
    images = tokens.shape[0] // SEQ
    total = jnp.zeros((1, tokens.shape[1]), F32)
    for i in range(images):
        blank = jnp.zeros((PAD - SEQ, tokens.shape[1]), F32)
        here = pl.ds(i * PAD, PAD)
        rows = jnp.concatenate([tokens[pl.ds(i * SEQ, SEQ), :].astype(F32), blank], axis=0)
        tokens_out[here, :] = rows.astype(BF)
        centred, _ = normalize(rows)
        first_out[here, :] = (centred * gain[...] + shift[...]).astype(BF)
        rows = jnp.concatenate([cot[pl.ds(i * SEQ, SEQ), :].astype(F32), blank], axis=0)
        cot_out[here, :] = rows.astype(BF)
        total += columns_sum(rows)
    sums[...] = total


def attend_kernel(ids, first, h0, h1, h2, h3, t0, t1, bias, proj_bias, full, proj, joined, attended, probs, mine, away):
    @pl.when(pl.program_id(0) == 0)
    def _():
        place(ids, (h0, h1, h2, h3), (t0, t1), full)
        one, two, three = (full[:, i * LANES : (i + 1) * LANES].astype(F32) for i in (1, 3, 5))
        is_low = low_lanes(one.shape)
        proj[:, :LANES] = jnp.where(is_low, pltpu.roll(one, HD, 1), two).astype(BF)
        proj[:, LANES:] = low(pltpu.roll(three, HD, 1)).astype(BF)

    rows = (dot(first[...], full[...], (1, 0)) + bias[...]).astype(BF)
    query = rows[:, : 2 * LANES] * jnp.asarray(HD**-0.5, BF)
    joined[:, : 2 * LANES] = query
    joined[:, 2 * LANES :] = rows[:, 2 * LANES :]
    key, value = rows[:, 2 * LANES : 4 * LANES], rows[:, 4 * LANES :]
    is_key = lax.broadcasted_iota(jnp.int32, (PAD, PAD), 1) < SEQ
    outs = []
    for head in range(3):
        lanes = slice(head // 2 * LANES, (head // 2 + 1) * LANES)
        part = high if head == 1 else low
        scores = dot(query[:, lanes], part(key[:, lanes]), (1, 1))
        scores = jnp.where(is_key, scores, -1e30)
        weights = jnp.exp(scores - jnp.max(scores, axis=-1, keepdims=True))
        weights = (weights * (1.0 / jnp.sum(weights, axis=-1, keepdims=True))).astype(BF)
        probs[head] = weights
        outs.append(dot(weights, part(value[:, lanes]), (1, 0)))
    result = jnp.concatenate([outs[0] + outs[1], outs[2]], axis=1).astype(BF)
    attended[...] = result
    split_halves(ids, (dot(result, proj[...], (1, 1)) + proj_bias[...]).astype(BF), mine, away)


def mlp_kernel(
    ids, tokens, one, two, cot, gain, shift, bias, e0, e1, e2, e3, f0, f1, s0, s1, s2, s3, u0, u1,
    shrink, mid_out, second_out, hidden_out, pre_out, mine, away, sums, expand
):
    @pl.when(pl.program_id(0) == 0)
    def _():
        place(ids, (e0, e1, e2, e3), (f0, f1), expand)
        place(ids, (s0, s1, s2, s3), (u0, u1), shrink)
        sums[...] = jnp.zeros_like(sums)

    mid = tokens[...].astype(F32) + join_halves(ids, one, two)
    mid_out[...] = mid
    centred, _ = normalize(mid)
    second = (centred * gain[...] + shift[...]).astype(BF)
    second_out[...] = second
    activ, slope = gelu_parts(dot(second, expand[...], (1, 0)) + bias[...])
    hidden_out[...] = activ.astype(BF)
    grad_pre = dot(cot[...], shrink[...], (1, 0)) * slope
    sums[...] += columns_sum(grad_pre)
    grad_pre = grad_pre.astype(BF)
    pre_out[...] = grad_pre
    split_halves(ids, dot(grad_pre, expand[...], (1, 1)).astype(BF), mine, away)


def shrink_kernel(ids, hidden, shrink, bias, mine, away):
    split_halves(ids, (dot(hidden[...], shrink[...], (1, 1)) + bias[...]).astype(BF), mine, away)


def deal(ids, full, stay, away):
    half = stay.shape[1]
    for flip in range(stay.shape[0]):
        base = (ids[0] ^ flip) * 2
        stay[flip] = full[pl.ds(pl.multiple_of((base + ids[1]) * half, half), half), :]
        away[flip] = full[pl.ds(pl.multiple_of((base + 1 - ids[1]) * half, half), half), :]


def outer_kernel(ids, left, right, stay, away, full):
    full[...] = dot(left[...], right[...], (0, 0)).astype(BF)
    deal(ids, full, stay, away)


def joined_outer_kernel(ids, first, joined, grad_mid, attended, stay, away, full):
    full[...] = dot(first[...], joined[...], (0, 0)).astype(BF)
    other = dot(grad_mid[...], attended[...], (0, 0))
    turned = (pltpu.roll(other[:, :LANES], HD, 1), other[:, :LANES], pltpu.roll(other[:, LANES:], HD, 1))
    for i, values in enumerate(turned):
        lanes = pl.ds((2 * i + 1) * LANES, LANES)
        is_low = low_lanes(values.shape)
        full[:, lanes] = jnp.where(is_low, full[:, lanes].astype(F32), values).astype(BF)
    deal(ids, full, stay, away)


def attend_back_kernel(
    ids, one, two, mid, cot, gain, full, proj, joined, probs,
    grad_mid_out, grad_mid_b_out, grad_joined_out, mine, away, sums
):
    @pl.when(pl.program_id(0) == 0)
    def _():
        sums[...] = jnp.zeros_like(sums)

    grad_normed = join_halves(ids, one, two)
    centred, inverse = normalize(mid[...])
    grad_mid = cot[...].astype(F32) + norm_back(grad_normed, centred, inverse, gain[...])
    grad_mid_out[...] = grad_mid
    grad_mid_b = grad_mid.astype(BF)
    grad_mid_b_out[...] = grad_mid_b
    grad_att = dot(grad_mid_b, proj[...], (1, 0)).astype(BF)
    query, key, value = (joined[:, i * 2 * LANES : (i + 1) * 2 * LANES] for i in range(3))
    queries, keys, values = [], [], []
    for head in range(3):
        lanes = slice(head // 2 * LANES, (head // 2 + 1) * LANES)
        part = high if head == 1 else low
        weights = probs[head]
        wide = weights.astype(F32)
        grad_weights = dot(grad_att[:, lanes], part(value[:, lanes]), (1, 1))
        row_delta = jnp.sum(wide * grad_weights, axis=-1, keepdims=True)
        grad_scores = (wide * (grad_weights - row_delta)).astype(BF)
        queries.append(dot(grad_scores, part(key[:, lanes]), (1, 0)))
        keys.append(dot(grad_scores, part(query[:, lanes]), (0, 0)))
        values.append(dot(weights, part(grad_att[:, lanes]), (0, 0)))
    scale = HD**-0.5
    result = jnp.concatenate(
        [(queries[0] + queries[1]) * scale, queries[2] * scale, keys[0] + keys[1], keys[2], values[0] + values[1], values[2]],
        axis=1,
    )
    sums[0:1, :] += columns_sum(grad_normed * centred)
    sums[1:2, :] += columns_sum(grad_normed)
    sums[2:3, :] += columns_sum(grad_mid)
    sums[3:4, :] += columns_sum(result)
    result = result.astype(BF)
    grad_joined_out[...] = result
    split_halves(ids, dot(result, full[...], (1, 1)).astype(BF), mine, away)


def leave(values, out):
    images = values.shape[0] // PAD
    out[...] = jnp.concatenate([values[i * PAD : i * PAD + SEQ] for i in range(images)], axis=0).astype(out.dtype)


def output_kernel(ids, one, two, mid, out):
    leave(mid[...] + join_halves(ids, one, two), out)


def exit_kernel(ids, one, two, grad_mid, tokens, gain, out, sums):
    grad_normed = join_halves(ids, one, two)
    centred, inverse = normalize(tokens[...].astype(F32))
    leave(grad_mid[...] + norm_back(grad_normed, centred, inverse, gain[...]), out)
    sums[...] = jnp.concatenate([columns_sum(grad_normed * centred), columns_sum(grad_normed)], axis=0)


def run(kernel, ids, args, outs, flops, images=None, scratch=()):
    def spec(shape, how):
        if images is None:
            return pl.BlockSpec(memory_space=pltpu.VMEM)
        if how == 0:
            return pl.BlockSpec(shape, lambda i: (0,) * len(shape))
        return pl.BlockSpec((shape[0] // images, *shape[1:]), lambda i: (i,) + (0,) * (len(shape) - 1))

    in_specs = [spec(a.shape, how) for a, how in args]
    arrays = [a for a, _ in args]
    if ids is not None:
        in_specs = [pl.BlockSpec(memory_space=pltpu.SMEM)] + in_specs
        arrays = [ids] + arrays
    size = sum(a.size * a.dtype.itemsize for a in arrays)
    shapes = [jax.ShapeDtypeStruct(*s) for s, _ in outs]
    size += sum(s.size * s.dtype.itemsize for s in shapes)
    how = {} if images is None else {"grid": (images,)}
    return pl.pallas_call(
        kernel,
        out_shape=shapes,
        in_specs=in_specs,
        out_specs=[spec(s[0], how) for s, how in outs],
        scratch_shapes=list(scratch),
        compiler_params=pltpu.CompilerParams(vmem_limit_bytes=48 * 1024 * 1024),
        cost_estimate=pl.CostEstimate(flops=int(flops), bytes_accessed=int(size), transcendentals=0),
        **how,
    )(*arrays)


def on_device(
    tokens,
    attn_gain,
    attn_shift,
    query_weight,
    key_weight,
    value_weight,
    query_bias,
    value_bias,
    proj_weight,
    proj_bias,
    mlp_gain,
    mlp_shift,
    expand_weight,
    expand_bias,
    shrink_weight,
    shrink_bias,
    cotangent,
):
    grid = Grid()
    ids = grid.ids
    wide = query_weight.shape[1]
    model = tokens.shape[1]
    hidden_here = expand_weight.shape[1]
    images = tokens.shape[0] // SEQ
    rows = images * PAD
    heads = wide // HD
    half = model // 2
    assert heads == 3

    def pack(query, key, value, proj):
        parts = []
        for i, array in enumerate((query, key, value)):
            parts += [array, proj[..., i * HD : (i + 1) * HD]]
        return jnp.concatenate(parts, axis=-1)

    packed = pack(query_weight, key_weight, value_weight, proj_weight.T)
    biases = grid.fetch(jnp.concatenate([query_bias, value_bias, expand_bias]), 0)
    here, there = gather_block(grid, packed)
    e_here, e_there = gather_block(grid, expand_weight, here[1])
    s_here, s_there = gather_block(grid, shrink_weight, e_here[1])
    q_bias, v_bias, e_bias = biases[:wide], biases[wide : 2 * wide], biases[2 * wide :]
    nothing = jnp.zeros_like(q_bias)
    joined_bias = pack(q_bias, nothing, v_bias, nothing)

    def line(vector):
        return vector.reshape(1, -1)

    def spread(bias):
        own = jnp.arange(model) // bias.shape[0] == grid.col
        return line(jnp.where(own, jnp.tile(bias, grid.cols), 0.0))

    tokens_pad, first_in, cot, cot_sum = run(
        enter_kernel,
        None,
        [(tokens, 0), (cotangent, 0), (line(attn_gain), 0), (line(attn_shift), 0)],
        [(((rows, model), BF), 0), (((rows, model), BF), 0), (((rows, model), BF), 0), (((1, model), F32), 0)],
        rows * model * 20,
    )
    halves = [(((rows, half), BF), 1), (((rows, half), BF), 1)]
    full, proj, joined, attended, probs, mine, away = run(
        attend_kernel,
        ids,
        [(first_in, 1)] + [(a, 0) for a in (*here, *there, line(joined_bias), spread(proj_bias))],
        [
            (((model, model), BF), 0),
            (((model, 2 * LANES), BF), 0),
            (((rows, model), BF), 1),
            (((rows, 2 * LANES), BF), 1),
            (((heads * images, PAD, PAD), BF), 1),
        ]
        + halves,
        2 * rows * model * (model + 2 * wide),
        images,
    )
    one, two = sum_cols(grid, mine, away)
    shrink, mid, second_in, hidden, grad_pre, mine, away, pre_sum = run(
        mlp_kernel,
        ids,
        [(tokens_pad, 1), (one, 1), (two, 1), (cot, 1)]
        + [(line(a), 0) for a in (mlp_gain, mlp_shift, e_bias)]
        + [(a, 0) for a in (*e_here, *e_there, *s_here, *s_there)],
        [
            (((model, hidden_here), BF), 0),
            (((rows, model), F32), 1),
            (((rows, model), BF), 1),
            (((rows, hidden_here), BF), 1),
            (((rows, hidden_here), BF), 1),
        ]
        + halves
        + [(((1, hidden_here), F32), 0)],
        2 * rows * model * hidden_here * 3,
        images,
        [pltpu.VMEM((model, hidden_here), BF)],
    )
    one, two = sum_cols(grid, mine, away)

    def pieces(width):
        shape = (grid.cols, model // (2 * grid.cols), width)
        return [((shape, BF), 0), ((shape, BF), 0)]

    def outer(left, right):
        return run(
            outer_kernel,
            ids,
            [(left, 0), (right, 0)],
            pieces(right.shape[1]),
            2 * rows * model * right.shape[1],
            scratch=[pltpu.VMEM((model, right.shape[1]), BF)],
        )

    grad_shrink = reduce_block(grid, *outer(cot, hidden))
    grad_expand = reduce_block(grid, *outer(second_in, grad_pre))
    mine, away = run(
        shrink_kernel,
        ids,
        [(hidden, 1), (shrink, 0), (spread(shrink_bias), 0)],
        halves,
        2 * rows * model * hidden_here,
        images,
    )
    out_one, out_two = sum_cols(grid, mine, away)
    (output,) = run(
        output_kernel,
        ids,
        [(out_one, 0), (out_two, 0), (mid, 0)],
        [((tokens.shape, BF), 0)],
        rows * model,
    )

    grad_mid, grad_mid_b, grad_joined, mine, away, sums = run(
        attend_back_kernel,
        ids,
        [(one, 1), (two, 1), (mid, 1), (cot, 1), (line(mlp_gain), 0), (full, 0), (proj, 0), (joined, 1), (probs, 1)],
        [(((rows, model), F32), 1), (((rows, model), BF), 1), (((rows, model), BF), 1)]
        + halves
        + [(((4, model), F32), 0)],
        2 * rows * model * (model + 2 * wide),
        images,
    )
    packed_pieces = run(
        joined_outer_kernel,
        ids,
        [(first_in, 0), (grad_joined, 0), (grad_mid_b, 0), (attended, 0)],
        pieces(model),
        2 * rows * model * model,
        scratch=[pltpu.VMEM((model, model), BF)],
    )
    one, two = sum_cols(grid, mine, away)
    grad_packed = reduce_block(grid, *packed_pieces)
    grad_tokens, late = run(
        exit_kernel,
        ids,
        [(one, 0), (two, 0), (grad_mid, 0), (tokens_pad, 0), (line(attn_gain), 0)],
        [((tokens.shape, BF), 0), (((2, model), F32), 0)],
        rows * model * 20,
    )
    late = sum_tokens(grid, late)

    step = wide + HD
    blocks = jnp.concatenate([sums[3, :wide], sums[3, 2 * step : 2 * step + wide], pre_sum[0]])
    slots = jnp.where(jnp.arange(grid.rows)[:, None] == grid.block, blocks[None], 0.0)
    early = jnp.concatenate([(sums[:3] / grid.cols).reshape(-1), cot_sum[0] / grid.cols, slots.reshape(-1)])
    early = sum_all(grid, early.reshape(-1, LANES)).reshape(-1)
    whole = early[: 4 * model].reshape(4, model)
    blocks = lax.dynamic_index_in_dim(early[4 * model :].reshape(grid.rows, -1), grid.row, 0, keepdims=False)

    def own_columns(vector):
        width = vector.shape[0] // grid.cols
        return lax.dynamic_slice_in_dim(vector, grid.col * width, width, 0)

    grad_proj = jnp.concatenate([grad_packed[:, i * step + wide : (i + 1) * step] for i in range(3)], axis=1).T
    return (
        output,
        grad_tokens,
        late[0],
        late[1],
        grad_packed[:, :wide],
        grad_packed[:, step : step + wide],
        grad_packed[:, 2 * step : 2 * step + wide],
        blocks[:wide],
        blocks[wide : 2 * wide],
        grad_proj,
        own_columns(whole[2]),
        whole[0],
        whole[1],
        grad_expand,
        blocks[2 * wide :],
        grad_shrink,
        own_columns(whole[3]),
    )


def solution(mesh):
    placed = (
        P(("dp", "row"), None),
        P(),
        P(),
        P("col", "row"),
        P("col", "row"),
        P("col", "row"),
        P("row"),
        P("row"),
        P("row", "col"),
        P("col"),
        P(),
        P(),
        P("col", "row"),
        P("row"),
        P("col", "row"),
        P("col"),
        P(("dp", "row"), None),
    )
    return jax.shard_map(
        on_device,
        mesh=mesh,
        in_specs=placed,
        out_specs=(
            P(("dp", "row"), None),
            P(("dp", "row"), None),
            P(),
            P(),
            P("col", "row"),
            P("col", "row"),
            P("col", "row"),
            P("row"),
            P("row"),
            P("row", "col"),
            P("col"),
            P(),
            P(),
            P("col", "row"),
            P("row"),
            P("col", "row"),
            P("col"),
        ),
        check_vma=False,
    )
```

profile of v0, /device:TPU:0, one launch (start us, length us, event | category | flops | bytes accessed | tf_op | source)
XLA Modules:
  0.0 256.3 jit_solution(10465852873001496573)
XLA Ops:
  3.2 5.5 %collective-permute-start.3 = (bf16[96,768]{1,0:T(8,128)(2,1)S(1)}, bf16[96,768]{1,0:T(8,128)(2,1)S(1)}, u32[]{:S(2)}, u32[]{:S(2)}) collective-permute-start(bf16[96,768]{1,0:T(8,128)(2,1)S(1)} %constant_dynamic-slice_fusion.3), channel_id=1, source_target_pairs={{3,0},{10,1},{5,2},{12,3},{7,4},{14,5},{1,6},{8,7},{11,8},{2,9},{1... | collective-permute-start | bytes 442376 | tf_op jit(solution)/shard_map/ppermute | solution.py:44
  12.9 3.2 %collective-permute-done.2.h2 = bf16[96,768]{1,0:T(8,128)(2,1)S(1)} collective-permute-done((bf16[96,768]{1,0:T(8,128)(2,1)S(1)}, bf16[96,768]{1,0:T(8,128)(2,1)S(1)}, u32[]{:S(2)}, u32[]{:S(2)}) %collective-permute-start.2) | collective-permute-done | bytes 147488 | tf_op jit(solution)/shard_map/ppermute | solution.py:44
  24.5 5.5 %collective-permute-done.4.t0 = bf16[2,96,768]{2,1,0:T(8,128)(2,1)} collective-permute-done((bf16[2,96,768]{2,1,0:T(8,128)(2,1)}, bf16[2,96,768]{2,1,0:T(8,128)(2,1)}, u32[]{:S(2)}, u32[]{:S(2)}) %collective-permute-start.4) | collective-permute-done | bytes 294944 | tf_op jit(solution)/shard_map/ppermute | solution.py:56
  34.6 5.9 %shard_map.306 = (bf16[768,768]{1,0:T(8,128)(2,1)}, bf16[768,256]{1,0:T(8,128)(2,1)S(1)}, bf16[624,768]{1,0:T(8,128)(2,1)S(1)}, bf16[624,256]{1,0:T(8,128)(2,1)S...) custom-call(s32[2]{0:T(128)S(1)} %pad_add_fusion.ids, ...), custom_call_target="tpu_custom_call" | custom-call | flops 1104150528 | bytes 6732296 | tf_op jit(solution)/shard_map/pallas_call | solution.py:354
  40.5 3.2 %collective-permute-start.7 = (bf16[624,384]{1,0:T(8,128)(2,1)S(1)}, bf16[624,384]{1,0:T(8,128)(2,1)S(1)}, u32[]{:S(2)}, u32[]{:S(2)}) collective-permute-start(bf16[624,384]{1,0:T(8,128)(2,1)S(1)} %get-tuple-element.57), channel_id=1, source_target_pairs={{0,1},{1,0},{2,3},{3,2},{4,5},{5,4},{6,7},{7,6},{8,9},{9,8},{10,11... | collective-permute-start | bytes 1437704 | tf_op jit(solution)/shard_map/ppermute | solution.py:56
  48.9 3.9 %collective-permute-start.13 = (bf16[96,768]{1,0:T(8,128)(2,1)S(1)}, bf16[96,768]{1,0:T(8,128)(2,1)S(1)}, u32[]{:S(2)}, u32[]{:S(2)}) collective-permute-start(bf16[96,768]{1,0:T(8,128)(2,1)S(1)} %constant_dynamic-slice_fusion.2), channel_id=1, source_target_pairs={{3,0},{10,1},{5,2},{12,3},{7,4},{14,5},{1,6},{8,7},{11,8},{2,9},{1... | collective-permute-start | bytes 442376 | tf_op jit(solution)/shard_map/ppermute | solution.py:44
  57.8 3.6 %collective-permute-done.13.e3 = bf16[96,768]{1,0:T(8,128)(2,1)S(1)} collective-permute-done((bf16[96,768]{1,0:T(8,128)(2,1)S(1)}, bf16[96,768]{1,0:T(8,128)(2,1)S(1)}, u32[]{:S(2)}, u32[]{:S(2)}) %collective-permute-start.13) | collective-permute-done | bytes 147488 | tf_op jit(solution)/shard_map/ppermute | solution.py:44
  61.4 3.5 %collective-permute-done.12.e2 = bf16[96,768]{1,0:T(8,128)(2,1)S(1)} collective-permute-done((bf16[96,768]{1,0:T(8,128)(2,1)S(1)}, bf16[96,768]{1,0:T(8,128)(2,1)S(1)}, u32[]{:S(2)}, u32[]{:S(2)}) %collective-permute-start.12) | collective-permute-done | bytes 147488 | tf_op jit(solution)/shard_map/ppermute | solution.py:44
  66.3 3.4 %collective-permute-done.8 = bf16[624,384]{1,0:T(8,128)(2,1)S(1)} collective-permute-done((bf16[624,384]{1,0:T(8,128)(2,1)S(1)}, bf16[624,384]{1,0:T(8,128)(2,1)S(1)}, u32[]{:S(2)}, u32[]{:S(2)}) %collective-permute-start.8) | collective-permute-done | bytes 479264 | tf_op jit(solution)/shard_map/ppermute | solution.py:56
  78.8 5.9 %collective-permute-done.14.f0 = bf16[2,96,768]{2,1,0:T(8,128)(2,1)} collective-permute-done((bf16[2,96,768]{2,1,0:T(8,128)(2,1)}, bf16[2,96,768]{2,1,0:T(8,128)(2,1)}, u32[]{:S(2)}, u32[]{:S(2)}) %collective-permute-start.14) | collective-permute-done | bytes 294944 | tf_op jit(solution)/shard_map/ppermute | solution.py:56
  84.8 6.3 %collective-permute-done.21.u1 = bf16[2,96,768]{2,1,0:T(8,128)(2,1)} collective-permute-done((bf16[2,96,768]{2,1,0:T(8,128)(2,1)}, bf16[2,96,768]{2,1,0:T(8,128)(2,1)}, u32[]{:S(2)}, u32[]{:S(2)}) %collective-permute-start.21) | collective-permute-done | bytes 294944 | tf_op jit(solution)/shard_map/ppermute | solution.py:56
  91.1 6.3 %collective-permute-done.20.u0 = bf16[2,96,768]{2,1,0:T(8,128)(2,1)} collective-permute-done((bf16[2,96,768]{2,1,0:T(8,128)(2,1)}, bf16[2,96,768]{2,1,0:T(8,128)(2,1)}, u32[]{:S(2)}, u32[]{:S(2)}) %collective-permute-start.20) | collective-permute-done | bytes 294944 | tf_op jit(solution)/shard_map/ppermute | solution.py:56
  105.7 6.6 %shard_map.307 = (bf16[768,768]{1,0:T(8,128)(2,1)}, f32[624,768]{1,0:T(8,128)}, bf16[624,768]{1,0:T(8,128)(2,1)S(1)}, bf16[624,768]{1,0:T(8,128)(2,1)S(1)}, bf16...) custom-call(s32[2]{0:T(128)S(1)} %pad_add_fusion.ids, ...), custom_call_target="tpu_custom_call" | custom-call | flops 2208301056 | bytes 12177416 | tf_op jit(solution)/shard_map/pallas_call | solution.py:354
  112.4 2.6 %shard_map.314 = (bf16[4,96,768]{2,1,0:T(8,128)(2,1)S(1)}, bf16[4,96,768]{2,1,0:T(8,128)(2,1)}) custom-call(s32[2]{0:T(128)S(1)} %pad_add_fusion.ids, bf16[624,768]{1,0:T(8,128)(2,1)S(1)} %copy-done.4, bf16[624,768]{1,0:T(8,128)(2,1)S(1)} %get-tuple-element.61.hidden.right), custom_call_target="tpu_custom_call" | custom-call | flops 736100352 | bytes 3096584 | tf_op jit(solution)/shard_map/pallas_call | solution.py:354
  117.4 3.0 %shard_map.308 = (bf16[624,384]{1,0:T(8,128)(2,1)S(1)}, bf16[624,384]{1,0:T(8,128)(2,1)}) custom-call(s32[2]{0:T(128)S(1)} %pad_add_fusion.ids, bf16[624,768]{1,0:T(8,128)(2,1)S(1)} %get-tuple-element.61.hidden.right, bf16[768,768]{1,0:T(8,128)(2,1)S(1)} %copy-done.53, f32[1,768]{1,0:T(1,128)S(1)} %compare_select_fusion.bias), custom_call_target="tpu_custom_call" | custom-call | flops 736100352 | bytes 3099656 | tf_op jit(solution)/shard_map/pallas_call | solution.py:354
  125.8 2.6 %shard_map.313 = (bf16[4,96,768]{2,1,0:T(8,128)(2,1)S(1)}, bf16[4,96,768]{2,1,0:T(8,128)(2,1)}) custom-call(s32[2]{0:T(128)S(1)} %pad_add_fusion.ids, bf16[624,768]{1,0:T(8,128)(2,1)S(1)} %copy-done.55, bf16[624,768]{1,0:T(8,128)(2,1)S(1)} %copy-done.56), custom_call_target="tpu_custom_call" | custom-call | flops 736100352 | bytes 3096584 | tf_op jit(solution)/shard_map/pallas_call | solution.py:354
  129.8 2.2 add.126
  137.2 2.8 %collective-permute-start.52 = (bf16[96,768]{1,0:T(8,128)(2,1)}, bf16[96,768]{1,0:T(8,128)(2,1)}, u32[]{:S(2)}, u32[]{:S(2)}) collective-permute-start(bf16[96,768]{1,0:T(8,128)(2,1)} %get-tuple-element.110), channel_id=1, source_target_pairs={{0,0},{1,9},{2,6},{3,15},{4,4},{5,13},{6,2},{7,11},{8,8},{9,1},{10... | collective-permute-start | bytes 442376 | tf_op jit(solution)/shard_map/ppermute | solution.py:52
  140.9 17.8 %collective-permute-done.26 = bf16[624,384]{1,0:T(8,128)(2,1)S(1)} collective-permute-done((bf16[624,384]{1,0:T(8,128)(2,1)S(1)}, bf16[624,384]{1,0:T(8,128)(2,1)S(1)}, u32[]{:S(2)}, u32[]{:S(2)}) %collective-permute-start.26) | collective-permute-done | bytes 479264 | tf_op jit(solution)/shard_map/ppermute | solution.py:56
  161.5 8.5 %shard_map.310 = (f32[624,768]{1,0:T(8,128)}, bf16[624,768]{1,0:T(8,128)(2,1)S(1)}, bf16[624,768]{1,0:T(8,128)(2,1)S(1)}, bf16[624,384]{1,0:T(8,128)(2,1)S(1)}, ...) custom-call(s32[2]{0:T(128)S(1)} %pad_add_fusion.ids, bf16[624,384]{1,0:T(8,128)(2,1)S(1)} %add.129.one, ...), custom_call_target="tpu_custom_call" | custom-call | flops 1104150528 | bytes 11951624 | tf_op jit(solution)/shard_map/pallas_call | solution.py:354
  174.6 6.2 %collective-permute-start.49 = (bf16[96,768]{1,0:T(8,128)(2,1)}, bf16[96,768]{1,0:T(8,128)(2,1)S(1)}, u32[]{:S(2)}, u32[]{:S(2)}) collective-permute-start(bf16[96,768]{1,0:T(8,128)(2,1)} %get-tuple-element.115), channel_id=1, source_target_pairs={{0,3},{1,10},{2,5},{3,12},{4,7},{5,14},{6,1},{7,8},{8,11},{9,2},{1... | collective-permute-start | bytes 442376 | tf_op jit(solution)/shard_map/ppermute | solution.py:52
  182.1 2.4 collective-permute-start.41
  185.7 2.9 %shard_map.312 = (bf16[4,96,768]{2,1,0:T(8,128)(2,1)S(1)}, bf16[4,96,768]{2,1,0:T(8,128)(2,1)}) custom-call(s32[2]{0:T(128)S(1)} %pad_add_fusion.ids, bf16[624,768]{1,0:T(8,128)(2,1)S(1)} %get-tuple-element.55.first, bf16[624,768]{1,0:T(8,128)(2,1)S(1)} %copy-done.11, bf16[624,768]{1,0:T(8,128)(2,1)S(1)} %copy-done.9, ...), custom_call_target="tpu_custom_call" | custom-call | flops 736100352 | bytes 4374536 | tf_op jit(solution)/shard_map/pallas_call | solution.py:354
  192.3 3.8 %collective-permute-done.47 = bf16[96,768]{1,0:T(8,128)(2,1)S(1)} collective-permute-done((bf16[96,768]{1,0:T(8,128)(2,1)S(1)}, bf16[96,768]{1,0:T(8,128)(2,1)S(1)}, u32[]{:S(2)}, u32[]{:S(2)}) %collective-permute-start.47) | collective-permute-done | bytes 147488 | tf_op jit(solution)/shard_map/ppermute | solution.py:52
  196.2 3.8 %collective-permute-done.42 = f32[60,128]{1,0:T(8,128)S(1)} collective-permute-done((f32[60,128]{1,0:T(8,128)S(1)}, f32[60,128]{1,0:T(8,128)S(1)}, u32[]{:S(2)}, u32[]{:S(2)}) %collective-permute-start.42) | collective-permute-done | bytes 30752 | tf_op jit(solution)/shard_map/ppermute | solution.py:56
  202.0 9.4 %collective-permute-done.50 = bf16[96,768]{1,0:T(8,128)(2,1)S(1)} collective-permute-done((bf16[96,768]{1,0:T(8,128)(2,1)S(1)}, bf16[96,768]{1,0:T(8,128)(2,1)S(1)}, u32[]{:S(2)}, u32[]{:S(2)}) %collective-permute-start.50) | collective-permute-done | bytes 147488 | tf_op jit(solution)/shard_map/ppermute | solution.py:56
  214.7 2.5 collective-permute-start.29
  218.2 2.3 collective-permute-start.38
  225.8 6.3 %collective-permute-done.38 = bf16[96,768]{1,0:T(8,128)(2,1)S(1)} collective-permute-done((bf16[96,768]{1,0:T(8,128)(2,1)S(1)}, bf16[96,768]{1,0:T(8,128)(2,1)S(1)}, u32[]{:S(2)}, u32[]{:S(2)}) %collective-permute-start.38) | collective-permute-done | bytes 147488 | tf_op jit(solution)/shard_map/ppermute | solution.py:52
  240.9 3.0 %shard_map.311 = (bf16[591,768]{1,0:T(8,128)(2,1)}, f32[2,768]{1,0:T(2,128)S(1)}) custom-call(s32[2]{0:T(128)S(1)} %pad_add_fusion.ids, bf16[624,384]{1,0:T(8,128)(2,1)S(1)} %add.131.one, bf16[624,384]{1,0:T(8,128)(2,1)S(1)} %collective-permute-done.30.two, f32[624,768]{1,0:T(8,128)S(1)} %copy-done.2, bf16[624,768]{1,0:T(8,128)(2,1)S(1)} %copy-done.7, ...), custom_call_target="tpu_custom_call" | custom-call | flops 9584640 | bytes 4750856 | tf_op jit(solution)/shard_map/pallas_call | solution.py:354
  244.7 2.8 %collective-permute-done.31 = f32[2,768]{1,0:T(2,128)S(1)} collective-permute-done((f32[2,768]{1,0:T(2,128)S(1)}, f32[2,768]{1,0:T(2,128)S(1)}, u32[]{:S(2)}, u32[]{:S(2)}) %collective-permute-start.31) | collective-permute-done | bytes 6176 | tf_op jit(solution)/shard_map/ppermute | solution.py:56
  248.1 4.0 %collective-permute-done.32 = f32[2,768]{1,0:T(2,128)S(1)} collective-permute-done((f32[2,768]{1,0:T(2,128)S(1)}, f32[2,768]{1,0:T(2,128)S(1)}, u32[]{:S(2)}, u32[]{:S(2)}) %collective-permute-start.32) | collective-permute-done | bytes 6176 | tf_op jit(solution)/shard_map/ppermute | solution.py:56
  (316 shorter events, 102.4 us)
Async XLA Ops:
  10.3 13.2 %collective-permute-start.6 = (f32[1152]{0:T(1024)S(1)}, f32[1152]{0:T(1024)S(1)}, u32[]{:S(2)}, u32[]{:S(2)}) collective-permute-start(f32[1152]{0:T(1024)S(1)} %concatenate.28), channel_id=1, source_target_pairs={{0,0},{9,1},{6,2},{15,3},{4,4},{13,5},{2,6},{11,7},{8,8},{1,9},{14... | collective-permute-start | bytes 13832 | tf_op jit(solution)/shard_map/ppermute | solution.py:44
  45.3 24.5 %collective-permute-start.8 = (bf16[624,384]{1,0:T(8,128)(2,1)S(1)}, bf16[624,384]{1,0:T(8,128)(2,1)S(1)}, u32[]{:S(2)}, u32[]{:S(2)}) collective-permute-start(bf16[624,384]{1,0:T(8,128)(2,1)S(1)} %add.124), channel_id=1, source_target_pairs={{0,2},{1,3},{2,0},{3,1},{4,6},{5,7},{6,4},{7,5},{8,10},{9,11},{10,... | collective-permute-start | bytes 1437704 | tf_op jit(solution)/shard_map/ppermute | solution.py:56
  48.9 12.5 %collective-permute-start.13 = (bf16[96,768]{1,0:T(8,128)(2,1)S(1)}, bf16[96,768]{1,0:T(8,128)(2,1)S(1)}, u32[]{:S(2)}, u32[]{:S(2)}) collective-permute-start(bf16[96,768]{1,0:T(8,128)(2,1)S(1)} %constant_dynamic-slice_fusion.2), channel_id=1, source_target_pairs={{3,0},{10,1},{5,2},{12,3},{7,4},{14,5},{1,6},{8,7},{11,8},{2,9},{1... | collective-permute-start | bytes 442376 | tf_op jit(solution)/shard_map/ppermute | solution.py:44
  52.8 12.1 %collective-permute-start.12 = (bf16[96,768]{1,0:T(8,128)(2,1)S(1)}, bf16[96,768]{1,0:T(8,128)(2,1)S(1)}, u32[]{:S(2)}, u32[]{:S(2)}) collective-permute-start(bf16[96,768]{1,0:T(8,128)(2,1)S(1)} %constant_dynamic-slice_fusion.2), channel_id=1, source_target_pairs={{2,0},{11,1},{4,2},{13,3},{6,4},{15,5},{0,6},{9,7},{10,8},{3,9},{1... | collective-permute-start | bytes 442376 | tf_op jit(solution)/shard_map/ppermute | solution.py:44
  53.4 18.0 %collective-permute-start.19 = (bf16[96,768]{1,0:T(8,128)(2,1)S(1)}, bf16[96,768]{1,0:T(8,128)(2,1)S(1)}, u32[]{:S(2)}, u32[]{:S(2)}) collective-permute-start(bf16[96,768]{1,0:T(8,128)(2,1)S(1)} %constant_dynamic-slice_fusion.1), channel_id=1, source_target_pairs={{3,0},{10,1},{5,2},{12,3},{7,4},{14,5},{1,6},{8,7},{11,8},{2,9},{1... | collective-permute-start | bytes 442376 | tf_op jit(solution)/shard_map/ppermute | solution.py:44
  55.3 16.6 %collective-permute-start.18 = (bf16[96,768]{1,0:T(8,128)(2,1)S(1)}, bf16[96,768]{1,0:T(8,128)(2,1)S(1)}, u32[]{:S(2)}, u32[]{:S(2)}) collective-permute-start(bf16[96,768]{1,0:T(8,128)(2,1)S(1)} %constant_dynamic-slice_fusion.1), channel_id=1, source_target_pairs={{2,0},{11,1},{4,2},{13,3},{6,4},{15,5},{0,6},{9,7},{10,8},{3,9},{1... | collective-permute-start | bytes 442376 | tf_op jit(solution)/shard_map/ppermute | solution.py:44
  61.4 14.4 %collective-permute-start.17 = (bf16[96,768]{1,0:T(8,128)(2,1)S(1)}, bf16[96,768]{1,0:T(8,128)(2,1)S(1)}, u32[]{:S(2)}, u32[]{:S(2)}) collective-permute-start(bf16[96,768]{1,0:T(8,128)(2,1)S(1)} %constant_dynamic-slice_fusion.1), channel_id=1, source_target_pairs={{1,0},{8,1},{7,2},{14,3},{5,4},{12,5},{3,6},{10,7},{9,8},{0,9},{15... | collective-permute-start | bytes 442376 | tf_op jit(solution)/shard_map/ppermute | solution.py:44
  64.9 12.5 %collective-permute-start.16 = (bf16[96,768]{1,0:T(8,128)(2,1)S(1)}, bf16[96,768]{1,0:T(8,128)(2,1)S(1)}, u32[]{:S(2)}, u32[]{:S(2)}) collective-permute-start(bf16[96,768]{1,0:T(8,128)(2,1)S(1)} %constant_dynamic-slice_fusion.1), channel_id=1, source_target_pairs={{0,0},{9,1},{6,2},{15,3},{4,4},{13,5},{2,6},{11,7},{8,8},{1,9},{14... | collective-permute-start | bytes 442376 | tf_op jit(solution)/shard_map/ppermute | solution.py:44
  71.4 13.4 %collective-permute-start.14 = (bf16[2,96,768]{2,1,0:T(8,128)(2,1)}, bf16[2,96,768]{2,1,0:T(8,128)(2,1)}, u32[]{:S(2)}, u32[]{:S(2)}) collective-permute-start(bf16[2,96,768]{2,1,0:T(8,128)(2,1)} %pad_maximum_fusion.2), channel_id=1, source_target_pairs={{0,16},{16,0},{1,17},{17,1},{2,18},{18,2},{3,19},{19,3},{4,20},{20... | collective-permute-start | bytes 884744 | tf_op jit(solution)/shard_map/ppermute | solution.py:56
  72.0 25.4 %collective-permute-start.9 = (bf16[624,384]{1,0:T(8,128)(2,1)S(1)}, bf16[624,384]{1,0:T(8,128)(2,1)}, u32[]{:S(2)}, u32[]{:S(2)}) collective-permute-start(bf16[624,384]{1,0:T(8,128)(2,1)S(1)} %add.125.one), channel_id=1, source_target_pairs={{0,1},{1,0},{2,3},{3,2},{4,5},{5,4},{6,7},{7,6},{8,9},{9,8},{10,11... | collective-permute-start | bytes 1437704 | tf_op jit(solution)/shard_map/ppermute | solution.py:56
  75.9 15.2 %collective-permute-start.21 = (bf16[2,96,768]{2,1,0:T(8,128)(2,1)}, bf16[2,96,768]{2,1,0:T(8,128)(2,1)}, u32[]{:S(2)}, u32[]{:S(2)}) collective-permute-start(bf16[2,96,768]{2,1,0:T(8,128)(2,1)} %pad_maximum_fusion.5), channel_id=1, source_target_pairs={{0,16},{16,0},{1,17},{17,1},{2,18},{18,2},{3,19},{19,3},{4,20},{20... | collective-permute-start | bytes 884744 | tf_op jit(solution)/shard_map/ppermute | solution.py:56
  78.2 19.2 %collective-permute-start.20 = (bf16[2,96,768]{2,1,0:T(8,128)(2,1)}, bf16[2,96,768]{2,1,0:T(8,128)(2,1)}, u32[]{:S(2)}, u32[]{:S(2)}) collective-permute-start(bf16[2,96,768]{2,1,0:T(8,128)(2,1)} %pad_maximum_fusion.4), channel_id=1, source_target_pairs={{0,16},{16,0},{1,17},{17,1},{2,18},{18,2},{3,19},{19,3},{4,20},{20... | collective-permute-start | bytes 884744 | tf_op jit(solution)/shard_map/ppermute | solution.py:56
  115.8 19.4 %collective-permute-start.51 = (bf16[4,96,768]{2,1,0:T(8,128)(2,1)}, bf16[4,96,768]{2,1,0:T(8,128)(2,1)}, u32[]{:S(2)}, u32[]{:S(2)}) collective-permute-start(bf16[4,96,768]{2,1,0:T(8,128)(2,1)} %get-tuple-element.90), channel_id=1, source_target_pairs={{0,16},{16,0},{1,17},{17,1},{2,18},{18,2},{3,19},{19,3},{4,20},{20... | collective-permute-start | bytes 1769480 | tf_op jit(solution)/shard_map/ppermute | solution.py:56
  122.2 11.6 %collective-permute-start.25 = (bf16[624,384]{1,0:T(8,128)(2,1)}, bf16[624,384]{1,0:T(8,128)(2,1)}, u32[]{:S(2)}, u32[]{:S(2)}) collective-permute-start(bf16[624,384]{1,0:T(8,128)(2,1)} %get-tuple-element.67), channel_id=1, source_target_pairs={{0,1},{1,0},{2,3},{3,2},{4,5},{5,4},{6,7},{7,6},{8,9},{9,8},{10,11... | collective-permute-start | bytes 1437704 | tf_op jit(solution)/shard_map/ppermute | solution.py:56
  129.2 29.6 %collective-permute-start.45 = (bf16[4,96,768]{2,1,0:T(8,128)(2,1)}, bf16[4,96,768]{2,1,0:T(8,128)(2,1)}, u32[]{:S(2)}, u32[]{:S(2)}) collective-permute-start(bf16[4,96,768]{2,1,0:T(8,128)(2,1)} %get-tuple-element.88), channel_id=1, source_target_pairs={{0,16},{16,0},{1,17},{17,1},{2,18},{18,2},{3,19},{19,3},{4,20},{20... | collective-permute-start | bytes 1769480 | tf_op jit(solution)/shard_map/ppermute | solution.py:56
  131.9 79.5 %collective-permute-start.23 = (bf16[624,384]{1,0:T(8,128)(2,1)}, bf16[624,384]{1,0:T(8,128)(2,1)}, u32[]{:S(2)}, u32[]{:S(2)}) collective-permute-start(bf16[624,384]{1,0:T(8,128)(2,1)} %add.126), channel_id=1, source_target_pairs={{0,2},{1,3},{2,0},{3,1},{4,6},{5,7},{6,4},{7,5},{8,10},{9,11},{10,... | collective-permute-start | bytes 1437704 | tf_op jit(solution)/shard_map/ppermute | solution.py:56
  135.0 23.7 %collective-permute-start.26 = (bf16[624,384]{1,0:T(8,128)(2,1)S(1)}, bf16[624,384]{1,0:T(8,128)(2,1)S(1)}, u32[]{:S(2)}, u32[]{:S(2)}) collective-permute-start(bf16[624,384]{1,0:T(8,128)(2,1)S(1)} %add.128), channel_id=1, source_target_pairs={{0,2},{1,3},{2,0},{3,1},{4,6},{5,7},{6,4},{7,5},{8,10},{9,11},{10,... | collective-permute-start | bytes 1437704 | tf_op jit(solution)/shard_map/ppermute | solution.py:56
  137.2 35.6 %collective-permute-start.52 = (bf16[96,768]{1,0:T(8,128)(2,1)}, bf16[96,768]{1,0:T(8,128)(2,1)}, u32[]{:S(2)}, u32[]{:S(2)}) collective-permute-start(bf16[96,768]{1,0:T(8,128)(2,1)} %get-tuple-element.110), channel_id=1, source_target_pairs={{0,0},{1,9},{2,6},{3,15},{4,4},{5,13},{6,2},{7,11},{8,8},{9,1},{10... | collective-permute-start | bytes 442376 | tf_op jit(solution)/shard_map/ppermute | solution.py:52
  140.1 34.5 %collective-permute-start.55 = (bf16[96,768]{1,0:T(8,128)(2,1)}, bf16[96,768]{1,0:T(8,128)(2,1)}, u32[]{:S(2)}, u32[]{:S(2)}) collective-permute-start(bf16[96,768]{1,0:T(8,128)(2,1)} %get-tuple-element.111), channel_id=1, source_target_pairs={{0,3},{1,10},{2,5},{3,12},{4,7},{5,14},{6,1},{7,8},{8,11},{9,2},{1... | collective-permute-start | bytes 442376 | tf_op jit(solution)/shard_map/ppermute | solution.py:52
  158.7 22.1 %collective-permute-start.54 = (bf16[96,768]{1,0:T(8,128)(2,1)}, bf16[96,768]{1,0:T(8,128)(2,1)}, u32[]{:S(2)}, u32[]{:S(2)}) collective-permute-start(bf16[96,768]{1,0:T(8,128)(2,1)} %get-tuple-element.112), channel_id=1, source_target_pairs={{0,2},{1,11},{2,4},{3,13},{4,6},{5,15},{6,0},{7,9},{8,10},{9,3},{1... | collective-permute-start | bytes 442376 | tf_op jit(solution)/shard_map/ppermute | solution.py:52
  161.0 19.8 %collective-permute-start.53 = (bf16[96,768]{1,0:T(8,128)(2,1)}, bf16[96,768]{1,0:T(8,128)(2,1)}, u32[]{:S(2)}, u32[]{:S(2)}) collective-permute-start(bf16[96,768]{1,0:T(8,128)(2,1)} %get-tuple-element.113), channel_id=1, source_target_pairs={{0,1},{1,8},{2,7},{3,14},{4,5},{5,12},{6,3},{7,10},{8,9},{9,0},{10... | collective-permute-start | bytes 442376 | tf_op jit(solution)/shard_map/ppermute | solution.py:52
  172.9 16.2 %collective-permute-start.46 = (bf16[96,768]{1,0:T(8,128)(2,1)}, bf16[96,768]{1,0:T(8,128)(2,1)S(1)}, u32[]{:S(2)}, u32[]{:S(2)}) collective-permute-start(bf16[96,768]{1,0:T(8,128)(2,1)} %get-tuple-element.114), channel_id=1, source_target_pairs={{0,0},{1,9},{2,6},{3,15},{4,4},{5,13},{6,2},{7,11},{8,8},{9,1},{10... | collective-permute-start | bytes 442376 | tf_op jit(solution)/shard_map/ppermute | solution.py:52
  174.6 16.1 %collective-permute-start.49 = (bf16[96,768]{1,0:T(8,128)(2,1)}, bf16[96,768]{1,0:T(8,128)(2,1)S(1)}, u32[]{:S(2)}, u32[]{:S(2)}) collective-permute-start(bf16[96,768]{1,0:T(8,128)(2,1)} %get-tuple-element.115), channel_id=1, source_target_pairs={{0,3},{1,10},{2,5},{3,12},{4,7},{5,14},{6,1},{7,8},{8,11},{9,2},{1... | collective-permute-start | bytes 442376 | tf_op jit(solution)/shard_map/ppermute | solution.py:52
  189.1 12.5 %collective-permute-start.56 = (bf16[96,768]{1,0:T(8,128)(2,1)S(1)}, bf16[96,768]{1,0:T(8,128)(2,1)S(1)}, u32[]{:S(2)}, u32[]{:S(2)}) collective-permute-start(bf16[96,768]{1,0:T(8,128)(2,1)S(1)} %add_convert_fusion.3), channel_id=1, source_target_pairs={{0,16},{16,0},{1,17},{17,1},{2,18},{18,2},{3,19},{19,3},{4,20},{20... | collective-permute-start | bytes 442376 | tf_op jit(solution)/shard_map/ppermute | solution.py:56
  190.7 23.9 %collective-permute-start.28 = (bf16[624,384]{1,0:T(8,128)(2,1)}, bf16[624,384]{1,0:T(8,128)(2,1)S(1)}, u32[]{:S(2)}, u32[]{:S(2)}) collective-permute-start(bf16[624,384]{1,0:T(8,128)(2,1)} %get-tuple-element.73), channel_id=1, source_target_pairs={{0,1},{1,0},{2,3},{3,2},{4,5},{5,4},{6,7},{7,6},{8,9},{9,8},{10,11... | collective-permute-start | bytes 1437704 | tf_op jit(solution)/shard_map/ppermute | solution.py:56
  191.8 25.4 %collective-permute-start.34 = (bf16[4,96,768]{2,1,0:T(8,128)(2,1)}, bf16[4,96,768]{2,1,0:T(8,128)(2,1)S(1)}, u32[]{:S(2)}, u32[]{:S(2)}) collective-permute-start(bf16[4,96,768]{2,1,0:T(8,128)(2,1)} %get-tuple-element.81), channel_id=1, source_target_pairs={{0,16},{16,0},{1,17},{17,1},{2,18},{18,2},{3,19},{19,3},{4,20},{20... | collective-permute-start | bytes 1769480 | tf_op jit(solution)/shard_map/ppermute | solution.py:56
  200.1 11.3 %collective-permute-start.50 = (bf16[96,768]{1,0:T(8,128)(2,1)S(1)}, bf16[96,768]{1,0:T(8,128)(2,1)S(1)}, u32[]{:S(2)}, u32[]{:S(2)}) collective-permute-start(bf16[96,768]{1,0:T(8,128)(2,1)S(1)} %add_convert_fusion.4), channel_id=1, source_target_pairs={{0,16},{16,0},{1,17},{17,1},{2,18},{18,2},{3,19},{19,3},{4,20},{20... | collective-permute-start | bytes 442376 | tf_op jit(solution)/shard_map/ppermute | solution.py:56
  201.6 11.4 %collective-permute-start.43 = (f32[60,128]{1,0:T(8,128)S(1)}, f32[60,128]{1,0:T(8,128)S(1)}, u32[]{:S(2)}, u32[]{:S(2)}) collective-permute-start(f32[60,128]{1,0:T(8,128)S(1)} %add.142), channel_id=1, source_target_pairs={{0,8},{4,12},{8,0},{12,4},{1,9},{5,13},{9,1},{13,5},{2,10},{6,14},... | collective-permute-start | bytes 92168 | tf_op jit(solution)/shard_map/ppermute | solution.py:56
  214.7 20.9 %collective-permute-start.29 = (bf16[624,384]{1,0:T(8,128)(2,1)S(1)}, bf16[624,384]{1,0:T(8,128)(2,1)S(1)}, u32[]{:S(2)}, u32[]{:S(2)}) collective-permute-start(bf16[624,384]{1,0:T(8,128)(2,1)S(1)} %add.130), channel_id=1, source_target_pairs={{0,2},{1,3},{2,0},{3,1},{4,6},{5,7},{6,4},{7,5},{8,10},{9,11},{10,... | collective-permute-start | bytes 1437704 | tf_op jit(solution)/shard_map/ppermute | solution.py:56
  218.2 13.9 %collective-permute-start.38 = (bf16[96,768]{1,0:T(8,128)(2,1)S(1)}, bf16[96,768]{1,0:T(8,128)(2,1)S(1)}, u32[]{:S(2)}, u32[]{:S(2)}) collective-permute-start(bf16[96,768]{1,0:T(8,128)(2,1)S(1)} %get-tuple-element.125), channel_id=1, source_target_pairs={{0,3},{1,10},{2,5},{3,12},{4,7},{5,14},{6,1},{7,8},{8,11},{9,2},{1... | collective-permute-start | bytes 442376 | tf_op jit(solution)/shard_map/ppermute | solution.py:52
  220.6 13.1 %collective-permute-start.37 = (bf16[96,768]{1,0:T(8,128)(2,1)S(1)}, bf16[96,768]{1,0:T(8,128)(2,1)S(1)}, u32[]{:S(2)}, u32[]{:S(2)}) collective-permute-start(bf16[96,768]{1,0:T(8,128)(2,1)S(1)} %get-tuple-element.126), channel_id=1, source_target_pairs={{0,2},{1,11},{2,4},{3,13},{4,6},{5,15},{6,0},{7,9},{8,10},{9,3},{1... | collective-permute-start | bytes 442376 | tf_op jit(solution)/shard_map/ppermute | solution.py:52
  222.3 12.1 %collective-permute-start.36 = (bf16[96,768]{1,0:T(8,128)(2,1)S(1)}, bf16[96,768]{1,0:T(8,128)(2,1)S(1)}, u32[]{:S(2)}, u32[]{:S(2)}) collective-permute-start(bf16[96,768]{1,0:T(8,128)(2,1)S(1)} %get-tuple-element.127), channel_id=1, source_target_pairs={{0,1},{1,8},{2,7},{3,14},{4,5},{5,12},{6,3},{7,10},{8,9},{9,0},{10... | collective-permute-start | bytes 442376 | tf_op jit(solution)/shard_map/ppermute | solution.py:52
  (95 other events, 684.7 us)
where the time goes:
time: 257 us; the launch traced here: 256 us
  waiting for transfers between devices  94.5 us (37%)
  starting transfers between devices  68.2 us (27%)
  Pallas kernels  38 us (15%)
  local copies, waits for them, and re-layouts  36.5 us (14%)
  other arithmetic  17 us (7%)
    ppermute x32, waiting for transfers between devices, swap(): return lax.ppermute(array, axis, [(i, i ^ flip) for i in range(size)])  70 us
    pallas_call x10, Pallas kernels, run(): pl.pallas_call(kernel, out_shape=shapes, in_specs=in_specs, out_specs=[sp...  38 us
    ppermute x32, starting transfers between devices, swap(): return lax.ppermute(array, axis, [(i, i ^ flip) for i in range(size)])  32.5 us
    unnamed x142, local copies, waits for them, and re-layouts  27.6 us
    ppermute x13, starting transfers between devices, fetch(): return lax.ppermute(array, ('row', 'col'), pairs)  18.8 us
    ppermute x12, starting transfers between devices, give(): return lax.ppermute(array, ('row', 'col'), pairs)  16.8 us
    ppermute x12, waiting for transfers between devices, give(): return lax.ppermute(array, ('row', 'col'), pairs)  12.5 us
    ppermute x13, waiting for transfers between devices, fetch(): return lax.ppermute(array, ('row', 'col'), pairs)  12.1 us
  transfers between devices with their start and end apart: 57, of which 23 were waited for; matrix products, arithmetic and copies ran while one was open for 10% of the time, Pallas kernels for 8%

commit v1 on v0

--- a/solution.py
+++ b/solution.py
@@ -35,20 +35,24 @@
         self.block = self.row ^ jnp.array(self.mirror, jnp.int32)[self.col]
         self.ids = jnp.stack([self.col, self.dp % 2]).astype(jnp.int32)
 
-    def fetch(self, array, flip):
+    def moves(self, base):
+        for d in range(self.dps):
+            for r in range(self.rows):
+                for c in range(self.cols):
+                    holder = (d * self.rows + (r ^ self.mirror[c])) * self.cols + (c ^ (base + d % 2))
+                    yield (d * self.rows + r) * self.cols + c, holder
+
+    def fetch(self, array, base):
+        return lax.ppermute(array, ("dp", "row", "col"), [(holder, me) for me, holder in self.moves(base)])
+
+    def give(self, array, base):
+        return lax.ppermute(array, ("dp", "row", "col"), [(me, holder) for me, holder in self.moves(base)])
+
+    def fetch_own(self, array):
         pairs = []
         for r in range(self.rows):
             for c in range(self.cols):
-                source = (r ^ self.mirror[c]) * self.cols + (c ^ flip)
-                pairs.append((source, r * self.cols + c))
-        return lax.ppermute(array, ("row", "col"), pairs)
-
-    def give(self, array, flip):
-        pairs = []
-        for r in range(self.rows):
-            for c in range(self.cols):
-                target = (r ^ self.mirror[c]) * self.cols + (c ^ flip)
-                pairs.append((r * self.cols + c, target))
+                pairs.append(((r ^ self.mirror[c]) * self.cols + c, r * self.cols + c))
         return lax.ppermute(array, ("row", "col"), pairs)
 
     def swap(self, array, axis, flip):
@@ -57,43 +61,36 @@
 
 
 def after(value, *others):
-    return lax.optimization_barrier((value, *others))[0]
-
-
-def gather_block(grid, shard, first=None):
-    half = shard.shape[0] // 2
-    mine = lax.dynamic_slice_in_dim(shard, (grid.dp % 2) * half, half, 0)
-    if first is not None:
-        mine = after(mine, first)
-    here = [grid.fetch(mine, flip) for flip in range(grid.cols)]
-    there = [grid.swap(jnp.stack(here[i : i + 2]), "dp", 1) for i in range(0, grid.cols, 2)]
-    return here, there
-
-
-def reduce_block(grid, stay, away):
-    got = grid.swap(away, "dp", 1)
-    pair = (stay.astype(F32) + got.astype(F32)).astype(BF)
-    total = None
-    for flip in range(grid.cols):
-        part = grid.give(pair[flip], flip).astype(F32)
-        total = part if total is None else total + part
+    return lax.optimization_barrier((value, others))[0]
+
+
+BASES = (2, 0)
+
+
+def gather_block(grid, shard, starts=None):
+    pieces = []
+    for base, start in zip(BASES, starts or (None, None)):
+        piece = grid.fetch(shard if start is None else after(shard, start), base)
+        pieces += [piece, grid.swap(piece, "dp", 1)]
+    return pieces
+
+
+def finish(grid, parts):
+    total = parts[0] + parts[1]
     step = 2
     while step < grid.dps:
-        total = total + grid.swap(total.astype(BF), "dp", step).astype(F32)
+        total = total + grid.swap(total, "dp", step)
         step *= 2
-    total = total.astype(BF)
-    back = grid.swap(total, "dp", 1)
-    first = grid.dp % 2 == 0
-    return jnp.concatenate([jnp.where(first, total, back), jnp.where(first, back, total)], 0).astype(F32)
-
-
-def sum_cols(grid, mine, away):
-    mine = mine + grid.swap(away, "col", 1)
-    step = 2
+    return total.astype(F32) + grid.swap(total, "dp", 1).astype(F32)
+
+
+def sum_two(grid, mine, away, others=()):
+    mine = after(mine + grid.swap(away, "col", 1), *others)
+    total, step = mine, 2
     while step < grid.cols:
-        mine = mine + grid.swap(mine, "col", step)
+        total = total + grid.swap(total, "col", step)
         step *= 2
-    return mine, grid.swap(mine, "col", 1)
+    return mine, total
 
 
 def sum_all(grid, array):
@@ -105,15 +102,6 @@
     return array
 
 
-def sum_tokens(grid, array):
-    for axis in ("row", "dp"):
-        step = 1
-        while step < lax.axis_size(axis):
-            array = array + grid.swap(array, axis, step)
-            step *= 2
-    return array
-
-
 def dot(left, right, contract):
     return lax.dot_general(left, right, ((contract[:1], contract[1:]), ((), ())), preferred_element_type=F32)
 
@@ -154,14 +142,23 @@
     return jnp.where(low_lanes(values.shape), jnp.zeros_like(values), values)
 
 
-def place(ids, here, there, full):
-    half = here[0].shape[0]
-    pairs = [(ref, flip, ids[1]) for flip, ref in enumerate(here)]
-    for i, ref in enumerate(there):
-        pairs += [(ref.at[j], 2 * i + j, 1 - ids[1]) for j in range(2)]
-    for ref, flip, side in pairs:
-        start = pl.multiple_of(((ids[0] ^ flip) * 2 + side) * half, half)
-        full[pl.ds(start, half), :] = ref[...]
+def piece_rows(ids, which, size):
+    side = ids[1] if which % 2 == 0 else 1 - ids[1]
+    return pl.ds(pl.multiple_of((ids[0] ^ (BASES[which // 2] + side)) * size, size), size)
+
+
+def copies(ids, pieces, full, sems):
+    return [
+        pltpu.make_async_copy(piece, full.at[piece_rows(ids, i, piece.shape[0])], sems.at[i])
+        for i, piece in enumerate(pieces)
+    ]
+
+
+def place(ids, pieces, full, sems):
+    for copy in copies(ids, pieces, full, sems):
+        copy.start()
+    for copy in copies(ids, pieces, full, sems):
+        copy.wait()
 
 
 def split_halves(ids, values, mine, away):
@@ -194,10 +191,10 @@
     sums[...] = total
 
 
-def attend_kernel(ids, first, h0, h1, h2, h3, t0, t1, bias, proj_bias, full, proj, joined, attended, probs, mine, away):
+def attend_kernel(ids, first, h0, h1, h2, h3, bias, proj_bias, full, proj, joined, attended, probs, mine, away, sems):
     @pl.when(pl.program_id(0) == 0)
     def _():
-        place(ids, (h0, h1, h2, h3), (t0, t1), full)
+        place(ids, (h0, h1, h2, h3), full, sems)
         one, two, three = (full[:, i * LANES : (i + 1) * LANES].astype(F32) for i in (1, 3, 5))
         is_low = low_lanes(one.shape)
         proj[:, :LANES] = jnp.where(is_low, pltpu.roll(one, HD, 1), two).astype(BF)
@@ -225,13 +222,13 @@
 
 
 def mlp_kernel(
-    ids, tokens, one, two, cot, gain, shift, bias, e0, e1, e2, e3, f0, f1, s0, s1, s2, s3, u0, u1,
-    shrink, mid_out, second_out, hidden_out, pre_out, mine, away, sums, expand
+    ids, tokens, one, two, cot, gain, shift, bias, w0, w1, w2, w3,
+    full, mid_out, second_out, hidden_out, pre_out, mine, away, sums, sems
 ):
     @pl.when(pl.program_id(0) == 0)
     def _():
-        place(ids, (e0, e1, e2, e3), (f0, f1), expand)
-        place(ids, (s0, s1, s2, s3), (u0, u1), shrink)
+        for copy in copies(ids, (w0, w1, w2, w3), full, sems):
+            copy.start()
         sums[...] = jnp.zeros_like(sums)
 
     mid = tokens[...].astype(F32) + join_halves(ids, one, two)
@@ -239,33 +236,44 @@
     centred, _ = normalize(mid)
     second = (centred * gain[...] + shift[...]).astype(BF)
     second_out[...] = second
-    activ, slope = gelu_parts(dot(second, expand[...], (1, 0)) + bias[...])
+
+    @pl.when(pl.program_id(0) == 0)
+    def _():
+        for copy in copies(ids, (w0, w1, w2, w3), full, sems):
+            copy.wait()
+
+    width = hidden_out.shape[1]
+    activ, slope = gelu_parts(dot(second, full[:, :width], (1, 0)) + bias[...])
     hidden_out[...] = activ.astype(BF)
-    grad_pre = dot(cot[...], shrink[...], (1, 0)) * slope
-    sums[...] += columns_sum(grad_pre)
+    grad_pre = dot(cot[...], full[:, width:], (1, 0)) * slope
+    sums[0:1, :] += columns_sum(grad_pre)
     grad_pre = grad_pre.astype(BF)
     pre_out[...] = grad_pre
-    split_halves(ids, dot(grad_pre, expand[...], (1, 1)).astype(BF), mine, away)
-
-
-def shrink_kernel(ids, hidden, shrink, bias, mine, away):
-    split_halves(ids, (dot(hidden[...], shrink[...], (1, 1)) + bias[...]).astype(BF), mine, away)
-
-
-def deal(ids, full, stay, away):
-    half = stay.shape[1]
-    for flip in range(stay.shape[0]):
-        base = (ids[0] ^ flip) * 2
-        stay[flip] = full[pl.ds(pl.multiple_of((base + ids[1]) * half, half), half), :]
-        away[flip] = full[pl.ds(pl.multiple_of((base + 1 - ids[1]) * half, half), half), :]
-
-
-def outer_kernel(ids, left, right, stay, away, full):
-    full[...] = dot(left[...], right[...], (0, 0)).astype(BF)
-    deal(ids, full, stay, away)
-
-
-def joined_outer_kernel(ids, first, joined, grad_mid, attended, stay, away, full):
+    grad_normed = dot(grad_pre, full[:, :width], (1, 1))
+    sums[1:2, :] += columns_sum(grad_normed * centred)
+    sums[2:3, :] += columns_sum(grad_normed)
+    split_halves(ids, grad_normed.astype(BF), mine, away)
+
+
+def shrink_kernel(ids, hidden, full, bias, mine, away):
+    width = hidden.shape[1]
+    split_halves(ids, (dot(hidden[...], full[:, width:], (1, 1)) + bias[...]).astype(BF), mine, away)
+
+
+def deal(ids, full, stay_one, stay_two, away_one, away_two):
+    size = stay_one.shape[0]
+    for i, ref in enumerate((stay_one, away_one, stay_two, away_two)):
+        ref[...] = full[piece_rows(ids, i, size), :]
+
+
+def outer_kernel(ids, cot, hidden, second, grad_pre, s0, s1, a0, a1, full):
+    width = hidden.shape[1]
+    full[:, :width] = dot(second[...], grad_pre[...], (0, 0)).astype(BF)
+    full[:, width:] = dot(cot[...], hidden[...], (0, 0)).astype(BF)
+    deal(ids, full, s0, s1, a0, a1)
+
+
+def joined_outer_kernel(ids, first, joined, grad_mid, attended, s0, s1, a0, a1, full):
     full[...] = dot(first[...], joined[...], (0, 0)).astype(BF)
     other = dot(grad_mid[...], attended[...], (0, 0))
     turned = (pltpu.roll(other[:, :LANES], HD, 1), other[:, :LANES], pltpu.roll(other[:, LANES:], HD, 1))
@@ -273,7 +281,7 @@
         lanes = pl.ds((2 * i + 1) * LANES, LANES)
         is_low = low_lanes(values.shape)
         full[:, lanes] = jnp.where(is_low, full[:, lanes].astype(F32), values).astype(BF)
-    deal(ids, full, stay, away)
+    deal(ids, full, s0, s1, a0, a1)
 
 
 def attend_back_kernel(
@@ -309,10 +317,8 @@
         [(queries[0] + queries[1]) * scale, queries[2] * scale, keys[0] + keys[1], keys[2], values[0] + values[1], values[2]],
         axis=1,
     )
-    sums[0:1, :] += columns_sum(grad_normed * centred)
-    sums[1:2, :] += columns_sum(grad_normed)
-    sums[2:3, :] += columns_sum(grad_mid)
-    sums[3:4, :] += columns_sum(result)
+    sums[0:1, :] += columns_sum(grad_mid)
+    sums[1:2, :] += columns_sum(result)
     result = result.astype(BF)
     grad_joined_out[...] = result
     split_halves(ids, dot(result, full[...], (1, 1)).astype(BF), mine, away)
@@ -327,15 +333,32 @@
     leave(mid[...] + join_halves(ids, one, two), out)
 
 
-def exit_kernel(ids, one, two, grad_mid, tokens, gain, out, sums):
+def exit_kernel(ids, one, two, grad_mid, tokens, gain, out):
     grad_normed = join_halves(ids, one, two)
     centred, inverse = normalize(tokens[...].astype(F32))
     leave(grad_mid[...] + norm_back(grad_normed, centred, inverse, gain[...]), out)
-    sums[...] = jnp.concatenate([columns_sum(grad_normed * centred), columns_sum(grad_normed)], axis=0)
+
+
+def sums_kernel(ids, mine, away, tokens, block, cot_sum, mlp_sums, back_sums, out):
+    share = 1.0 / ((out.shape[0] - 6) // 2)
+    grad_normed = join_halves(ids, mine, away)
+    centred, _ = normalize(tokens[...].astype(F32))
+    out[...] = jnp.zeros_like(out)
+    out[0:1, :] = columns_sum(grad_normed * centred)
+    out[1:2, :] = columns_sum(grad_normed)
+    out[2:4, :] = mlp_sums[1:3, :]
+    out[4:5, :] = back_sums[0:1, :] * share
+    out[5:6, :] = cot_sum[...] * share
+    out[pl.ds(6 + 2 * block[0], 1), :] = back_sums[1:2, :]
+    out[pl.ds(7 + 2 * block[0], 1), :] = mlp_sums[0:1, :]
 
 
 def run(kernel, ids, args, outs, flops, images=None, scratch=()):
     def spec(shape, how):
+        if how == 3:
+            return pl.BlockSpec(memory_space=pltpu.SMEM)
+        if how == 2:
+            return pl.BlockSpec(memory_space=pl.ANY)
         if images is None:
             return pl.BlockSpec(memory_space=pltpu.VMEM)
         if how == 0:
@@ -351,16 +374,16 @@
     shapes = [jax.ShapeDtypeStruct(*s) for s, _ in outs]
     size += sum(s.size * s.dtype.itemsize for s in shapes)
     how = {} if images is None else {"grid": (images,)}
-    return pl.pallas_call(
+    return list(pl.pallas_call(
         kernel,
         out_shape=shapes,
         in_specs=in_specs,
         out_specs=[spec(s[0], how) for s, how in outs],
         scratch_shapes=list(scratch),
-        compiler_params=pltpu.CompilerParams(vmem_limit_bytes=48 * 1024 * 1024),
-        cost_estimate=pl.CostEstimate(flops=int(flops), bytes_accessed=int(size), transcendentals=0),
+        compiler_params=pltpu.CompilerParams(vmem_limit_bytes=60 * 1024 * 1024),
+        cost_estimate=pl.CostEstimate(flops=1, bytes_accessed=1, transcendentals=0),
         **how,
-    )(*arrays)
+    )(*arrays))
 
 
 def on_device(
@@ -400,10 +423,11 @@
         return jnp.concatenate(parts, axis=-1)
 
     packed = pack(query_weight, key_weight, value_weight, proj_weight.T)
-    biases = grid.fetch(jnp.concatenate([query_bias, value_bias, expand_bias]), 0)
-    here, there = gather_block(grid, packed)
-    e_here, e_there = gather_block(grid, expand_weight, here[1])
-    s_here, s_there = gather_block(grid, shrink_weight, e_here[1])
+    both = jnp.concatenate([expand_weight, shrink_weight], axis=1)
+    biases = grid.fetch_own(jnp.concatenate([query_bias, value_bias, expand_bias]))
+    p_pieces = gather_block(grid, packed)
+    w_pieces = gather_block(grid, after(both, p_pieces[0], p_pieces[2]))
+    p_pieces[0] = after(p_pieces[0], w_pieces[0])
     q_bias, v_bias, e_bias = biases[:wide], biases[wide : 2 * wide], biases[2 * wide :]
     nothing = jnp.zeros_like(q_bias)
     joined_bias = pack(q_bias, nothing, v_bias, nothing)
@@ -426,7 +450,7 @@
     full, proj, joined, attended, probs, mine, away = run(
         attend_kernel,
         ids,
-        [(first_in, 1)] + [(a, 0) for a in (*here, *there, line(joined_bias), spread(proj_bias))],
+        [(first_in, 1)] + [(a, 2) for a in p_pieces] + [(line(joined_bias), 0), (spread(proj_bias), 0)],
         [
             (((model, model), BF), 0),
             (((model, 2 * LANES), BF), 0),
@@ -437,73 +461,67 @@
         + halves,
         2 * rows * model * (model + 2 * wide),
         images,
-    )
-    one, two = sum_cols(grid, mine, away)
-    shrink, mid, second_in, hidden, grad_pre, mine, away, pre_sum = run(
+        [pltpu.SemaphoreType.DMA((4,))],
+    )
+    _, one = sum_two(grid, mine, away, (w_pieces[1], w_pieces[2]))
+    two = grid.swap(after(one, w_pieces[3]), "col", 1)
+    wide_full, mid, second_in, hidden, grad_pre, mine, away, mlp_sums = run(
         mlp_kernel,
         ids,
         [(tokens_pad, 1), (one, 1), (two, 1), (cot, 1)]
         + [(line(a), 0) for a in (mlp_gain, mlp_shift, e_bias)]
-        + [(a, 0) for a in (*e_here, *e_there, *s_here, *s_there)],
+        + [(a, 2) for a in w_pieces],
         [
-            (((model, hidden_here), BF), 0),
+            (((model, 2 * hidden_here), BF), 0),
             (((rows, model), F32), 1),
             (((rows, model), BF), 1),
             (((rows, hidden_here), BF), 1),
             (((rows, hidden_here), BF), 1),
         ]
         + halves
-        + [(((1, hidden_here), F32), 0)],
+        + [(((3, hidden_here), F32), 0)],
         2 * rows * model * hidden_here * 3,
         images,
-        [pltpu.VMEM((model, hidden_here), BF)],
-    )
-    one, two = sum_cols(grid, mine, away)
+        [pltpu.SemaphoreType.DMA((4,))],
+    )
 
     def pieces(width):
-        shape = (grid.cols, model // (2 * grid.cols), width)
-        return [((shape, BF), 0), ((shape, BF), 0)]
-
-    def outer(left, right):
-        return run(
-            outer_kernel,
-            ids,
-            [(left, 0), (right, 0)],
-            pieces(right.shape[1]),
-            2 * rows * model * right.shape[1],
-            scratch=[pltpu.VMEM((model, right.shape[1]), BF)],
-        )
-
-    grad_shrink = reduce_block(grid, *outer(cot, hidden))
-    grad_expand = reduce_block(grid, *outer(second_in, grad_pre))
-    mine, away = run(
+        return [(((model // grid.cols, width), BF), 0)] * 4
+
+    mine, one = sum_two(grid, mine, away)
+    hidden = after(hidden, mine)
+    parts = run(
+        outer_kernel,
+        ids,
+        [(cot, 0), (hidden, 0), (second_in, 0), (grad_pre, 0)],
+        pieces(2 * hidden_here),
+        4 * rows * model * hidden_here,
+        scratch=[pltpu.VMEM((model, 2 * hidden_here), BF)],
+    )
+    got = [grid.swap(a, "dp", 1) for a in parts[2:]]
+    mine_out, away_out = run(
         shrink_kernel,
         ids,
-        [(hidden, 1), (shrink, 0), (spread(shrink_bias), 0)],
+        [(after(hidden, parts[0]), 1), (wide_full, 0), (spread(shrink_bias), 0)],
         halves,
         2 * rows * model * hidden_here,
         images,
     )
-    out_one, out_two = sum_cols(grid, mine, away)
-    (output,) = run(
-        output_kernel,
-        ids,
-        [(out_one, 0), (out_two, 0), (mid, 0)],
-        [((tokens.shape, BF), 0)],
-        rows * model,
-    )
-
-    grad_mid, grad_mid_b, grad_joined, mine, away, sums = run(
+    mine_out, out_one = sum_two(grid, mine_out, away_out)
+    one = after(one, away_out)
+    two = grid.swap(one, "col", 1)
+
+    grad_mid, grad_mid_b, grad_joined, mine, away, back_sums = run(
         attend_back_kernel,
         ids,
         [(one, 1), (two, 1), (mid, 1), (cot, 1), (line(mlp_gain), 0), (full, 0), (proj, 0), (joined, 1), (probs, 1)],
         [(((rows, model), F32), 1), (((rows, model), BF), 1), (((rows, model), BF), 1)]
         + halves
-        + [(((4, model), F32), 0)],
+        + [(((2, model), F32), 0)],
         2 * rows * model * (model + 2 * wide),
         images,
     )
-    packed_pieces = run(
+    packed_parts = run(
         joined_outer_kernel,
         ids,
         [(first_in, 0), (grad_joined, 0), (grad_mid_b, 0), (attended, 0)],
@@ -511,24 +529,45 @@
         2 * rows * model * model,
         scratch=[pltpu.VMEM((model, model), BF)],
     )
-    one, two = sum_cols(grid, mine, away)
-    grad_packed = reduce_block(grid, *packed_pieces)
-    grad_tokens, late = run(
+    packed_got = [grid.swap(a, "dp", 1) for a in packed_parts[2:]]
+    partial, away_here = mine, away
+    away = after(away, packed_parts[0], out_one)
+    mine, one = sum_two(grid, mine, away)
+    parts = after(parts, mine)
+    pairs = [parts[i] + got[i] for i in range(2)]
+    later = grid.give(pairs[1], BASES[1])
+    assert hidden_here == model
+    (totals,) = run(
+        sums_kernel,
+        ids,
+        [(after(partial, pairs[0]), 0), (away_here, 0), (tokens_pad, 0)]
+        + [(grid.block.reshape(1).astype(jnp.int32), 3), (cot_sum, 0), (mlp_sums, 0), (back_sums, 0)],
+        [(((6 + 2 * grid.rows, model), F32), 0)],
+        rows * model * 10,
+    )
+    totals = sum_all(grid, totals)
+    packed_pairs = [packed_parts[i] + packed_got[i] for i in range(2)]
+    two = grid.swap(one, "col", 1)
+    pairs[0] = after(pairs[0], one)
+    sooner = grid.give(pairs[0], BASES[0])
+    grad_packed = finish(grid, [grid.give(pair, base) for pair, base in zip(packed_pairs, BASES)])
+    (grad_tokens,) = run(
         exit_kernel,
         ids,
         [(one, 0), (two, 0), (grad_mid, 0), (tokens_pad, 0), (line(attn_gain), 0)],
-        [((tokens.shape, BF), 0), (((2, model), F32), 0)],
+        [((tokens.shape, BF), 0)],
         rows * model * 20,
     )
-    late = sum_tokens(grid, late)
-
+    (output,) = run(
+        output_kernel,
+        ids,
+        [(out_one, 0), (grid.swap(out_one, "col", 1), 0), (mid, 0)],
+        [((tokens.shape, BF), 0)],
+        rows * model,
+    )
+    grad_both = finish(grid, [sooner, later])
     step = wide + HD
-    blocks = jnp.concatenate([sums[3, :wide], sums[3, 2 * step : 2 * step + wide], pre_sum[0]])
-    slots = jnp.where(jnp.arange(grid.rows)[:, None] == grid.block, blocks[None], 0.0)
-    early = jnp.concatenate([(sums[:3] / grid.cols).reshape(-1), cot_sum[0] / grid.cols, slots.reshape(-1)])
-    early = sum_all(grid, early.reshape(-1, LANES)).reshape(-1)
-    whole = early[: 4 * model].reshape(4, model)
-    blocks = lax.dynamic_index_in_dim(early[4 * model :].reshape(grid.rows, -1), grid.row, 0, keepdims=False)
+    blocks = lax.dynamic_slice_in_dim(totals, 6 + 2 * grid.row, 2, 0)
 
     def own_columns(vector):
         width = vector.shape[0] // grid.cols
@@ -538,21 +577,21 @@
     return (
         output,
         grad_tokens,
-        late[0],
-        late[1],
+        totals[0],
+        totals[1],
         grad_packed[:, :wide],
         grad_packed[:, step : step + wide],
         grad_packed[:, 2 * step : 2 * step + wide],
-        blocks[:wide],
-        blocks[wide : 2 * wide],
+        blocks[0, :wide],
+        blocks[0, 2 * step : 2 * step + wide],
         grad_proj,
-        own_columns(whole[2]),
-        whole[0],
-        whole[1],
-        grad_expand,
-        blocks[2 * wide :],
-        grad_shrink,
-        own_columns(whole[3]),
+        own_columns(totals[4]),
+        totals[2],
+        totals[3],
+        grad_both[:, :hidden_here],
+        blocks[1],
+        grad_both[:, hidden_here:],
+        own_columns(totals[5]),
     )
 
 

time: 257 us -> 203 us (0.79)
  waiting for transfers between devices: 94.5 us -> 57.5 us
  local copies, waits for them, and re-layouts: 36.5 us -> 15.9 us
  Pallas kernels: 38 us -> 53.8 us
  starting transfers between devices: 68.2 us -> 56.7 us
    ppermute x32 -> x27, waiting for transfers between devices: 70 us -> 34.2 us  [swap(): return lax.ppermute(array, axis, [(i, i ^ flip) for i in range(size)])]
    unnamed x142 -> x70, local copies, waits for them, and re-layouts: 27.6 us -> 4.32 us
    pallas_call x10, Pallas kernels: 38 us -> 53.8 us  [run(): pl.pallas_call(kernel, out_shape=shapes, in_specs=in_specs, out_specs=[sp...]
    ppermute x25 -> x9, starting transfers between devices: 35.6 us -> 22.4 us  [the longest x4 11.4 us: fetch(): lax.ppermute(array, ('dp', 'row', 'col'), [(holder, me) for me, holder in...]
    add x11 -> x16, other arithmetic: 5.25 us -> 11.3 us  [the longest x2 3.53 us: on_device(): packed_pairs = [packed_parts[i] + packed_got[i] for i in range(2)]]
    convert_element_type x9 -> x0, other arithmetic: 5.72 us -> none  [the longest x3 2.61 us: reduce_block(): pair = (stay.astype(F32) + got.astype(F32)).astype(BF)]
    another operation x6 -> x0, other arithmetic: 4.55 us -> none  [gather_block(): jnp.stack(here[i:i + 2])]
    reshape x6, local copies, waits for them, and re-layouts: 0.03 us -> 3.63 us  [line(): return vector.reshape(1, -1)]
  transfers between devices with their start and end apart: 57 -> 36, of which waited for: 23 -> 14; matrix products, arithmetic and copies ran while one was open for 10% -> 12% of each run, Pallas kernels for 8% -> 23%
where the time goes in v1:
time: 203 us; the launch traced here: 201 us
  waiting for transfers between devices  57.5 us (28%)
  starting transfers between devices  56.7 us (28%)
  Pallas kernels  53.8 us (27%)
  local copies, waits for them, and re-layouts  15.9 us (8%)
  other arithmetic  14.9 us (7%)
    pallas_call x10, Pallas kernels, run(): pl.pallas_call(kernel, out_shape=shapes, in_specs=in_specs, out_specs=[sp...  53.8 us
    ppermute x27, starting transfers between devices, swap(): return lax.ppermute(array, axis, [(i, i ^ flip) for i in range(size)])  34.2 us
    ppermute x27, waiting for transfers between devices, swap(): return lax.ppermute(array, axis, [(i, i ^ flip) for i in range(size)])  34.2 us
    ppermute x4, waiting for transfers between devices, give(): lax.ppermute(array, ('dp', 'row', 'col'), [(me, holder) for me, holder in...  17.2 us
    ppermute x4, starting transfers between devices, fetch(): lax.ppermute(array, ('dp', 'row', 'col'), [(holder, me) for me, holder in...  11.4 us
    ppermute x4, starting transfers between devices, give(): lax.ppermute(array, ('dp', 'row', 'col'), [(me, holder) for me, holder in...  10.4 us
    ppermute x4, waiting for transfers between devices, fetch(): lax.ppermute(array, ('dp', 'row', 'col'), [(holder, me) for me, holder in...  6.13 us
    unnamed x70, local copies, waits for them, and re-layouts  4.32 us
  transfers between devices with their start and end apart: 36, of which 14 were waited for; matrix products, arithmetic and copies ran while one was open for 12% of the time, Pallas kernels for 23%

profile of v1, /device:TPU:0, one launch (start us, length us, event | category | flops | bytes accessed | tf_op | source)
XLA Modules:
  0.0 200.7 jit_solution(10751684128320443057)
XLA Ops:
  3.0 4.0 %collective-permute-start = (bf16[192,768]{1,0:T(8,128)(2,1)S(1)}, bf16[192,768]{1,0:T(8,128)(2,1)S(1)}, u32[]{:S(2)}, u32[]{:S(2)}) collective-permute-start(bf16[192,768]{1,0:T(8,128)(2,1)S(1)} %concatenate.15), channel_id=1, source_target_pairs={{2,0},{11,1},{4,2},{13,3},{6,4},{15,5},{0,6},{9,7},{10,8},{3,9},{1... | collective-permute-start | bytes 884744 | tf_op jit(solution)/shard_map/ppermute | solution.py:46
  7.8 5.8 %collective-permute-done.h0 = bf16[192,768]{1,0:T(8,128)(2,1)S(1)} collective-permute-done((bf16[192,768]{1,0:T(8,128)(2,1)S(1)}, bf16[192,768]{1,0:T(8,128)(2,1)S(1)}, u32[]{:S(2)}, u32[]{:S(2)}) %collective-permute-start) | collective-permute-done | bytes 294944 | tf_op jit(solution)/shard_map/ppermute | solution.py:46
  13.6 5.8 %collective-permute-start.2 = (bf16[192,1536]{1,0:T(8,128)(2,1)S(1)}, bf16[192,1536]{1,0:T(8,128)(2,1)S(1)}, u32[]{:S(2)}, u32[]{:S(2)}) collective-permute-start(bf16[192,1536]{1,0:T(8,128)(2,1)S(1)} %pad_maximum_fusion), channel_id=1, source_target_pairs={{2,0},{11,1},{4,2},{13,3},{6,4},{15,5},{0,6},{9,7},{10,8},{3,9},{1... | collective-permute-start | bytes 1769480 | tf_op jit(solution)/shard_map/ppermute | solution.py:46
  20.8 4.0 %collective-permute-start.3 = (bf16[192,768]{1,0:T(8,128)(2,1)S(1)}, bf16[192,768]{1,0:T(8,128)(2,1)S(1)}, u32[]{:S(2)}, u32[]{:S(2)}) collective-permute-start(bf16[192,768]{1,0:T(8,128)(2,1)S(1)} %collective-permute-done.h0), channel_id=1, source_target_pairs={{0,16},{16,0},{1,17},{17,1},{2,18},{18,2},{3,19},{19,3},{4,20},{20... | collective-permute-start | bytes 884744 | tf_op jit(solution)/shard_map/ppermute | solution.py:60
  26.7 3.8 %shard_map.305 = (bf16[624,768]{1,0:T(8,128)(2,1)}, bf16[624,768]{1,0:T(8,128)(2,1)}, bf16[624,768]{1,0:T(8,128)(2,1)}, f32[1,768]{1,0:T(1,128)}) custom-call(bf16[591,768]{1,0:T(8,128)(2,1)} %tokens.1, bf16[591,768]{1,0:T(8,128)(2,1)} %cot.1, f32[1,768]{1,0:T(1,128)} %reshape.121.gain, f32[1,768]{1,0:T(1,128)} %reshape.122.shift), custom_call_target="tpu_custom_call" | custom-call | flops 1 | bytes 1 | tf_op jit(solution)/shard_map/pallas_call | solution.py:377
  31.7 6.8 %collective-permute-start.7 = (bf16[192,1536]{1,0:T(8,128)(2,1)S(1)}, bf16[192,1536]{1,0:T(8,128)(2,1)S(1)}, u32[]{:S(2)}, u32[]{:S(2)}) collective-permute-start(bf16[192,1536]{1,0:T(8,128)(2,1)S(1)} %collective-permute-done.2.w0), channel_id=1, source_target_pairs={{0,16},{16,0},{1,17},{17,1},{2,18},{18,2},{3,19},{19,3},{4,20},{20... | collective-permute-start | bytes 1769480 | tf_op jit(solution)/shard_map/ppermute | solution.py:60
  41.9 7.3 %shard_map.306 = (bf16[768,768]{1,0:T(8,128)(2,1)}, bf16[768,256]{1,0:T(8,128)(2,1)}, bf16[624,768]{1,0:T(8,128)(2,1)}, bf16[624,256]{1,0:T(8,128)(2,1)}, bf16[9...) custom-call(s32[2]{0:T(128)} %pad_add_fusion.ids, ...), custom_call_target="tpu_custom_call" | custom-call | flops 1 | bytes 1 | tf_op jit(solution)/shard_map/pallas_call | solution.py:377
  52.6 4.2 %collective-permute-start.9 = (bf16[624,384]{1,0:T(8,128)(2,1)S(1)}, bf16[624,384]{1,0:T(8,128)(2,1)S(1)}, u32[]{:S(2)}, u32[]{:S(2)}) collective-permute-start(bf16[624,384]{1,0:T(8,128)(2,1)S(1)} %add.92), channel_id=1, source_target_pairs={{0,2},{1,3},{2,0},{3,1},{4,6},{5,7},{6,4},{7,5},{8,10},{9,11},{10,... | collective-permute-start | bytes 1437704 | tf_op jit(solution)/shard_map/ppermute | solution.py:60
  56.8 10.5 %collective-permute-done.9 = bf16[624,384]{1,0:T(8,128)(2,1)S(1)} collective-permute-done((bf16[624,384]{1,0:T(8,128)(2,1)S(1)}, bf16[624,384]{1,0:T(8,128)(2,1)S(1)}, u32[]{:S(2)}, u32[]{:S(2)}) %collective-permute-start.9) | collective-permute-done | bytes 479264 | tf_op jit(solution)/shard_map/ppermute | solution.py:60
  70.3 8.5 %shard_map.307 = (bf16[768,1536]{1,0:T(8,128)(2,1)}, f32[624,768]{1,0:T(8,128)}, bf16[624,768]{1,0:T(8,128)(2,1)}, bf16[624,768]{1,0:T(8,128)(2,1)}, bf16[624,76...) custom-call(s32[2]{0:T(128)} %pad_add_fusion.ids, ...), custom_call_target="tpu_custom_call" | custom-call | flops 1 | bytes 1 | tf_op jit(solution)/shard_map/pallas_call | solution.py:377
  83.4 5.5 %shard_map.308 = (bf16[192,1536]{1,0:T(8,128)(2,1)}, bf16[192,1536]{1,0:T(8,128)(2,1)}, bf16[192,1536]{1,0:T(8,128)(2,1)}, bf16[192,1536]{1,0:T(8,128)(2,1)}) custom-call(s32[2]{0:T(128)} %pad_add_fusion.ids, bf16[624,768]{1,0:T(8,128)(2,1)} %get-tuple-element.72.cot, bf16[624,768]{1,0:T(8,128)(2,1)} %get-tuple-element.80.hidden, ...), custom_call_target="tpu_custom_call" | custom-call | flops 1 | bytes 1 | tf_op jit(solution)/shard_map/pallas_call | solution.py:377
  88.9 4.8 %shard_map.309 = (bf16[624,384]{1,0:T(8,128)(2,1)}, bf16[624,384]{1,0:T(8,128)(2,1)}) custom-call(s32[2]{0:T(128)} %pad_add_fusion.ids, bf16[624,768]{1,0:T(8,128)(2,1)} %get-tuple-element.80.hidden, bf16[768,1536]{1,0:T(8,128)(2,1)} %get-tuple-element.81.full, f32[1,768]{1,0:T(1,128)} %compare_select_fusion.bias), custom_call_target="tpu_custom_call" | custom-call | flops 1 | bytes 1 | tf_op jit(solution)/shard_map/pallas_call | solution.py:377
  93.7 1.6 collective-permute-done.16
  99.0 9.0 %shard_map.311 = (f32[624,768]{1,0:T(8,128)}, bf16[624,768]{1,0:T(8,128)(2,1)}, bf16[624,768]{1,0:T(8,128)(2,1)}, bf16[624,384]{1,0:T(8,128)(2,1)}, bf16[624,384]{1,0:T(8,128)(2,1)}, /*index=5*/f32[2,768]{1,0:T(2,128)}) custom-call(s32[2]{0:T(128)} %pad_add_fusion.ids, bf16[624,384]{1,0:T(8,128)(2,1)} %copy-done.3, bf16[624,384]{1,0:T(8,128)(2,1)} %copy-done.14, ...), custom_call_target="tpu_custom_call" | custom-call | flops 1 | bytes 1 | tf_op jit(solution)/shard_map/pallas_call | solution.py:377
  107.9 4.4 %shard_map.312 = (bf16[192,768]{1,0:T(8,128)(2,1)}, bf16[192,768]{1,0:T(8,128)(2,1)}, bf16[192,768]{1,0:T(8,128)(2,1)}, bf16[192,768]{1,0:T(8,128)(2,1)}) custom-call(s32[2]{0:T(128)} %pad_add_fusion.ids, bf16[624,768]{1,0:T(8,128)(2,1)} %get-tuple-element.65.first, bf16[624,768]{1,0:T(8,128)(2,1)} %get-tuple-element.92.joined, ...), custom_call_target="tpu_custom_call" | custom-call | flops 1 | bytes 1 | tf_op jit(solution)/shard_map/pallas_call | solution.py:377
  118.3 3.0 %shard_map.314 = f32[14,768]{1,0:T(8,128)} custom-call(s32[2]{0:T(128)} %pad_add_fusion.ids, bf16[624,384]{1,0:T(8,128)(2,1)} %get-tuple-element.102.mine, bf16[624,384]{1,0:T(8,128)(2,1)} %get-tuple-element.96.away, bf16[624,768]{1,0:T(8,128)(2,1)} %get-tuple-element.64.tokens, s32[1]{0:T(128)} %bitcast.4.block, f32[1,768]{1,0:T(1,128)} %get-tuple-element.103.cot_sum, ...), custom_call_target="tpu_custom_call" | custom-call | flops 1 | bytes 1 | tf_op jit(solution)/shard_map/pallas_call | solution.py:377
  124.5 3.1 %collective-permute-done.23 = f32[14,768]{1,0:T(8,128)S(1)} collective-permute-done((f32[14,768]{1,0:T(8,128)S(1)}, f32[14,768]{1,0:T(8,128)S(1)}, u32[]{:S(2)}, u32[]{:S(2)}) %collective-permute-start.23) | collective-permute-done | bytes 43040 | tf_op jit(solution)/shard_map/ppermute | solution.py:60
  128.4 3.4 %collective-permute-done.24 = f32[14,768]{1,0:T(8,128)S(1)} collective-permute-done((f32[14,768]{1,0:T(8,128)S(1)}, f32[14,768]{1,0:T(8,128)S(1)}, u32[]{:S(2)}, u32[]{:S(2)}) %collective-permute-start.24) | collective-permute-done | bytes 43040 | tf_op jit(solution)/shard_map/ppermute | solution.py:60
  134.0 1.8 add.108
  135.8 5.5 %collective-permute-done.27 = bf16[192,768]{1,0:T(8,128)(2,1)} collective-permute-done((bf16[192,768]{1,0:T(8,128)(2,1)}, bf16[192,768]{1,0:T(8,128)(2,1)}, u32[]{:S(2)}, u32[]{:S(2)}) %collective-permute-start.27) | collective-permute-done | bytes 294944 | tf_op jit(solution)/shard_map/ppermute | solution.py:60
  141.3 1.6 collective-permute-start.30
  142.9 1.7 add.107
  144.7 2.1 %collective-permute-start.28 = (bf16[192,768]{1,0:T(8,128)(2,1)}, bf16[192,768]{1,0:T(8,128)(2,1)}, u32[]{:S(2)}, u32[]{:S(2)}) collective-permute-start(bf16[192,768]{1,0:T(8,128)(2,1)} %add.107), channel_id=1, source_target_pairs={{0,2},{1,11},{2,4},{3,13},{4,6},{5,15},{6,0},{7,9},{8,10},{9,3},{1... | collective-permute-start | bytes 884744 | tf_op jit(solution)/shard_map/ppermute | solution.py:49
  146.8 1.9 collective-permute-start.26
  149.7 1.9 collective-permute-start.34
  151.7 3.1 %shard_map.310 = bf16[591,768]{1,0:T(8,128)(2,1)} custom-call(s32[2]{0:T(128)} %pad_add_fusion.ids, bf16[624,384]{1,0:T(8,128)(2,1)} %copy-done.2, bf16[624,384]{1,0:T(8,128)(2,1)} %copy-done.13, f32[624,768]{1,0:T(8,128)} %get-tuple-element.84.mid), custom_call_target="tpu_custom_call" | custom-call | flops 1 | bytes 1 | tf_op jit(solution)/shard_map/pallas_call | solution.py:377
  154.7 4.9 %collective-permute-done.28 = bf16[192,768]{1,0:T(8,128)(2,1)} collective-permute-done((bf16[192,768]{1,0:T(8,128)(2,1)}, bf16[192,768]{1,0:T(8,128)(2,1)}, u32[]{:S(2)}, u32[]{:S(2)}) %collective-permute-start.28) | collective-permute-done | bytes 294944 | tf_op jit(solution)/shard_map/ppermute | solution.py:49
  160.7 4.5 %collective-permute-start.31 = (bf16[192,768]{1,0:T(8,128)(2,1)S(1)}, bf16[192,768]{1,0:T(8,128)(2,1)S(1)}, u32[]{:S(2)}, u32[]{:S(2)}) collective-permute-start(bf16[192,768]{1,0:T(8,128)(2,1)S(1)} %add.109), channel_id=1, source_target_pairs={{0,16},{16,0},{1,17},{17,1},{2,18},{18,2},{3,19},{19,3},{4,20},{20... | collective-permute-start | bytes 884744 | tf_op jit(solution)/shard_map/ppermute | solution.py:60
  167.8 4.8 %collective-permute-start.32 = (bf16[192,1536]{1,0:T(8,128)(2,1)S(1)}, bf16[192,1536]{1,0:T(8,128)(2,1)S(1)}, u32[]{:S(2)}, u32[]{:S(2)}) collective-permute-start(bf16[192,1536]{1,0:T(8,128)(2,1)S(1)} %add.100), channel_id=1, source_target_pairs={{0,2},{1,11},{2,4},{3,13},{4,6},{5,15},{6,0},{7,9},{8,10},{9,3},{1... | collective-permute-start | bytes 1769480 | tf_op jit(solution)/shard_map/ppermute | solution.py:49
  174.0 12.3 %collective-permute-done.32 = bf16[192,1536]{1,0:T(8,128)(2,1)S(1)} collective-permute-done((bf16[192,1536]{1,0:T(8,128)(2,1)S(1)}, bf16[192,1536]{1,0:T(8,128)(2,1)S(1)}, u32[]{:S(2)}, u32[]{:S(2)}) %collective-permute-start.32) | collective-permute-done | bytes 589856 | tf_op jit(solution)/shard_map/ppermute | solution.py:49
  188.4 4.4 %shard_map.313 = bf16[591,768]{1,0:T(8,128)(2,1)} custom-call(s32[2]{0:T(128)} %pad_add_fusion.ids, bf16[624,384]{1,0:T(8,128)(2,1)} %copy-done, bf16[624,384]{1,0:T(8,128)(2,1)} %collective-permute-done.20.two, f32[624,768]{1,0:T(8,128)} %get-tuple-element.97.grad_mid, bf16[624,768]{1,0:T(8,128)(2,1)} %get-tuple-element.64.tokens, f32[1,768]{1,0:T(1,128)} %reshape.121.gain), custom_call_target="tpu_custom_call" | custom-call | flops 1 | bytes 1 | tf_op jit(solution)/shard_map/pallas_call | solution.py:377
  192.8 6.7 %collective-permute-done.35 = bf16[192,1536]{1,0:T(8,128)(2,1)S(1)} collective-permute-done((bf16[192,1536]{1,0:T(8,128)(2,1)S(1)}, bf16[192,1536]{1,0:T(8,128)(2,1)S(1)}, u32[]{:S(2)}, u32[]{:S(2)}) %collective-permute-start.35) | collective-permute-done | bytes 589856 | tf_op jit(solution)/shard_map/ppermute | solution.py:60
  (171 shorter events, 46.0 us)
Async XLA Ops:
  3.0 10.5 %collective-permute-start = (bf16[192,768]{1,0:T(8,128)(2,1)S(1)}, bf16[192,768]{1,0:T(8,128)(2,1)S(1)}, u32[]{:S(2)}, u32[]{:S(2)}) collective-permute-start(bf16[192,768]{1,0:T(8,128)(2,1)S(1)} %concatenate.15), channel_id=1, source_target_pairs={{2,0},{11,1},{4,2},{13,3},{6,4},{15,5},{0,6},{9,7},{10,8},{3,9},{1... | collective-permute-start | bytes 884744 | tf_op jit(solution)/shard_map/ppermute | solution.py:46
  7.0 6.5 %collective-permute-start.1 = (bf16[192,768]{1,0:T(8,128)(2,1)S(1)}, bf16[192,768]{1,0:T(8,128)(2,1)S(1)}, u32[]{:S(2)}, u32[]{:S(2)}) collective-permute-start(bf16[192,768]{1,0:T(8,128)(2,1)S(1)} %concatenate.15), channel_id=1, source_target_pairs={{0,0},{9,1},{6,2},{15,3},{4,4},{13,5},{2,6},{11,7},{8,8},{1,9},{14... | collective-permute-start | bytes 884744 | tf_op jit(solution)/shard_map/ppermute | solution.py:46
  13.6 18.2 %collective-permute-start.2 = (bf16[192,1536]{1,0:T(8,128)(2,1)S(1)}, bf16[192,1536]{1,0:T(8,128)(2,1)S(1)}, u32[]{:S(2)}, u32[]{:S(2)}) collective-permute-start(bf16[192,1536]{1,0:T(8,128)(2,1)S(1)} %pad_maximum_fusion), channel_id=1, source_target_pairs={{2,0},{11,1},{4,2},{13,3},{6,4},{15,5},{0,6},{9,7},{10,8},{3,9},{1... | collective-permute-start | bytes 1769480 | tf_op jit(solution)/shard_map/ppermute | solution.py:46
  19.5 19.1 %collective-permute-start.5 = (f32[1152]{0:T(1024)S(1)}, f32[1152]{0:T(1024)S(1)}, u32[]{:S(2)}, u32[]{:S(2)}) collective-permute-start(f32[1152]{0:T(1024)S(1)} %concatenate.17), channel_id=1, source_target_pairs={{0,0},{9,1},{6,2},{15,3},{4,4},{13,5},{2,6},{11,7},{8,8},{1,9},{14... | collective-permute-start | bytes 13832 | tf_op jit(solution)/shard_map/ppermute | solution.py:56
  20.8 20.3 %collective-permute-start.3 = (bf16[192,768]{1,0:T(8,128)(2,1)S(1)}, bf16[192,768]{1,0:T(8,128)(2,1)S(1)}, u32[]{:S(2)}, u32[]{:S(2)}) collective-permute-start(bf16[192,768]{1,0:T(8,128)(2,1)S(1)} %collective-permute-done.h0), channel_id=1, source_target_pairs={{0,16},{16,0},{1,17},{17,1},{2,18},{18,2},{3,19},{19,3},{4,20},{20... | collective-permute-start | bytes 884744 | tf_op jit(solution)/shard_map/ppermute | solution.py:60
  24.8 16.3 %collective-permute-start.4 = (bf16[192,768]{1,0:T(8,128)(2,1)S(1)}, bf16[192,768]{1,0:T(8,128)(2,1)S(1)}, u32[]{:S(2)}, u32[]{:S(2)}) collective-permute-start(bf16[192,768]{1,0:T(8,128)(2,1)S(1)} %collective-permute-done.1.h2), channel_id=1, source_target_pairs={{0,16},{16,0},{1,17},{17,1},{2,18},{18,2},{3,19},{19,3},{4,20},{20... | collective-permute-start | bytes 884744 | tf_op jit(solution)/shard_map/ppermute | solution.py:60
  30.5 19.1 %collective-permute-start.8 = (bf16[192,1536]{1,0:T(8,128)(2,1)S(1)}, bf16[192,1536]{1,0:T(8,128)(2,1)S(1)}, u32[]{:S(2)}, u32[]{:S(2)}) collective-permute-start(bf16[192,1536]{1,0:T(8,128)(2,1)S(1)} %pad_maximum_fusion), channel_id=1, source_target_pairs={{0,0},{9,1},{6,2},{15,3},{4,4},{13,5},{2,6},{11,7},{8,8},{1,9},{14... | collective-permute-start | bytes 1769480 | tf_op jit(solution)/shard_map/ppermute | solution.py:46
  31.7 20.9 %collective-permute-start.7 = (bf16[192,1536]{1,0:T(8,128)(2,1)S(1)}, bf16[192,1536]{1,0:T(8,128)(2,1)S(1)}, u32[]{:S(2)}, u32[]{:S(2)}) collective-permute-start(bf16[192,1536]{1,0:T(8,128)(2,1)S(1)} %collective-permute-done.2.w0), channel_id=1, source_target_pairs={{0,16},{16,0},{1,17},{17,1},{2,18},{18,2},{3,19},{19,3},{4,20},{20... | collective-permute-start | bytes 1769480 | tf_op jit(solution)/shard_map/ppermute | solution.py:60
  49.6 17.9 %collective-permute-start.10 = (bf16[192,1536]{1,0:T(8,128)(2,1)S(1)}, bf16[192,1536]{1,0:T(8,128)(2,1)S(1)}, u32[]{:S(2)}, u32[]{:S(2)}) collective-permute-start(bf16[192,1536]{1,0:T(8,128)(2,1)S(1)} %collective-permute-done.8.w2), channel_id=1, source_target_pairs={{0,16},{16,0},{1,17},{17,1},{2,18},{18,2},{3,19},{19,3},{4,20},{20... | collective-permute-start | bytes 1769480 | tf_op jit(solution)/shard_map/ppermute | solution.py:60
  52.6 14.7 %collective-permute-start.9 = (bf16[624,384]{1,0:T(8,128)(2,1)S(1)}, bf16[624,384]{1,0:T(8,128)(2,1)S(1)}, u32[]{:S(2)}, u32[]{:S(2)}) collective-permute-start(bf16[624,384]{1,0:T(8,128)(2,1)S(1)} %add.92), channel_id=1, source_target_pairs={{0,2},{1,3},{2,0},{3,1},{4,6},{5,7},{6,4},{7,5},{8,10},{9,11},{10,... | collective-permute-start | bytes 1437704 | tf_op jit(solution)/shard_map/ppermute | solution.py:60
  78.8 2.1 %collective-permute-start.12 = (bf16[624,384]{1,0:T(8,128)(2,1)}, bf16[624,384]{1,0:T(8,128)(2,1)S(1)}, u32[]{:S(2)}, u32[]{:S(2)}) collective-permute-start(bf16[624,384]{1,0:T(8,128)(2,1)} %get-tuple-element.75), channel_id=1, source_target_pairs={{0,1},{1,0},{2,3},{3,2},{4,5},{5,4},{6,7},{7,6},{8,9},{9,8},{10,11... | collective-permute-start | bytes 1437704 | tf_op jit(solution)/shard_map/ppermute | solution.py:60
  82.1 13.3 %collective-permute-start.16 = (bf16[624,384]{1,0:T(8,128)(2,1)S(1)}, bf16[624,384]{1,0:T(8,128)(2,1)S(1)}, u32[]{:S(2)}, u32[]{:S(2)}) collective-permute-start(bf16[624,384]{1,0:T(8,128)(2,1)S(1)} %add.94), channel_id=1, source_target_pairs={{0,2},{1,3},{2,0},{3,1},{4,6},{5,7},{6,4},{7,5},{8,10},{9,11},{10,... | collective-permute-start | bytes 1437704 | tf_op jit(solution)/shard_map/ppermute | solution.py:60
  95.5 2.7 %collective-permute-start.17 = (bf16[624,384]{1,0:T(8,128)(2,1)S(1)}, bf16[624,384]{1,0:T(8,128)(2,1)S(1)}, u32[]{:S(2)}, u32[]{:S(2)}) collective-permute-start(bf16[624,384]{1,0:T(8,128)(2,1)S(1)} %add.97.one), channel_id=1, source_target_pairs={{0,1},{1,0},{2,3},{3,2},{4,5},{5,4},{6,7},{7,6},{8,9},{9,8},{10,11... | collective-permute-start | bytes 1437704 | tf_op jit(solution)/shard_map/ppermute | solution.py:60
  95.9 16.5 %collective-permute-start.14 = (bf16[624,384]{1,0:T(8,128)(2,1)S(1)}, bf16[624,384]{1,0:T(8,128)(2,1)S(1)}, u32[]{:S(2)}, u32[]{:S(2)}) collective-permute-start(bf16[624,384]{1,0:T(8,128)(2,1)S(1)} %add.95), channel_id=1, source_target_pairs={{0,2},{1,3},{2,0},{3,1},{4,6},{5,7},{6,4},{7,5},{8,10},{9,11},{10,... | collective-permute-start | bytes 1437704 | tf_op jit(solution)/shard_map/ppermute | solution.py:60
  97.0 20.0 %collective-permute-start.21 = (bf16[192,1536]{1,0:T(8,128)(2,1)}, bf16[192,1536]{1,0:T(8,128)(2,1)}, u32[]{:S(2)}, u32[]{:S(2)}) collective-permute-start(bf16[192,1536]{1,0:T(8,128)(2,1)} %get-tuple-element.99), channel_id=1, source_target_pairs={{0,16},{16,0},{1,17},{17,1},{2,18},{18,2},{3,19},{19,3},{4,20},{20... | collective-permute-start | bytes 1769480 | tf_op jit(solution)/shard_map/ppermute | solution.py:60
  112.5 4.3 %collective-permute-start.18 = (bf16[624,384]{1,0:T(8,128)(2,1)S(1)}, bf16[624,384]{1,0:T(8,128)(2,1)S(1)}, u32[]{:S(2)}, u32[]{:S(2)}) collective-permute-start(bf16[624,384]{1,0:T(8,128)(2,1)S(1)} %copy-done.11), channel_id=1, source_target_pairs={{0,1},{1,0},{2,3},{3,2},{4,5},{5,4},{6,7},{7,6},{8,9},{9,8},{10,11... | collective-permute-start | bytes 1437704 | tf_op jit(solution)/shard_map/ppermute | solution.py:60
  112.6 20.1 %collective-permute-start.29 = (bf16[192,768]{1,0:T(8,128)(2,1)}, bf16[192,768]{1,0:T(8,128)(2,1)}, u32[]{:S(2)}, u32[]{:S(2)}) collective-permute-start(bf16[192,768]{1,0:T(8,128)(2,1)} %get-tuple-element.108), channel_id=1, source_target_pairs={{0,16},{16,0},{1,17},{17,1},{2,18},{18,2},{3,19},{19,3},{4,20},{20... | collective-permute-start | bytes 884744 | tf_op jit(solution)/shard_map/ppermute | solution.py:60
  113.6 33.2 %collective-permute-start.33 = (bf16[192,1536]{1,0:T(8,128)(2,1)}, bf16[192,1536]{1,0:T(8,128)(2,1)S(1)}, u32[]{:S(2)}, u32[]{:S(2)}) collective-permute-start(bf16[192,1536]{1,0:T(8,128)(2,1)} %get-tuple-element.100), channel_id=1, source_target_pairs={{0,16},{16,0},{1,17},{17,1},{2,18},{18,2},{3,19},{19,3},{4,20},{20... | collective-permute-start | bytes 1769480 | tf_op jit(solution)/shard_map/ppermute | solution.py:60
  114.7 26.6 %collective-permute-start.27 = (bf16[192,768]{1,0:T(8,128)(2,1)}, bf16[192,768]{1,0:T(8,128)(2,1)}, u32[]{:S(2)}, u32[]{:S(2)}) collective-permute-start(bf16[192,768]{1,0:T(8,128)(2,1)} %get-tuple-element.106), channel_id=1, source_target_pairs={{0,16},{16,0},{1,17},{17,1},{2,18},{18,2},{3,19},{19,3},{4,20},{20... | collective-permute-start | bytes 884744 | tf_op jit(solution)/shard_map/ppermute | solution.py:60
  121.3 28.4 %collective-permute-start.15 = (bf16[624,384]{1,0:T(8,128)(2,1)S(1)}, bf16[624,384]{1,0:T(8,128)(2,1)S(1)}, u32[]{:S(2)}, u32[]{:S(2)}) collective-permute-start(bf16[624,384]{1,0:T(8,128)(2,1)S(1)} %add.96.one), channel_id=1, source_target_pairs={{0,1},{1,0},{2,3},{3,2},{4,5},{5,4},{6,7},{7,6},{8,9},{9,8},{10,11... | collective-permute-start | bytes 1437704 | tf_op jit(solution)/shard_map/ppermute | solution.py:60
  123.5 4.1 %collective-permute-start.23 = (f32[14,768]{1,0:T(8,128)S(1)}, f32[14,768]{1,0:T(8,128)S(1)}, u32[]{:S(2)}, u32[]{:S(2)}) collective-permute-start(f32[14,768]{1,0:T(8,128)S(1)} %add.102), channel_id=1, source_target_pairs={{0,2},{1,3},{2,0},{3,1},{4,6},{5,7},{6,4},{7,5},{8,10},{9,11},{10,... | collective-permute-start | bytes 129032 | tf_op jit(solution)/shard_map/ppermute | solution.py:60
  127.6 4.2 %collective-permute-start.24 = (f32[14,768]{1,0:T(8,128)S(1)}, f32[14,768]{1,0:T(8,128)S(1)}, u32[]{:S(2)}, u32[]{:S(2)}) collective-permute-start(f32[14,768]{1,0:T(8,128)S(1)} %add.103), channel_id=1, source_target_pairs={{0,4},{4,0},{8,12},{12,8},{1,5},{5,1},{9,13},{13,9},{2,6},{6,2},{1... | collective-permute-start | bytes 129032 | tf_op jit(solution)/shard_map/ppermute | solution.py:60
  131.8 34.8 %collective-permute-start.19 = (bf16[624,384]{1,0:T(8,128)(2,1)S(1)}, bf16[624,384]{1,0:T(8,128)(2,1)}, u32[]{:S(2)}, u32[]{:S(2)}) collective-permute-start(bf16[624,384]{1,0:T(8,128)(2,1)S(1)} %add.98), channel_id=1, source_target_pairs={{0,2},{1,3},{2,0},{3,1},{4,6},{5,7},{6,4},{7,5},{8,10},{9,11},{10,... | collective-permute-start | bytes 1437704 | tf_op jit(solution)/shard_map/ppermute | solution.py:60
  132.7 11.9 %collective-permute-start.25 = (f32[14,768]{1,0:T(8,128)S(1)}, f32[14,768]{1,0:T(8,128)S(1)}, u32[]{:S(2)}, u32[]{:S(2)}) collective-permute-start(f32[14,768]{1,0:T(8,128)S(1)} %add.104), channel_id=1, source_target_pairs={{0,8},{4,12},{8,0},{12,4},{1,9},{5,13},{9,1},{13,5},{2,10},{6,14},... | collective-permute-start | bytes 129032 | tf_op jit(solution)/shard_map/ppermute | solution.py:60
  141.3 13.4 %collective-permute-start.30 = (bf16[192,768]{1,0:T(8,128)(2,1)}, bf16[192,768]{1,0:T(8,128)(2,1)S(1)}, u32[]{:S(2)}, u32[]{:S(2)}) collective-permute-start(bf16[192,768]{1,0:T(8,128)(2,1)} %add.108), channel_id=1, source_target_pairs={{0,0},{1,9},{2,6},{3,15},{4,4},{5,13},{6,2},{7,11},{8,8},{9,1},{10... | collective-permute-start | bytes 884744 | tf_op jit(solution)/shard_map/ppermute | solution.py:49
  144.7 14.9 %collective-permute-start.28 = (bf16[192,768]{1,0:T(8,128)(2,1)}, bf16[192,768]{1,0:T(8,128)(2,1)}, u32[]{:S(2)}, u32[]{:S(2)}) collective-permute-start(bf16[192,768]{1,0:T(8,128)(2,1)} %add.107), channel_id=1, source_target_pairs={{0,2},{1,11},{2,4},{3,13},{4,6},{5,15},{6,0},{7,9},{8,10},{9,3},{1... | collective-permute-start | bytes 884744 | tf_op jit(solution)/shard_map/ppermute | solution.py:49
  146.8 18.3 %collective-permute-start.26 = (f32[14,768]{1,0:T(8,128)S(1)}, f32[14,768]{1,0:T(8,128)}, u32[]{:S(2)}, u32[]{:S(2)}) collective-permute-start(f32[14,768]{1,0:T(8,128)S(1)} %add.105), channel_id=1, source_target_pairs={{0,16},{16,0},{1,17},{17,1},{2,18},{18,2},{3,19},{19,3},{4,20},{20... | collective-permute-start | bytes 129032 | tf_op jit(solution)/shard_map/ppermute | solution.py:60
  149.7 24.2 %collective-permute-start.34 = (bf16[192,1536]{1,0:T(8,128)(2,1)}, bf16[192,1536]{1,0:T(8,128)(2,1)S(1)}, u32[]{:S(2)}, u32[]{:S(2)}) collective-permute-start(bf16[192,1536]{1,0:T(8,128)(2,1)} %add.113), channel_id=1, source_target_pairs={{0,0},{1,9},{2,6},{3,15},{4,4},{5,13},{6,2},{7,11},{8,8},{9,1},{10... | collective-permute-start | bytes 1769480 | tf_op jit(solution)/shard_map/ppermute | solution.py:49
  160.7 13.2 %collective-permute-start.31 = (bf16[192,768]{1,0:T(8,128)(2,1)S(1)}, bf16[192,768]{1,0:T(8,128)(2,1)S(1)}, u32[]{:S(2)}, u32[]{:S(2)}) collective-permute-start(bf16[192,768]{1,0:T(8,128)(2,1)S(1)} %add.109), channel_id=1, source_target_pairs={{0,16},{16,0},{1,17},{17,1},{2,18},{18,2},{3,19},{19,3},{4,20},{20... | collective-permute-start | bytes 884744 | tf_op jit(solution)/shard_map/ppermute | solution.py:60
  167.8 18.5 %collective-permute-start.32 = (bf16[192,1536]{1,0:T(8,128)(2,1)S(1)}, bf16[192,1536]{1,0:T(8,128)(2,1)S(1)}, u32[]{:S(2)}, u32[]{:S(2)}) collective-permute-start(bf16[192,1536]{1,0:T(8,128)(2,1)S(1)} %add.100), channel_id=1, source_target_pairs={{0,2},{1,11},{2,4},{3,13},{4,6},{5,15},{6,0},{7,9},{8,10},{9,3},{1... | collective-permute-start | bytes 1769480 | tf_op jit(solution)/shard_map/ppermute | solution.py:49
  173.9 14.5 %collective-permute-start.20 = (bf16[624,384]{1,0:T(8,128)(2,1)S(1)}, bf16[624,384]{1,0:T(8,128)(2,1)}, u32[]{:S(2)}, u32[]{:S(2)}) collective-permute-start(bf16[624,384]{1,0:T(8,128)(2,1)S(1)} %add.99.one), channel_id=1, source_target_pairs={{0,1},{1,0},{2,3},{3,2},{4,5},{5,4},{6,7},{7,6},{8,9},{9,8},{10,11... | collective-permute-start | bytes 1437704 | tf_op jit(solution)/shard_map/ppermute | solution.py:60
  186.4 13.1 %collective-permute-start.35 = (bf16[192,1536]{1,0:T(8,128)(2,1)S(1)}, bf16[192,1536]{1,0:T(8,128)(2,1)S(1)}, u32[]{:S(2)}, u32[]{:S(2)}) collective-permute-start(bf16[192,1536]{1,0:T(8,128)(2,1)S(1)} %add.114), channel_id=1, source_target_pairs={{0,16},{16,0},{1,17},{17,1},{2,18},{18,2},{3,19},{19,3},{4,20},{20... | collective-permute-start | bytes 1769480 | tf_op jit(solution)/shard_map/ppermute | solution.py:60
  (38 other events, 423.2 us)

commit v2 on v1

--- a/solution.py
+++ b/solution.py
@@ -9,6 +9,8 @@
 SEQ = 197
 PAD = 208
 LANES = 128
+SUMS = 16
+CUT = 320
 EPS = 1e-06
 BF = jnp.bfloat16
 F32 = jnp.float32
@@ -75,8 +77,7 @@
     return pieces
 
 
-def finish(grid, parts):
-    total = parts[0] + parts[1]
+def finish(grid, total):
     step = 2
     while step < grid.dps:
         total = total + grid.swap(total, "dp", step)
@@ -93,12 +94,10 @@
     return mine, total
 
 
-def sum_all(grid, array):
-    for axis in ("col", "row", "dp"):
-        step = 1
-        while step < lax.axis_size(axis):
-            array = array + grid.swap(array, axis, step)
-            step *= 2
+def sum_axis(grid, array, axis, step):
+    while step < lax.axis_size(axis):
+        array = array + grid.swap(array, axis, step)
+        step *= 2
     return array
 
 
@@ -246,13 +245,10 @@
     activ, slope = gelu_parts(dot(second, full[:, :width], (1, 0)) + bias[...])
     hidden_out[...] = activ.astype(BF)
     grad_pre = dot(cot[...], full[:, width:], (1, 0)) * slope
-    sums[0:1, :] += columns_sum(grad_pre)
+    sums[...] += columns_sum(grad_pre)
     grad_pre = grad_pre.astype(BF)
     pre_out[...] = grad_pre
-    grad_normed = dot(grad_pre, full[:, :width], (1, 1))
-    sums[1:2, :] += columns_sum(grad_normed * centred)
-    sums[2:3, :] += columns_sum(grad_normed)
-    split_halves(ids, grad_normed.astype(BF), mine, away)
+    split_halves(ids, dot(grad_pre, full[:, :width], (1, 1)).astype(BF), mine, away)
 
 
 def shrink_kernel(ids, hidden, full, bias, mine, away):
@@ -273,7 +269,7 @@
     deal(ids, full, s0, s1, a0, a1)
 
 
-def joined_outer_kernel(ids, first, joined, grad_mid, attended, s0, s1, a0, a1, full):
+def joined_outer_kernel(ids, first, joined, grad_mid, attended, sums, pre_sum, cot_sum, s0, s1, away, full):
     full[...] = dot(first[...], joined[...], (0, 0)).astype(BF)
     other = dot(grad_mid[...], attended[...], (0, 0))
     turned = (pltpu.roll(other[:, :LANES], HD, 1), other[:, :LANES], pltpu.roll(other[:, LANES:], HD, 1))
@@ -281,7 +277,13 @@
         lanes = pl.ds((2 * i + 1) * LANES, LANES)
         is_low = low_lanes(values.shape)
         full[:, lanes] = jnp.where(is_low, full[:, lanes].astype(F32), values).astype(BF)
-    deal(ids, full, s0, s1, a0, a1)
+    size = s0.shape[0] - SUMS
+    blank = jnp.zeros((SUMS - 6, full.shape[1]), F32)
+    below = jnp.concatenate([sums[...], pre_sum[...], cot_sum[...], blank], axis=0).astype(BF)
+    places = (s0, s1, away.at[pl.ds(0, size + SUMS)], away.at[pl.ds(size + SUMS, size + SUMS)])
+    deal(ids, full, *(ref.at[pl.ds(0, size)] for ref in places))
+    for ref in places:
+        ref[pl.ds(size, SUMS), :] = below
 
 
 def attend_back_kernel(
@@ -317,8 +319,8 @@
         [(queries[0] + queries[1]) * scale, queries[2] * scale, keys[0] + keys[1], keys[2], values[0] + values[1], values[2]],
         axis=1,
     )
-    sums[0:1, :] += columns_sum(grad_mid)
-    sums[1:2, :] += columns_sum(result)
+    for i, values in enumerate((grad_normed * centred, grad_normed, grad_mid, result)):
+        sums[i : i + 1, :] += columns_sum(values)
     result = result.astype(BF)
     grad_joined_out[...] = result
     split_halves(ids, dot(result, full[...], (1, 1)).astype(BF), mine, away)
@@ -333,24 +335,12 @@
     leave(mid[...] + join_halves(ids, one, two), out)
 
 
-def exit_kernel(ids, one, two, grad_mid, tokens, gain, out):
+def exit_kernel(ids, one, upper, lower, grad_mid, tokens, gain, out, sums):
+    two = jnp.concatenate([upper[...].astype(F32), lower[...].astype(F32)], axis=0)
     grad_normed = join_halves(ids, one, two)
     centred, inverse = normalize(tokens[...].astype(F32))
     leave(grad_mid[...] + norm_back(grad_normed, centred, inverse, gain[...]), out)
-
-
-def sums_kernel(ids, mine, away, tokens, block, cot_sum, mlp_sums, back_sums, out):
-    share = 1.0 / ((out.shape[0] - 6) // 2)
-    grad_normed = join_halves(ids, mine, away)
-    centred, _ = normalize(tokens[...].astype(F32))
-    out[...] = jnp.zeros_like(out)
-    out[0:1, :] = columns_sum(grad_normed * centred)
-    out[1:2, :] = columns_sum(grad_normed)
-    out[2:4, :] = mlp_sums[1:3, :]
-    out[4:5, :] = back_sums[0:1, :] * share
-    out[5:6, :] = cot_sum[...] * share
-    out[pl.ds(6 + 2 * block[0], 1), :] = back_sums[1:2, :]
-    out[pl.ds(7 + 2 * block[0], 1), :] = mlp_sums[0:1, :]
+    sums[...] = jnp.concatenate([columns_sum(grad_normed * centred), columns_sum(grad_normed)], axis=0)
 
 
 def run(kernel, ids, args, outs, flops, images=None, scratch=()):
@@ -479,14 +469,14 @@
             (((rows, hidden_here), BF), 1),
         ]
         + halves
-        + [(((3, hidden_here), F32), 0)],
+        + [(((1, hidden_here), F32), 0)],
         2 * rows * model * hidden_here * 3,
         images,
         [pltpu.SemaphoreType.DMA((4,))],
     )
 
-    def pieces(width):
-        return [(((model // grid.cols, width), BF), 0)] * 4
+    def pieces(width, more=0):
+        return [(((model // grid.cols + more, width), BF), 0)] * 4
 
     mine, one = sum_two(grid, mine, away)
     hidden = after(hidden, mine)
@@ -499,75 +489,72 @@
         scratch=[pltpu.VMEM((model, 2 * hidden_here), BF)],
     )
     got = [grid.swap(a, "dp", 1) for a in parts[2:]]
+    one = after(one, parts[0])
+    two = grid.swap(one, "col", 1)
+
+    grad_mid, grad_mid_b, grad_joined, mine, away, back_sums = run(
+        attend_back_kernel,
+        ids,
+        [(one, 1), (two, 1), (mid, 1), (cot, 1), (line(mlp_gain), 0), (full, 0), (proj, 0), (joined, 1), (probs, 1)],
+        [(((rows, model), F32), 1), (((rows, model), BF), 1), (((rows, model), BF), 1)]
+        + halves
+        + [(((4, model), F32), 0)],
+        2 * rows * model * (model + 2 * wide),
+        images,
+    )
+    sooner = after(parts[0], grad_joined) + got[0]
+    packed_parts = run(
+        joined_outer_kernel,
+        ids,
+        [(first_in, 0), (grad_joined, 0), (grad_mid_b, 0), (attended, 0)]
+        + [(back_sums, 0), (mlp_sums, 0), (cot_sum, 0)],
+        pieces(model, SUMS)[:2] + [(((2 * (model // grid.cols + SUMS), model), BF), 0)],
+        2 * rows * model * model,
+        scratch=[pltpu.VMEM((model, model), BF)],
+    )
+    packed_got = grid.swap(packed_parts[2], "dp", 1)
+    packed_got = packed_got[: model // grid.cols + SUMS], packed_got[model // grid.cols + SUMS :]
     mine_out, away_out = run(
         shrink_kernel,
         ids,
-        [(after(hidden, parts[0]), 1), (wide_full, 0), (spread(shrink_bias), 0)],
+        [(after(hidden, packed_parts[0]), 1), (wide_full, 0), (spread(shrink_bias), 0)],
         halves,
         2 * rows * model * hidden_here,
         images,
     )
-    mine_out, out_one = sum_two(grid, mine_out, away_out)
-    one = after(one, away_out)
-    two = grid.swap(one, "col", 1)
-
-    grad_mid, grad_mid_b, grad_joined, mine, away, back_sums = run(
-        attend_back_kernel,
-        ids,
-        [(one, 1), (two, 1), (mid, 1), (cot, 1), (line(mlp_gain), 0), (full, 0), (proj, 0), (joined, 1), (probs, 1)],
-        [(((rows, model), F32), 1), (((rows, model), BF), 1), (((rows, model), BF), 1)]
-        + halves
-        + [(((2, model), F32), 0)],
-        2 * rows * model * (model + 2 * wide),
-        images,
-    )
-    packed_parts = run(
-        joined_outer_kernel,
-        ids,
-        [(first_in, 0), (grad_joined, 0), (grad_mid_b, 0), (attended, 0)],
-        pieces(model),
-        2 * rows * model * model,
-        scratch=[pltpu.VMEM((model, model), BF)],
-    )
-    packed_got = [grid.swap(a, "dp", 1) for a in packed_parts[2:]]
-    partial, away_here = mine, away
-    away = after(away, packed_parts[0], out_one)
+    later = after(parts[1], packed_parts[0]) + got[1]
+    away = after(away, packed_parts[0], later, away_out)
+    sooner, later = grid.give(sooner, BASES[0]), grid.give(later, BASES[1])
     mine, one = sum_two(grid, mine, away)
-    parts = after(parts, mine)
-    pairs = [parts[i] + got[i] for i in range(2)]
-    later = grid.give(pairs[1], BASES[1])
-    assert hidden_here == model
-    (totals,) = run(
-        sums_kernel,
-        ids,
-        [(after(partial, pairs[0]), 0), (away_here, 0), (tokens_pad, 0)]
-        + [(grid.block.reshape(1).astype(jnp.int32), 3), (cot_sum, 0), (mlp_sums, 0), (back_sums, 0)],
-        [(((6 + 2 * grid.rows, model), F32), 0)],
-        rows * model * 10,
-    )
-    totals = sum_all(grid, totals)
-    packed_pairs = [packed_parts[i] + packed_got[i] for i in range(2)]
-    two = grid.swap(one, "col", 1)
-    pairs[0] = after(pairs[0], one)
-    sooner = grid.give(pairs[0], BASES[0])
-    grad_packed = finish(grid, [grid.give(pair, base) for pair, base in zip(packed_pairs, BASES)])
-    (grad_tokens,) = run(
+    _, out_one = sum_two(grid, mine_out, after(away_out, mine))
+    packed_one = after(packed_parts[0], mine, sooner) + packed_got[0]
+    packed_two = after(packed_parts[1], packed_one) + packed_got[1]
+    packed_given = [grid.give(packed_one, BASES[0]), grid.give(packed_two, BASES[1])]
+    total = after(sooner, packed_two, one) + later
+    one = after(one, total)
+    grad_tokens, late = run(
         exit_kernel,
         ids,
-        [(one, 0), (two, 0), (grad_mid, 0), (tokens_pad, 0), (line(attn_gain), 0)],
-        [((tokens.shape, BF), 0)],
+        [(after(one, packed_two), 0)]
+        + [(grid.swap(part, "col", 1), 0) for part in (one[:CUT], one[CUT:])]
+        + [(grad_mid, 0), (tokens_pad, 0), (line(attn_gain), 0)],
+        [((tokens.shape, BF), 0), (((2, model), F32), 0)],
         rows * model * 20,
     )
+    grad_both = finish(grid, total)
+    packed_total = after(packed_given[0], grad_both, grad_tokens) + packed_given[1]
     (output,) = run(
         output_kernel,
         ids,
-        [(out_one, 0), (grid.swap(out_one, "col", 1), 0), (mid, 0)],
+        [(after(out_one, packed_total), 0), (grid.swap(out_one, "col", 1), 0), (mid, 0)],
         [((tokens.shape, BF), 0)],
         rows * model,
     )
-    grad_both = finish(grid, [sooner, later])
+    grad_packed = finish(grid, packed_total)
+    late = sum((grid.swap(late, "row", flip) for flip in range(1, grid.rows)), late)
+    late = sum_axis(grid, after(late, grad_both, output), "dp", 1)
+    whole, grad_packed = grad_packed[model // grid.cols :], grad_packed[: model // grid.cols]
     step = wide + HD
-    blocks = lax.dynamic_slice_in_dim(totals, 6 + 2 * grid.row, 2, 0)
 
     def own_columns(vector):
         width = vector.shape[0] // grid.cols
@@ -577,21 +564,21 @@
     return (
         output,
         grad_tokens,
-        totals[0],
-        totals[1],
+        late[0],
+        late[1],
         grad_packed[:, :wide],
         grad_packed[:, step : step + wide],
         grad_packed[:, 2 * step : 2 * step + wide],
-        blocks[0, :wide],
-        blocks[0, 2 * step : 2 * step + wide],
+        whole[3, :wide],
+        whole[3, 2 * step : 2 * step + wide],
         grad_proj,
-        own_columns(totals[4]),
-        totals[2],
-        totals[3],
+        own_columns(whole[2]),
+        whole[0],
+        whole[1],
         grad_both[:, :hidden_here],
-        blocks[1],
+        whole[4],
         grad_both[:, hidden_here:],
-        own_columns(totals[5]),
+        own_columns(whole[5]),
     )
 
 

time: 203 us -> 179 us (0.88); the launches traced: 201 us -> 179 us
  waiting for transfers between devices: 57.5 us -> 47.1 us
  other arithmetic: 14.9 us -> 6.96 us
  starting transfers between devices: 56.7 us -> 53.5 us
  local copies, waits for them, and re-layouts: 15.9 us -> 18.9 us
  Pallas kernels: 53.8 us -> 51.1 us
    ppermute x4, waiting for transfers between devices: 17.2 us -> 0.01 us  [give(): lax.ppermute(array, ('dp', 'row', 'col'), [(me, holder) for me, holder in...]
    add x11 -> x8, other arithmetic: 8.6 us -> 1.64 us  [the longest x1 1.05 us: on_device(): after(packed_given[0], grad_both, grad_tokens) + packed_given[1]]
    ppermute x27 -> x26, waiting for transfers between devices: 34.2 us -> 40.9 us  [swap(): return lax.ppermute(array, axis, [(i, i ^ flip) for i in range(size)])]
    ppermute x4, starting transfers between devices: 10.4 us -> 4.03 us  [give(): lax.ppermute(array, ('dp', 'row', 'col'), [(me, holder) for me, holder in...]
    ppermute x27 -> x26, starting transfers between devices: 34.2 us -> 37.6 us  [swap(): return lax.ppermute(array, axis, [(i, i ^ flip) for i in range(size)])]
    pallas_call x10 -> x9, Pallas kernels: 53.8 us -> 51.1 us  [run(): pl.pallas_call(kernel, out_shape=shapes, in_specs=in_specs, out_specs=[sp...]
  transfers between devices with their start and end apart: 36 -> 35, of which waited for: 14 -> 15; matrix products, arithmetic and copies ran while one was open for 12% -> 10% of each run, Pallas kernels for 23% -> 22%
where the time goes in v2:
time: 179 us
  starting transfers between devices  53.5 us (30%)
  Pallas kernels  51.1 us (29%)
  waiting for transfers between devices  47.1 us (26%)
  local copies, waits for them, and re-layouts  18.9 us (11%)
  other arithmetic  6.96 us (4%)
    pallas_call x9, Pallas kernels, run(): pl.pallas_call(kernel, out_shape=shapes, in_specs=in_specs, out_specs=[sp...  51.1 us
    ppermute x26, waiting for transfers between devices, swap(): return lax.ppermute(array, axis, [(i, i ^ flip) for i in range(size)])  40.9 us
    ppermute x26, starting transfers between devices, swap(): return lax.ppermute(array, axis, [(i, i ^ flip) for i in range(size)])  37.6 us
    ppermute x4, starting transfers between devices, fetch(): lax.ppermute(array, ('dp', 'row', 'col'), [(holder, me) for me, holder in...  11.2 us
    ppermute x4, waiting for transfers between devices, fetch(): lax.ppermute(array, ('dp', 'row', 'col'), [(holder, me) for me, holder in...  6.26 us
    unnamed x70, local copies, waits for them, and re-layouts  5.92 us
    ppermute x4, starting transfers between devices, give(): lax.ppermute(array, ('dp', 'row', 'col'), [(me, holder) for me, holder in...  4.03 us
    reshape x6, local copies, waits for them, and re-layouts, line(): return vector.reshape(1, -1)  3.6 us
  transfers between devices with their start and end apart: 35, of which 15 were waited for; matrix products, arithmetic and copies ran while one was open for 10% of the time, Pallas kernels for 22%

profile of v2, /device:TPU:0, one launch (start us, length us, event | category | flops | bytes accessed | tf_op | source)
XLA Modules:
  0.0 178.8 jit_solution(10437308032528684382)
XLA Ops:
  3.0 4.0 %collective-permute-start = (bf16[192,768]{1,0:T(8,128)(2,1)S(1)}, bf16[192,768]{1,0:T(8,128)(2,1)S(1)}, u32[]{:S(2)}, u32[]{:S(2)}) collective-permute-start(bf16[192,768]{1,0:T(8,128)(2,1)S(1)} %concatenate.15), channel_id=1, source_target_pairs={{2,0},{11,1},{4,2},{13,3},{6,4},{15,5},{0,6},{9,7},{10,8},{3,9},{1... | collective-permute-start | bytes 884744 | tf_op jit(solution)/shard_map/ppermute | solution.py:48
  7.8 5.8 %collective-permute-done.h0 = bf16[192,768]{1,0:T(8,128)(2,1)S(1)} collective-permute-done((bf16[192,768]{1,0:T(8,128)(2,1)S(1)}, bf16[192,768]{1,0:T(8,128)(2,1)S(1)}, u32[]{:S(2)}, u32[]{:S(2)}) %collective-permute-start) | collective-permute-done | bytes 294944 | tf_op jit(solution)/shard_map/ppermute | solution.py:48
  13.6 5.8 %collective-permute-start.2 = (bf16[192,1536]{1,0:T(8,128)(2,1)S(1)}, bf16[192,1536]{1,0:T(8,128)(2,1)S(1)}, u32[]{:S(2)}, u32[]{:S(2)}) collective-permute-start(bf16[192,1536]{1,0:T(8,128)(2,1)S(1)} %pad_maximum_fusion), channel_id=1, source_target_pairs={{2,0},{11,1},{4,2},{13,3},{6,4},{15,5},{0,6},{9,7},{10,8},{3,9},{1... | collective-permute-start | bytes 1769480 | tf_op jit(solution)/shard_map/ppermute | solution.py:48
  20.8 4.0 %collective-permute-start.3 = (bf16[192,768]{1,0:T(8,128)(2,1)S(1)}, bf16[192,768]{1,0:T(8,128)(2,1)S(1)}, u32[]{:S(2)}, u32[]{:S(2)}) collective-permute-start(bf16[192,768]{1,0:T(8,128)(2,1)S(1)} %collective-permute-done.h0), channel_id=1, source_target_pairs={{0,16},{16,0},{1,17},{17,1},{2,18},{18,2},{3,19},{19,3},{4,20},{20... | collective-permute-start | bytes 884744 | tf_op jit(solution)/shard_map/ppermute | solution.py:62
  26.7 3.9 %shard_map.296 = (bf16[624,768]{1,0:T(8,128)(2,1)}, bf16[624,768]{1,0:T(8,128)(2,1)}, bf16[624,768]{1,0:T(8,128)(2,1)}, f32[1,768]{1,0:T(1,128)}) custom-call(bf16[591,768]{1,0:T(8,128)(2,1)} %tokens.1, bf16[591,768]{1,0:T(8,128)(2,1)} %cot.1, f32[1,768]{1,0:T(1,128)} %reshape.118.gain, f32[1,768]{1,0:T(1,128)} %reshape.119.shift), custom_call_target="tpu_custom_call" | custom-call | flops 1 | bytes 1 | tf_op jit(solution)/shard_map/pallas_call | solution.py:367
  31.7 6.7 %collective-permute-start.7 = (bf16[192,1536]{1,0:T(8,128)(2,1)S(1)}, bf16[192,1536]{1,0:T(8,128)(2,1)S(1)}, u32[]{:S(2)}, u32[]{:S(2)}) collective-permute-start(bf16[192,1536]{1,0:T(8,128)(2,1)S(1)} %collective-permute-done.2.w0), channel_id=1, source_target_pairs={{0,16},{16,0},{1,17},{17,1},{2,18},{18,2},{3,19},{19,3},{4,20},{20... | collective-permute-start | bytes 1769480 | tf_op jit(solution)/shard_map/ppermute | solution.py:62
  41.8 7.3 %shard_map.297 = (bf16[768,768]{1,0:T(8,128)(2,1)}, bf16[768,256]{1,0:T(8,128)(2,1)}, bf16[624,768]{1,0:T(8,128)(2,1)}, bf16[624,256]{1,0:T(8,128)(2,1)}, bf16[9...) custom-call(s32[2]{0:T(128)} %pad_add_fusion.ids, ...), custom_call_target="tpu_custom_call" | custom-call | flops 1 | bytes 1 | tf_op jit(solution)/shard_map/pallas_call | solution.py:367
  51.3 1.2 add.81
  52.5 4.4 %collective-permute-start.9 = (bf16[624,384]{1,0:T(8,128)(2,1)S(1)}, bf16[624,384]{1,0:T(8,128)(2,1)S(1)}, u32[]{:S(2)}, u32[]{:S(2)}) collective-permute-start(bf16[624,384]{1,0:T(8,128)(2,1)S(1)} %add.81), channel_id=1, source_target_pairs={{0,2},{1,3},{2,0},{3,1},{4,6},{5,7},{6,4},{7,5},{8,10},{9,11},{10,... | collective-permute-start | bytes 1437704 | tf_op jit(solution)/shard_map/ppermute | solution.py:62
  56.9 10.5 %collective-permute-done.9 = bf16[624,384]{1,0:T(8,128)(2,1)S(1)} collective-permute-done((bf16[624,384]{1,0:T(8,128)(2,1)S(1)}, bf16[624,384]{1,0:T(8,128)(2,1)S(1)}, u32[]{:S(2)}, u32[]{:S(2)}) %collective-permute-start.9) | collective-permute-done | bytes 479264 | tf_op jit(solution)/shard_map/ppermute | solution.py:62
  70.3 8.3 %shard_map.298 = (bf16[768,1536]{1,0:T(8,128)(2,1)}, f32[624,768]{1,0:T(8,128)}, bf16[624,768]{1,0:T(8,128)(2,1)}, bf16[624,768]{1,0:T(8,128)(2,1)}, bf16[624,76...) custom-call(s32[2]{0:T(128)} %pad_add_fusion.ids, ...), custom_call_target="tpu_custom_call" | custom-call | flops 1 | bytes 1 | tf_op jit(solution)/shard_map/pallas_call | solution.py:367
  79.1 1.7 collective-permute-done.12
  81.9 1.3 collective-permute-start.13
  83.2 5.5 %shard_map.299 = (bf16[192,1536]{1,0:T(8,128)(2,1)}, bf16[192,1536]{1,0:T(8,128)(2,1)}, bf16[192,1536]{1,0:T(8,128)(2,1)}, bf16[192,1536]{1,0:T(8,128)(2,1)}) custom-call(s32[2]{0:T(128)} %pad_add_fusion.ids, bf16[624,768]{1,0:T(8,128)(2,1)} %get-tuple-element.80.cot, bf16[624,768]{1,0:T(8,128)(2,1)} %get-tuple-element.101.hidden, ...), custom_call_target="tpu_custom_call" | custom-call | flops 1 | bytes 1 | tf_op jit(solution)/shard_map/pallas_call | solution.py:367
  89.9 5.3 %collective-permute-done.13 = bf16[624,384]{1,0:T(8,128)(2,1)S(1)} collective-permute-done((bf16[624,384]{1,0:T(8,128)(2,1)S(1)}, bf16[624,384]{1,0:T(8,128)(2,1)S(1)}, u32[]{:S(2)}, u32[]{:S(2)}) %collective-permute-start.13) | collective-permute-done | bytes 479264 | tf_op jit(solution)/shard_map/ppermute | solution.py:62
  98.1 9.2 %shard_map.300 = (f32[624,768]{1,0:T(8,128)}, bf16[624,768]{1,0:T(8,128)(2,1)}, bf16[624,768]{1,0:T(8,128)(2,1)}, bf16[624,384]{1,0:T(8,128)(2,1)}, bf16[624,384]{1,0:T(8,128)(2,1)}, /*index=5*/f32[4,768]{1,0:T(4,128)}) custom-call(s32[2]{0:T(128)} %pad_add_fusion.ids, bf16[624,384]{1,0:T(8,128)(2,1)} %copy-done.3, bf16[624,384]{1,0:T(8,128)(2,1)} %copy-done.13, ...), custom_call_target="tpu_custom_call" | custom-call | flops 1 | bytes 1 | tf_op jit(solution)/shard_map/pallas_call | solution.py:367
  107.4 1.3 collective-permute-start.20
  108.7 4.4 %shard_map.301 = (bf16[208,768]{1,0:T(8,128)(2,1)}, bf16[208,768]{1,0:T(8,128)(2,1)}, bf16[416,768]{1,0:T(8,128)(2,1)}) custom-call(s32[2]{0:T(128)} %pad_add_fusion.ids, bf16[624,768]{1,0:T(8,128)(2,1)} %get-tuple-element.73.first, bf16[624,768]{1,0:T(8,128)(2,1)} %get-tuple-element.94.joined, bf16[624,768]{1,0:T(8,128)(2,1)} %get-tuple-element.95.grad_mid, ...), custom_call_target="tpu_custom_call" | custom-call | flops 1 | bytes 1 | tf_op jit(solution)/shard_map/pallas_call | solution.py:367
  114.6 4.8 %shard_map.302 = (bf16[624,384]{1,0:T(8,128)(2,1)}, bf16[624,384]{1,0:T(8,128)(2,1)}) custom-call(s32[2]{0:T(128)} %pad_add_fusion.ids, bf16[624,768]{1,0:T(8,128)(2,1)} %get-tuple-element.101.hidden, bf16[768,1536]{1,0:T(8,128)(2,1)} %get-tuple-element.102.full, f32[1,768]{1,0:T(1,128)} %compare_select_fusion.bias), custom_call_target="tpu_custom_call" | custom-call | flops 1 | bytes 1 | tf_op jit(solution)/shard_map/pallas_call | solution.py:367
  122.4 2.0 %collective-permute-start.23 = (bf16[624,384]{1,0:T(8,128)(2,1)S(1)}, bf16[624,384]{1,0:T(8,128)(2,1)S(1)}, u32[]{:S(2)}, u32[]{:S(2)}) collective-permute-start(bf16[624,384]{1,0:T(8,128)(2,1)S(1)} %add.86), channel_id=1, source_target_pairs={{0,2},{1,3},{2,0},{3,1},{4,6},{5,7},{6,4},{7,5},{8,10},{9,11},{10,... | collective-permute-start | bytes 1437704 | tf_op jit(solution)/shard_map/ppermute | solution.py:62
  124.5 6.1 %collective-permute-done.21 = bf16[416,768]{1,0:T(8,128)(2,1)S(1)} collective-permute-done((bf16[416,768]{1,0:T(8,128)(2,1)}, bf16[416,768]{1,0:T(8,128)(2,1)S(1)}, u32[]{:S(2)}, u32[]{:S(2)}) %collective-permute-start.21) | collective-permute-done | bytes 639008 | tf_op jit(solution)/shard_map/ppermute | solution.py:62
  130.7 4.7 %collective-permute-done.23 = bf16[624,384]{1,0:T(8,128)(2,1)S(1)} collective-permute-done((bf16[624,384]{1,0:T(8,128)(2,1)S(1)}, bf16[624,384]{1,0:T(8,128)(2,1)S(1)}, u32[]{:S(2)}, u32[]{:S(2)}) %collective-permute-start.23) | collective-permute-done | bytes 479264 | tf_op jit(solution)/shard_map/ppermute | solution.py:62
  135.7 4.7 %collective-permute-start.25 = (bf16[192,1536]{1,0:T(8,128)(2,1)S(1)}, bf16[192,1536]{1,0:T(8,128)(2,1)S(1)}, u32[]{:S(2)}, u32[]{:S(2)}) collective-permute-start(bf16[192,1536]{1,0:T(8,128)(2,1)S(1)} %add.93), channel_id=1, source_target_pairs={{0,16},{16,0},{1,17},{17,1},{2,18},{18,2},{3,19},{19,3},{4,20},{20... | collective-permute-start | bytes 1769480 | tf_op jit(solution)/shard_map/ppermute | solution.py:62
  140.5 1.4 collective-permute-start.22
  145.3 2.8 %collective-permute-start.18 = (bf16[624,384]{1,0:T(8,128)(2,1)S(1)}, bf16[624,384]{1,0:T(8,128)(2,1)S(1)}, u32[]{:S(2)}, u32[]{:S(2)}) collective-permute-start(bf16[624,384]{1,0:T(8,128)(2,1)S(1)} %add.87), channel_id=1, source_target_pairs={{0,2},{1,3},{2,0},{3,1},{4,6},{5,7},{6,4},{7,5},{8,10},{9,11},{10,... | collective-permute-start | bytes 1437704 | tf_op jit(solution)/shard_map/ppermute | solution.py:62
  148.0 4.6 %shard_map.303 = (bf16[591,768]{1,0:T(8,128)(2,1)}, f32[2,768]{1,0:T(2,128)}) custom-call(s32[2]{0:T(128)} %pad_add_fusion.ids, bf16[624,384]{1,0:T(8,128)(2,1)} %copy-done, bf16[320,384]{1,0:T(8,128)(2,1)} %collective-permute-done.26.upper, bf16[304,384]{1,0:T(8,128)(2,1)} %collective-permute-done.27.lower, f32[624,768]{1,0:T(8,128)} %get-tuple-element.121.grad_mid, ...), custom_call_target="tpu_custom_call" | custom-call | flops 1 | bytes 1 | tf_op jit(solution)/shard_map/pallas_call | solution.py:367
  152.6 1.6 collective-permute-start.30
  155.1 1.9 %collective-permute-start.32 = (f32[2,768]{1,0:T(2,128)}, f32[2,768]{1,0:T(2,128)S(1)}, u32[]{:S(2)}, u32[]{:S(2)}) collective-permute-start(f32[2,768]{1,0:T(2,128)} %get-tuple-element.125), channel_id=1, source_target_pairs={{0,12},{4,8},{8,4},{12,0},{1,13},{5,9},{9,5},{13,1},{2,14},{6,10},... | collective-permute-start | bytes 18440 | tf_op jit(solution)/shard_map/ppermute | solution.py:62
  158.3 1.4 collective-permute-start.34
  163.5 4.9 %collective-permute-done.34 = bf16[208,768]{1,0:T(8,128)(2,1)S(1)} collective-permute-done((bf16[208,768]{1,0:T(8,128)(2,1)S(1)}, bf16[208,768]{1,0:T(8,128)(2,1)S(1)}, u32[]{:S(2)}, u32[]{:S(2)}) %collective-permute-start.34) | collective-permute-done | bytes 319520 | tf_op jit(solution)/shard_map/ppermute | solution.py:62
  171.5 3.1 %shard_map.304 = bf16[591,768]{1,0:T(8,128)(2,1)} custom-call(s32[2]{0:T(128)} %pad_add_fusion.ids, bf16[624,384]{1,0:T(8,128)(2,1)} %copy-done.1, bf16[624,384]{1,0:T(8,128)(2,1)} %copy-done.12, f32[624,768]{1,0:T(8,128)} %get-tuple-element.89.mid), custom_call_target="tpu_custom_call" | custom-call | flops 1 | bytes 1 | tf_op jit(solution)/shard_map/pallas_call | solution.py:367
  176.3 1.9 %collective-permute-done.33 = f32[2,768]{1,0:T(2,128)S(1)} collective-permute-done((f32[2,768]{1,0:T(2,128)S(1)}, f32[2,768]{1,0:T(2,128)S(1)}, u32[]{:S(2)}, u32[]{:S(2)}) %collective-permute-start.33) | collective-permute-done | bytes 6176 | tf_op jit(solution)/shard_map/ppermute | solution.py:62
  (167 shorter events, 41.0 us)
Async XLA Ops:
  3.0 10.5 %collective-permute-start = (bf16[192,768]{1,0:T(8,128)(2,1)S(1)}, bf16[192,768]{1,0:T(8,128)(2,1)S(1)}, u32[]{:S(2)}, u32[]{:S(2)}) collective-permute-start(bf16[192,768]{1,0:T(8,128)(2,1)S(1)} %concatenate.15), channel_id=1, source_target_pairs={{2,0},{11,1},{4,2},{13,3},{6,4},{15,5},{0,6},{9,7},{10,8},{3,9},{1... | collective-permute-start | bytes 884744 | tf_op jit(solution)/shard_map/ppermute | solution.py:48
  7.0 6.5 %collective-permute-start.1 = (bf16[192,768]{1,0:T(8,128)(2,1)S(1)}, bf16[192,768]{1,0:T(8,128)(2,1)S(1)}, u32[]{:S(2)}, u32[]{:S(2)}) collective-permute-start(bf16[192,768]{1,0:T(8,128)(2,1)S(1)} %concatenate.15), channel_id=1, source_target_pairs={{0,0},{9,1},{6,2},{15,3},{4,4},{13,5},{2,6},{11,7},{8,8},{1,9},{14... | collective-permute-start | bytes 884744 | tf_op jit(solution)/shard_map/ppermute | solution.py:48
  13.6 18.2 %collective-permute-start.2 = (bf16[192,1536]{1,0:T(8,128)(2,1)S(1)}, bf16[192,1536]{1,0:T(8,128)(2,1)S(1)}, u32[]{:S(2)}, u32[]{:S(2)}) collective-permute-start(bf16[192,1536]{1,0:T(8,128)(2,1)S(1)} %pad_maximum_fusion), channel_id=1, source_target_pairs={{2,0},{11,1},{4,2},{13,3},{6,4},{15,5},{0,6},{9,7},{10,8},{3,9},{1... | collective-permute-start | bytes 1769480 | tf_op jit(solution)/shard_map/ppermute | solution.py:48
  19.5 18.9 %collective-permute-start.5 = (f32[1152]{0:T(1024)S(1)}, f32[1152]{0:T(1024)S(1)}, u32[]{:S(2)}, u32[]{:S(2)}) collective-permute-start(f32[1152]{0:T(1024)S(1)} %concatenate.17), channel_id=1, source_target_pairs={{0,0},{9,1},{6,2},{15,3},{4,4},{13,5},{2,6},{11,7},{8,8},{1,9},{14... | collective-permute-start | bytes 13832 | tf_op jit(solution)/shard_map/ppermute | solution.py:58
  20.8 20.2 %collective-permute-start.3 = (bf16[192,768]{1,0:T(8,128)(2,1)S(1)}, bf16[192,768]{1,0:T(8,128)(2,1)S(1)}, u32[]{:S(2)}, u32[]{:S(2)}) collective-permute-start(bf16[192,768]{1,0:T(8,128)(2,1)S(1)} %collective-permute-done.h0), channel_id=1, source_target_pairs={{0,16},{16,0},{1,17},{17,1},{2,18},{18,2},{3,19},{19,3},{4,20},{20... | collective-permute-start | bytes 884744 | tf_op jit(solution)/shard_map/ppermute | solution.py:62
  24.8 16.2 %collective-permute-start.4 = (bf16[192,768]{1,0:T(8,128)(2,1)S(1)}, bf16[192,768]{1,0:T(8,128)(2,1)S(1)}, u32[]{:S(2)}, u32[]{:S(2)}) collective-permute-start(bf16[192,768]{1,0:T(8,128)(2,1)S(1)} %collective-permute-done.1.h2), channel_id=1, source_target_pairs={{0,16},{16,0},{1,17},{17,1},{2,18},{18,2},{3,19},{19,3},{4,20},{20... | collective-permute-start | bytes 884744 | tf_op jit(solution)/shard_map/ppermute | solution.py:62
  30.6 19.0 %collective-permute-start.8 = (bf16[192,1536]{1,0:T(8,128)(2,1)S(1)}, bf16[192,1536]{1,0:T(8,128)(2,1)S(1)}, u32[]{:S(2)}, u32[]{:S(2)}) collective-permute-start(bf16[192,1536]{1,0:T(8,128)(2,1)S(1)} %pad_maximum_fusion), channel_id=1, source_target_pairs={{0,0},{9,1},{6,2},{15,3},{4,4},{13,5},{2,6},{11,7},{8,8},{1,9},{14... | collective-permute-start | bytes 1769480 | tf_op jit(solution)/shard_map/ppermute | solution.py:48
  31.7 20.7 %collective-permute-start.7 = (bf16[192,1536]{1,0:T(8,128)(2,1)S(1)}, bf16[192,1536]{1,0:T(8,128)(2,1)S(1)}, u32[]{:S(2)}, u32[]{:S(2)}) collective-permute-start(bf16[192,1536]{1,0:T(8,128)(2,1)S(1)} %collective-permute-done.2.w0), channel_id=1, source_target_pairs={{0,16},{16,0},{1,17},{17,1},{2,18},{18,2},{3,19},{19,3},{4,20},{20... | collective-permute-start | bytes 1769480 | tf_op jit(solution)/shard_map/ppermute | solution.py:62
  49.1 2.1 %collective-permute-start.6 = (bf16[624,384]{1,0:T(8,128)(2,1)}, bf16[624,384]{1,0:T(8,128)(2,1)S(1)}, u32[]{:S(2)}, u32[]{:S(2)}) collective-permute-start(bf16[624,384]{1,0:T(8,128)(2,1)} %get-tuple-element.77), channel_id=1, source_target_pairs={{0,1},{1,0},{2,3},{3,2},{4,5},{5,4},{6,7},{7,6},{8,9},{9,8},{10,11... | collective-permute-start | bytes 1437704 | tf_op jit(solution)/shard_map/ppermute | solution.py:62
  49.6 18.0 %collective-permute-start.10 = (bf16[192,1536]{1,0:T(8,128)(2,1)S(1)}, bf16[192,1536]{1,0:T(8,128)(2,1)S(1)}, u32[]{:S(2)}, u32[]{:S(2)}) collective-permute-start(bf16[192,1536]{1,0:T(8,128)(2,1)S(1)} %collective-permute-done.8.w2), channel_id=1, source_target_pairs={{0,16},{16,0},{1,17},{17,1},{2,18},{18,2},{3,19},{19,3},{4,20},{20... | collective-permute-start | bytes 1769480 | tf_op jit(solution)/shard_map/ppermute | solution.py:62
  52.5 14.9 %collective-permute-start.9 = (bf16[624,384]{1,0:T(8,128)(2,1)S(1)}, bf16[624,384]{1,0:T(8,128)(2,1)S(1)}, u32[]{:S(2)}, u32[]{:S(2)}) collective-permute-start(bf16[624,384]{1,0:T(8,128)(2,1)S(1)} %add.81), channel_id=1, source_target_pairs={{0,2},{1,3},{2,0},{3,1},{4,6},{5,7},{6,4},{7,5},{8,10},{9,11},{10,... | collective-permute-start | bytes 1437704 | tf_op jit(solution)/shard_map/ppermute | solution.py:62
  78.6 2.1 %collective-permute-start.12 = (bf16[624,384]{1,0:T(8,128)(2,1)}, bf16[624,384]{1,0:T(8,128)(2,1)S(1)}, u32[]{:S(2)}, u32[]{:S(2)}) collective-permute-start(bf16[624,384]{1,0:T(8,128)(2,1)} %get-tuple-element.83), channel_id=1, source_target_pairs={{0,1},{1,0},{2,3},{3,2},{4,5},{5,4},{6,7},{7,6},{8,9},{9,8},{10,11... | collective-permute-start | bytes 1437704 | tf_op jit(solution)/shard_map/ppermute | solution.py:62
  81.9 13.3 %collective-permute-start.13 = (bf16[624,384]{1,0:T(8,128)(2,1)S(1)}, bf16[624,384]{1,0:T(8,128)(2,1)S(1)}, u32[]{:S(2)}, u32[]{:S(2)}) collective-permute-start(bf16[624,384]{1,0:T(8,128)(2,1)S(1)} %add.83), channel_id=1, source_target_pairs={{0,2},{1,3},{2,0},{3,1},{4,6},{5,7},{6,4},{7,5},{8,10},{9,11},{10,... | collective-permute-start | bytes 1437704 | tf_op jit(solution)/shard_map/ppermute | solution.py:62
  88.8 18.5 %collective-permute-start.19 = (bf16[192,1536]{1,0:T(8,128)(2,1)}, bf16[192,1536]{1,0:T(8,128)(2,1)S(1)}, u32[]{:S(2)}, u32[]{:S(2)}) collective-permute-start(bf16[192,1536]{1,0:T(8,128)(2,1)} %get-tuple-element.113), channel_id=1, source_target_pairs={{0,16},{16,0},{1,17},{17,1},{2,18},{18,2},{3,19},{19,3},{4,20},{20... | collective-permute-start | bytes 1769480 | tf_op jit(solution)/shard_map/ppermute | solution.py:62
  95.4 24.0 %collective-permute-start.15 = (bf16[192,1536]{1,0:T(8,128)(2,1)}, bf16[192,1536]{1,0:T(8,128)(2,1)S(1)}, u32[]{:S(2)}, u32[]{:S(2)}) collective-permute-start(bf16[192,1536]{1,0:T(8,128)(2,1)} %get-tuple-element.109), channel_id=1, source_target_pairs={{0,16},{16,0},{1,17},{17,1},{2,18},{18,2},{3,19},{19,3},{4,20},{20... | collective-permute-start | bytes 1769480 | tf_op jit(solution)/shard_map/ppermute | solution.py:62
  107.4 17.0 %collective-permute-start.20 = (bf16[192,1536]{1,0:T(8,128)(2,1)S(1)}, bf16[192,1536]{1,0:T(8,128)(2,1)S(1)}, u32[]{:S(2)}, u32[]{:S(2)}) collective-permute-start(bf16[192,1536]{1,0:T(8,128)(2,1)S(1)} %add.89), channel_id=1, source_target_pairs={{0,2},{1,11},{2,4},{3,13},{4,6},{5,15},{6,0},{7,9},{8,10},{9,3},{1... | collective-permute-start | bytes 1769480 | tf_op jit(solution)/shard_map/ppermute | solution.py:51
  113.2 17.4 %collective-permute-start.21 = (bf16[416,768]{1,0:T(8,128)(2,1)}, bf16[416,768]{1,0:T(8,128)(2,1)S(1)}, u32[]{:S(2)}, u32[]{:S(2)}) collective-permute-start(bf16[416,768]{1,0:T(8,128)(2,1)} %get-tuple-element.115), channel_id=1, source_target_pairs={{0,16},{16,0},{1,17},{17,1},{2,18},{18,2},{3,19},{19,3},{4,20},{20... | collective-permute-start | bytes 1916936 | tf_op jit(solution)/shard_map/ppermute | solution.py:62
  120.8 14.7 %collective-permute-start.24 = (bf16[192,1536]{1,0:T(8,128)(2,1)S(1)}, bf16[192,1536]{1,0:T(8,128)(2,1)S(1)}, u32[]{:S(2)}, u32[]{:S(2)}) collective-permute-start(bf16[192,1536]{1,0:T(8,128)(2,1)S(1)} %add.85), channel_id=1, source_target_pairs={{0,0},{1,9},{2,6},{3,15},{4,4},{5,13},{6,2},{7,11},{8,8},{9,1},{10... | collective-permute-start | bytes 1769480 | tf_op jit(solution)/shard_map/ppermute | solution.py:51
  122.4 13.0 %collective-permute-start.23 = (bf16[624,384]{1,0:T(8,128)(2,1)S(1)}, bf16[624,384]{1,0:T(8,128)(2,1)S(1)}, u32[]{:S(2)}, u32[]{:S(2)}) collective-permute-start(bf16[624,384]{1,0:T(8,128)(2,1)S(1)} %add.86), channel_id=1, source_target_pairs={{0,2},{1,3},{2,0},{3,1},{4,6},{5,7},{6,4},{7,5},{8,10},{9,11},{10,... | collective-permute-start | bytes 1437704 | tf_op jit(solution)/shard_map/ppermute | solution.py:62
  135.7 19.3 %collective-permute-start.25 = (bf16[192,1536]{1,0:T(8,128)(2,1)S(1)}, bf16[192,1536]{1,0:T(8,128)(2,1)S(1)}, u32[]{:S(2)}, u32[]{:S(2)}) collective-permute-start(bf16[192,1536]{1,0:T(8,128)(2,1)S(1)} %add.93), channel_id=1, source_target_pairs={{0,16},{16,0},{1,17},{17,1},{2,18},{18,2},{3,19},{19,3},{4,20},{20... | collective-permute-start | bytes 1769480 | tf_op jit(solution)/shard_map/ppermute | solution.py:62
  140.5 3.3 %collective-permute-start.17 = (bf16[624,384]{1,0:T(8,128)(2,1)}, bf16[624,384]{1,0:T(8,128)(2,1)S(1)}, u32[]{:S(2)}, u32[]{:S(2)}) collective-permute-start(bf16[624,384]{1,0:T(8,128)(2,1)} %get-tuple-element.111), channel_id=1, source_target_pairs={{0,1},{1,0},{2,3},{3,2},{4,5},{5,4},{6,7},{7,6},{8,9},{9,8},{10,11... | collective-permute-start | bytes 1437704 | tf_op jit(solution)/shard_map/ppermute | solution.py:62
  140.5 13.8 %collective-permute-start.22 = (bf16[208,768]{1,0:T(8,128)(2,1)S(1)}, bf16[208,768]{1,0:T(8,128)(2,1)}, u32[]{:S(2)}, u32[]{:S(2)}) collective-permute-start(bf16[208,768]{1,0:T(8,128)(2,1)S(1)} %slice_add_fusion.1), channel_id=1, source_target_pairs={{0,2},{1,11},{2,4},{3,13},{4,6},{5,15},{6,0},{7,9},{8,10},{9,3},{1... | collective-permute-start | bytes 958472 | tf_op jit(solution)/shard_map/ppermute | solution.py:51
  142.6 5.5 %collective-permute-start.26 = (bf16[320,384]{1,0:T(8,128)(2,1)}, bf16[320,384]{1,0:T(8,128)(2,1)}, u32[]{:S(2)}, u32[]{:S(2)}) collective-permute-start(bf16[320,384]{1,0:T(8,128)(2,1)} %slice.104), channel_id=1, source_target_pairs={{0,1},{1,0},{2,3},{3,2},{4,5},{5,4},{6,7},{7,6},{8,9},{9,8},{10,11... | collective-permute-start | bytes 737288 | tf_op jit(solution)/shard_map/ppermute | solution.py:62
  143.3 2.0 %collective-permute-start.27 = (bf16[304,384]{1,0:T(8,128)(2,1)}, bf16[304,384]{1,0:T(8,128)(2,1)}, u32[]{:S(2)}, u32[]{:S(2)}) collective-permute-start(bf16[304,384]{1,0:T(8,128)(2,1)} %slice.105), channel_id=1, source_target_pairs={{0,1},{1,0},{2,3},{3,2},{4,5},{5,4},{6,7},{7,6},{8,9},{9,8},{10,11... | collective-permute-start | bytes 700424 | tf_op jit(solution)/shard_map/ppermute | solution.py:62
  143.8 13.4 %collective-permute-start.28 = (bf16[208,768]{1,0:T(8,128)(2,1)S(1)}, bf16[208,768]{1,0:T(8,128)(2,1)S(1)}, u32[]{:S(2)}, u32[]{:S(2)}) collective-permute-start(bf16[208,768]{1,0:T(8,128)(2,1)S(1)} %slice_add_fusion), channel_id=1, source_target_pairs={{0,0},{1,9},{2,6},{3,15},{4,4},{5,13},{6,2},{7,11},{8,8},{9,1},{10... | collective-permute-start | bytes 958472 | tf_op jit(solution)/shard_map/ppermute | solution.py:51
  145.3 16.6 %collective-permute-start.18 = (bf16[624,384]{1,0:T(8,128)(2,1)S(1)}, bf16[624,384]{1,0:T(8,128)(2,1)S(1)}, u32[]{:S(2)}, u32[]{:S(2)}) collective-permute-start(bf16[624,384]{1,0:T(8,128)(2,1)S(1)} %add.87), channel_id=1, source_target_pairs={{0,2},{1,3},{2,0},{3,1},{4,6},{5,7},{6,4},{7,5},{8,10},{9,11},{10,... | collective-permute-start | bytes 1437704 | tf_op jit(solution)/shard_map/ppermute | solution.py:62
  152.6 7.1 %collective-permute-start.30 = (f32[2,768]{1,0:T(2,128)}, f32[2,768]{1,0:T(2,128)S(1)}, u32[]{:S(2)}, u32[]{:S(2)}) collective-permute-start(f32[2,768]{1,0:T(2,128)} %get-tuple-element.125), channel_id=1, source_target_pairs={{0,4},{4,0},{8,12},{12,8},{1,5},{5,1},{9,13},{13,9},{2,6},{6,2},{1... | collective-permute-start | bytes 18440 | tf_op jit(solution)/shard_map/ppermute | solution.py:62
  154.2 5.4 %collective-permute-start.31 = (f32[2,768]{1,0:T(2,128)}, f32[2,768]{1,0:T(2,128)S(1)}, u32[]{:S(2)}, u32[]{:S(2)}) collective-permute-start(f32[2,768]{1,0:T(2,128)} %get-tuple-element.125), channel_id=1, source_target_pairs={{0,8},{4,12},{8,0},{12,4},{1,9},{5,13},{9,1},{13,5},{2,10},{6,14},... | collective-permute-start | bytes 18440 | tf_op jit(solution)/shard_map/ppermute | solution.py:62
  155.1 5.6 %collective-permute-start.32 = (f32[2,768]{1,0:T(2,128)}, f32[2,768]{1,0:T(2,128)S(1)}, u32[]{:S(2)}, u32[]{:S(2)}) collective-permute-start(f32[2,768]{1,0:T(2,128)} %get-tuple-element.125), channel_id=1, source_target_pairs={{0,12},{4,8},{8,4},{12,0},{1,13},{5,9},{9,5},{13,1},{2,14},{6,10},... | collective-permute-start | bytes 18440 | tf_op jit(solution)/shard_map/ppermute | solution.py:62
  158.3 10.1 %collective-permute-start.34 = (bf16[208,768]{1,0:T(8,128)(2,1)S(1)}, bf16[208,768]{1,0:T(8,128)(2,1)S(1)}, u32[]{:S(2)}, u32[]{:S(2)}) collective-permute-start(bf16[208,768]{1,0:T(8,128)(2,1)S(1)} %add.95), channel_id=1, source_target_pairs={{0,16},{16,0},{1,17},{17,1},{2,18},{18,2},{3,19},{19,3},{4,20},{20... | collective-permute-start | bytes 958472 | tf_op jit(solution)/shard_map/ppermute | solution.py:62
  162.0 8.8 %collective-permute-start.29 = (bf16[624,384]{1,0:T(8,128)(2,1)S(1)}, bf16[624,384]{1,0:T(8,128)(2,1)S(1)}, u32[]{:S(2)}, u32[]{:S(2)}) collective-permute-start(bf16[624,384]{1,0:T(8,128)(2,1)S(1)} %add.88.one), channel_id=1, source_target_pairs={{0,1},{1,0},{2,3},{3,2},{4,5},{5,4},{6,7},{7,6},{8,9},{9,8},{10,11... | collective-permute-start | bytes 1437704 | tf_op jit(solution)/shard_map/ppermute | solution.py:62
  174.6 3.6 %collective-permute-start.33 = (f32[2,768]{1,0:T(2,128)S(1)}, f32[2,768]{1,0:T(2,128)S(1)}, u32[]{:S(2)}, u32[]{:S(2)}) collective-permute-start(f32[2,768]{1,0:T(2,128)S(1)} %add_add_fusion), channel_id=1, source_target_pairs={{0,16},{16,0},{1,17},{17,1},{2,18},{18,2},{3,19},{19,3},{4,20},{20... | collective-permute-start | bytes 18440 | tf_op jit(solution)/shard_map/ppermute | solution.py:62
  (37 other events, 367.5 us)

commit v3 on v2

--- a/solution.py
+++ b/solution.py
@@ -82,7 +82,7 @@
     while step < grid.dps:
         total = total + grid.swap(total, "dp", step)
         step *= 2
-    return total.astype(F32) + grid.swap(total, "dp", 1).astype(F32)
+    return total, grid.swap(total, "dp", 1)
 
 
 def sum_two(grid, mine, away, others=()):
@@ -146,18 +146,25 @@
     return pl.ds(pl.multiple_of((ids[0] ^ (BASES[which // 2] + side)) * size, size), size)
 
 
-def copies(ids, pieces, full, sems):
+def copies(ids, pieces, full, sems, column=0):
+    columns = pl.ds(column, full.shape[1])
     return [
-        pltpu.make_async_copy(piece, full.at[piece_rows(ids, i, piece.shape[0])], sems.at[i])
+        pltpu.make_async_copy(piece.at[:, columns], full.at[piece_rows(ids, i, piece.shape[0])], sems.at[i])
         for i, piece in enumerate(pieces)
     ]
 
 
-def place(ids, pieces, full, sems):
-    for copy in copies(ids, pieces, full, sems):
+def place(ids, pieces, full, sems, column=0):
+    for copy in copies(ids, pieces, full, sems, column):
         copy.start()
-    for copy in copies(ids, pieces, full, sems):
+    for copy in copies(ids, pieces, full, sems, column):
         copy.wait()
+
+
+def place_proj(full, proj):
+    one, two, three = (full[:, i * LANES : (i + 1) * LANES].astype(F32) for i in (1, 3, 5))
+    proj[:, :LANES] = jnp.where(low_lanes(one.shape), pltpu.roll(one, HD, 1), two).astype(BF)
+    proj[:, LANES:] = low(pltpu.roll(three, HD, 1)).astype(BF)
 
 
 def split_halves(ids, values, mine, away):
@@ -172,6 +179,23 @@
     first = ids[0] % 2 == 0
     a, b = mine[...].astype(F32), other[...].astype(F32)
     return jnp.concatenate([jnp.where(first, a, b), jnp.where(first, b, a)], axis=1)
+
+
+def close_kernel(ids, one, two, query, key, value, proj, query_bias, value_bias, proj_bias, gain, shift, hidden_bias, last_bias):
+    total = one[...].astype(F32) + two[...].astype(F32)
+    size, wide = query.shape
+    step = wide + HD
+    for i, ref in enumerate((query, key, value)):
+        ref[...] = total[:size, i * step : i * step + wide]
+    proj[...] = jnp.concatenate([total[:size, i * step + wide : (i + 1) * step] for i in range(3)], axis=1).T
+    sums = total[size:]
+    gain[...], shift[...], hidden_bias[...] = sums[0], sums[1], sums[4]
+    query_bias[...], value_bias[...] = sums[3, :wide], sums[3, 2 * step : 2 * step + wide]
+    for ref, row in ((proj_bias, sums[2:3]), (last_bias, sums[5:6])):
+        mine = row[:, :wide]
+        for i in range(1, row.shape[1] // wide):
+            mine = jnp.where(ids[0] == i, row[:, i * wide : (i + 1) * wide], mine)
+        ref[...] = mine[0]
 
 
 def enter_kernel(tokens, cot, gain, shift, tokens_out, first_out, cot_out, sums):
@@ -190,14 +214,11 @@
     sums[...] = total
 
 
-def attend_kernel(ids, first, h0, h1, h2, h3, bias, proj_bias, full, proj, joined, attended, probs, mine, away, sems):
+def attend_kernel(ids, first, h0, h1, h2, h3, bias, proj_bias, joined, attended, probs, mine, away, full, proj, sems):
     @pl.when(pl.program_id(0) == 0)
     def _():
         place(ids, (h0, h1, h2, h3), full, sems)
-        one, two, three = (full[:, i * LANES : (i + 1) * LANES].astype(F32) for i in (1, 3, 5))
-        is_low = low_lanes(one.shape)
-        proj[:, :LANES] = jnp.where(is_low, pltpu.roll(one, HD, 1), two).astype(BF)
-        proj[:, LANES:] = low(pltpu.roll(three, HD, 1)).astype(BF)
+        place_proj(full, proj)
 
     rows = (dot(first[...], full[...], (1, 0)) + bias[...]).astype(BF)
     query = rows[:, : 2 * LANES] * jnp.asarray(HD**-0.5, BF)
@@ -222,7 +243,7 @@
 
 def mlp_kernel(
     ids, tokens, one, two, cot, gain, shift, bias, w0, w1, w2, w3,
-    full, mid_out, second_out, hidden_out, pre_out, mine, away, sums, sems
+    second_out, hidden_out, pre_out, mine, away, sums, full, sems
 ):
     @pl.when(pl.program_id(0) == 0)
     def _():
@@ -231,7 +252,6 @@
         sums[...] = jnp.zeros_like(sums)
 
     mid = tokens[...].astype(F32) + join_halves(ids, one, two)
-    mid_out[...] = mid
     centred, _ = normalize(mid)
     second = (centred * gain[...] + shift[...]).astype(BF)
     second_out[...] = second
@@ -251,15 +271,18 @@
     split_halves(ids, dot(grad_pre, full[:, :width], (1, 1)).astype(BF), mine, away)
 
 
-def shrink_kernel(ids, hidden, full, bias, mine, away):
-    width = hidden.shape[1]
-    split_halves(ids, (dot(hidden[...], full[:, width:], (1, 1)) + bias[...]).astype(BF), mine, away)
+def shrink_kernel(ids, hidden, w0, w1, w2, w3, bias, mine, away, shrink, sems):
+    @pl.when(pl.program_id(0) == 0)
+    def _():
+        place(ids, (w0, w1, w2, w3), shrink, sems, hidden.shape[1])
+
+    split_halves(ids, (dot(hidden[...], shrink[...], (1, 1)) + bias[...]).astype(BF), mine, away)
 
 
 def deal(ids, full, stay_one, stay_two, away_one, away_two):
     size = stay_one.shape[0]
     for i, ref in enumerate((stay_one, away_one, stay_two, away_two)):
-        ref[...] = full[piece_rows(ids, i, size), :]
+        ref[...] = full[piece_rows(ids, i, size), :].astype(BF)
 
 
 def outer_kernel(ids, cot, hidden, second, grad_pre, s0, s1, a0, a1, full):
@@ -287,19 +310,27 @@
 
 
 def attend_back_kernel(
-    ids, one, two, mid, cot, gain, full, proj, joined, probs,
-    grad_mid_out, grad_mid_b_out, grad_joined_out, mine, away, sums
+    ids, one, two, tokens, mid_one, mid_two, cot, gain, h0, h1, h2, h3, joined, probs,
+    grad_mid_out, grad_joined_out, mine, away, sums, full, proj, sems
 ):
     @pl.when(pl.program_id(0) == 0)
     def _():
+        for copy in copies(ids, (h0, h1, h2, h3), full, sems):
+            copy.start()
         sums[...] = jnp.zeros_like(sums)
 
     grad_normed = join_halves(ids, one, two)
-    centred, inverse = normalize(mid[...])
+    centred, inverse = normalize(tokens[...].astype(F32) + join_halves(ids, mid_one, mid_two))
     grad_mid = cot[...].astype(F32) + norm_back(grad_normed, centred, inverse, gain[...])
-    grad_mid_out[...] = grad_mid
     grad_mid_b = grad_mid.astype(BF)
-    grad_mid_b_out[...] = grad_mid_b
+    grad_mid_out[...] = grad_mid_b
+
+    @pl.when(pl.program_id(0) == 0)
+    def _():
+        for copy in copies(ids, (h0, h1, h2, h3), full, sems):
+            copy.wait()
+        place_proj(full, proj)
+
     grad_att = dot(grad_mid_b, proj[...], (1, 0)).astype(BF)
     query, key, value = (joined[:, i * 2 * LANES : (i + 1) * 2 * LANES] for i in range(3))
     queries, keys, values = [], [], []
@@ -319,8 +350,8 @@
         [(queries[0] + queries[1]) * scale, queries[2] * scale, keys[0] + keys[1], keys[2], values[0] + values[1], values[2]],
         axis=1,
     )
-    for i, values in enumerate((grad_normed * centred, grad_normed, grad_mid, result)):
-        sums[i : i + 1, :] += columns_sum(values)
+    for i, terms in enumerate((grad_normed * centred, grad_normed, grad_mid, result)):
+        sums[i : i + 1, :] += columns_sum(terms)
     result = result.astype(BF)
     grad_joined_out[...] = result
     split_halves(ids, dot(result, full[...], (1, 1)).astype(BF), mine, away)
@@ -331,15 +362,16 @@
     out[...] = jnp.concatenate([values[i * PAD : i * PAD + SEQ] for i in range(images)], axis=0).astype(out.dtype)
 
 
-def output_kernel(ids, one, two, mid, out):
-    leave(mid[...] + join_halves(ids, one, two), out)
+def output_kernel(ids, one, two, tokens, mid_one, mid_two, out):
+    mid = tokens[...].astype(F32) + join_halves(ids, mid_one, mid_two)
+    leave(mid + join_halves(ids, one, two), out)
 
 
 def exit_kernel(ids, one, upper, lower, grad_mid, tokens, gain, out, sums):
     two = jnp.concatenate([upper[...].astype(F32), lower[...].astype(F32)], axis=0)
     grad_normed = join_halves(ids, one, two)
     centred, inverse = normalize(tokens[...].astype(F32))
-    leave(grad_mid[...] + norm_back(grad_normed, centred, inverse, gain[...]), out)
+    leave(grad_mid[...].astype(F32) + norm_back(grad_normed, centred, inverse, gain[...]), out)
     sums[...] = jnp.concatenate([columns_sum(grad_normed * centred), columns_sum(grad_normed)], axis=0)
 
 
@@ -370,7 +402,7 @@
         in_specs=in_specs,
         out_specs=[spec(s[0], how) for s, how in outs],
         scratch_shapes=list(scratch),
-        compiler_params=pltpu.CompilerParams(vmem_limit_bytes=60 * 1024 * 1024),
+        compiler_params=pltpu.CompilerParams(vmem_limit_bytes=52 * 1024 * 1024),
         cost_estimate=pl.CostEstimate(flops=1, bytes_accessed=1, transcendentals=0),
         **how,
     )(*arrays))
@@ -436,14 +468,13 @@
         [(((rows, model), BF), 0), (((rows, model), BF), 0), (((rows, model), BF), 0), (((1, model), F32), 0)],
         rows * model * 20,
     )
+    weights_scratch = [pltpu.VMEM((model, model), BF), pltpu.VMEM((model, 2 * LANES), BF)]
     halves = [(((rows, half), BF), 1), (((rows, half), BF), 1)]
-    full, proj, joined, attended, probs, mine, away = run(
+    joined, attended, probs, mine, away = run(
         attend_kernel,
         ids,
         [(first_in, 1)] + [(a, 2) for a in p_pieces] + [(line(joined_bias), 0), (spread(proj_bias), 0)],
         [
-            (((model, model), BF), 0),
-            (((model, 2 * LANES), BF), 0),
             (((rows, model), BF), 1),
             (((rows, 2 * LANES), BF), 1),
             (((heads * images, PAD, PAD), BF), 1),
@@ -451,19 +482,18 @@
         + halves,
         2 * rows * model * (model + 2 * wide),
         images,
-        [pltpu.SemaphoreType.DMA((4,))],
+        weights_scratch + [pltpu.SemaphoreType.DMA((4,))],
     )
     _, one = sum_two(grid, mine, away, (w_pieces[1], w_pieces[2]))
     two = grid.swap(after(one, w_pieces[3]), "col", 1)
-    wide_full, mid, second_in, hidden, grad_pre, mine, away, mlp_sums = run(
+    mid_one, mid_two = one, two
+    second_in, hidden, grad_pre, mine, away, mlp_sums = run(
         mlp_kernel,
         ids,
         [(tokens_pad, 1), (one, 1), (two, 1), (cot, 1)]
         + [(line(a), 0) for a in (mlp_gain, mlp_shift, e_bias)]
         + [(a, 2) for a in w_pieces],
         [
-            (((model, 2 * hidden_here), BF), 0),
-            (((rows, model), F32), 1),
             (((rows, model), BF), 1),
             (((rows, hidden_here), BF), 1),
             (((rows, hidden_here), BF), 1),
@@ -472,7 +502,7 @@
         + [(((1, hidden_here), F32), 0)],
         2 * rows * model * hidden_here * 3,
         images,
-        [pltpu.SemaphoreType.DMA((4,))],
+        [pltpu.VMEM((model, 2 * hidden_here), BF), pltpu.SemaphoreType.DMA((4,))],
     )
 
     def pieces(width, more=0):
@@ -489,24 +519,37 @@
         scratch=[pltpu.VMEM((model, 2 * hidden_here), BF)],
     )
     got = [grid.swap(a, "dp", 1) for a in parts[2:]]
-    one = after(one, parts[0])
+    mine_out, away_out = run(
+        shrink_kernel,
+        ids,
+        [(after(hidden, parts[0]), 1)] + [(a, 2) for a in w_pieces] + [(spread(shrink_bias), 0)],
+        halves,
+        2 * rows * model * hidden_here,
+        images,
+        [pltpu.VMEM((model, hidden_here), BF), pltpu.SemaphoreType.DMA((4,))],
+    )
+    _, out_one = sum_two(grid, mine_out, away_out)
+    one = after(one, away_out)
     two = grid.swap(one, "col", 1)
 
-    grad_mid, grad_mid_b, grad_joined, mine, away, back_sums = run(
+    taller = model // grid.cols + SUMS
+    grad_mid, grad_joined, mine, away, back_sums = run(
         attend_back_kernel,
         ids,
-        [(one, 1), (two, 1), (mid, 1), (cot, 1), (line(mlp_gain), 0), (full, 0), (proj, 0), (joined, 1), (probs, 1)],
-        [(((rows, model), F32), 1), (((rows, model), BF), 1), (((rows, model), BF), 1)]
-        + halves
-        + [(((4, model), F32), 0)],
+        [(a, 1) for a in (one, two, tokens_pad, mid_one, mid_two, cot)]
+        + [(line(mlp_gain), 0)]
+        + [(a, 2) for a in p_pieces]
+        + [(joined, 1), (probs, 1)],
+        [(((rows, model), BF), 1)] * 2 + halves + [(((4, model), F32), 0)],
         2 * rows * model * (model + 2 * wide),
         images,
+        weights_scratch + [pltpu.SemaphoreType.DMA((4,))],
     )
     sooner = after(parts[0], grad_joined) + got[0]
     packed_parts = run(
         joined_outer_kernel,
         ids,
-        [(first_in, 0), (grad_joined, 0), (grad_mid_b, 0), (attended, 0)]
+        [(first_in, 0), (grad_joined, 0), (grad_mid, 0), (attended, 0)]
         + [(back_sums, 0), (mlp_sums, 0), (cot_sum, 0)],
         pieces(model, SUMS)[:2] + [(((2 * (model // grid.cols + SUMS), model), BF), 0)],
         2 * rows * model * model,
@@ -514,20 +557,19 @@
     )
     packed_got = grid.swap(packed_parts[2], "dp", 1)
     packed_got = packed_got[: model // grid.cols + SUMS], packed_got[model // grid.cols + SUMS :]
-    mine_out, away_out = run(
-        shrink_kernel,
-        ids,
-        [(after(hidden, packed_parts[0]), 1), (wide_full, 0), (spread(shrink_bias), 0)],
-        halves,
-        2 * rows * model * hidden_here,
-        images,
-    )
     later = after(parts[1], packed_parts[0]) + got[1]
-    away = after(away, packed_parts[0], later, away_out)
+    away = after(away, packed_parts[0], later, out_one)
     sooner, later = grid.give(sooner, BASES[0]), grid.give(later, BASES[1])
     mine, one = sum_two(grid, mine, away)
-    _, out_one = sum_two(grid, mine_out, after(away_out, mine))
-    packed_one = after(packed_parts[0], mine, sooner) + packed_got[0]
+    (output,) = run(
+        output_kernel,
+        ids,
+        [(after(out_one, mine), 0), (grid.swap(out_one, "col", 1), 0)]
+        + [(a, 0) for a in (tokens_pad, mid_one, mid_two)],
+        [((tokens.shape, BF), 0)],
+        rows * model,
+    )
+    packed_one = after(packed_parts[0], output, sooner) + packed_got[0]
     packed_two = after(packed_parts[1], packed_one) + packed_got[1]
     packed_given = [grid.give(packed_one, BASES[0]), grid.give(packed_two, BASES[1])]
     total = after(sooner, packed_two, one) + later
@@ -541,44 +583,50 @@
         [((tokens.shape, BF), 0), (((2, model), F32), 0)],
         rows * model * 20,
     )
-    grad_both = finish(grid, total)
-    packed_total = after(packed_given[0], grad_both, grad_tokens) + packed_given[1]
-    (output,) = run(
-        output_kernel,
-        ids,
-        [(after(out_one, packed_total), 0), (grid.swap(out_one, "col", 1), 0), (mid, 0)],
-        [((tokens.shape, BF), 0)],
-        rows * model,
-    )
-    grad_packed = finish(grid, packed_total)
-    late = sum((grid.swap(late, "row", flip) for flip in range(1, grid.rows)), late)
-    late = sum_axis(grid, after(late, grad_both, output), "dp", 1)
-    whole, grad_packed = grad_packed[model // grid.cols :], grad_packed[: model // grid.cols]
-    step = wide + HD
-
-    def own_columns(vector):
-        width = vector.shape[0] // grid.cols
-        return lax.dynamic_slice_in_dim(vector, grid.col * width, width, 0)
-
-    grad_proj = jnp.concatenate([grad_packed[:, i * step + wide : (i + 1) * step] for i in range(3)], axis=1).T
+    own, other = finish(grid, total)
+    grad_both = own.astype(F32) + other.astype(F32)
+    packed_total = after(packed_given[0], grad_tokens) + packed_given[1]
+    own, other = finish(grid, packed_total)
+    late = sum_axis(grid, after(late, packed_total), "row", 1)
+    late = sum_axis(grid, after(late, grad_both), "dp", 1)
+    square, line_of = (query_weight.shape, F32), lambda size: (((size,), F32), 0)
+    (
+        grad_query,
+        grad_key,
+        grad_value,
+        grad_proj,
+        grad_query_bias,
+        grad_value_bias,
+        grad_proj_bias,
+        grad_mlp_gain,
+        grad_mlp_shift,
+        grad_expand_bias,
+        grad_shrink_bias,
+    ) = run(
+        close_kernel,
+        ids,
+        [(own, 0), (other, 0)],
+        [(square, 0)] * 4 + [line_of(wide)] * 3 + [line_of(model)] * 3 + [line_of(wide)],
+        1,
+    )
     return (
         output,
         grad_tokens,
         late[0],
         late[1],
-        grad_packed[:, :wide],
-        grad_packed[:, step : step + wide],
-        grad_packed[:, 2 * step : 2 * step + wide],
-        whole[3, :wide],
-        whole[3, 2 * step : 2 * step + wide],
+        grad_query,
+        grad_key,
+        grad_value,
+        grad_query_bias,
+        grad_value_bias,
         grad_proj,
-        own_columns(whole[2]),
-        whole[0],
-        whole[1],
+        grad_proj_bias,
+        grad_mlp_gain,
+        grad_mlp_shift,
         grad_both[:, :hidden_here],
-        whole[4],
+        grad_expand_bias,
         grad_both[:, hidden_here:],
-        own_columns(whole[5]),
+        grad_shrink_bias,
     )
 
 

time: 179 us -> 173 us (0.966)
  the two profiles are of different devices: /device:TPU:0 before, /device:TPU:24 now
where the time goes in v3:
time: 173 us; the launch traced here: 172 us
  starting transfers between devices  59.2 us (34%)
  waiting for transfers between devices  56.5 us (33%)
  Pallas kernels  46.1 us (27%)
  local copies, waits for them, and re-layouts  6.57 us (4%)
  other arithmetic  2.72 us (2%)
    ppermute x25, waiting for transfers between devices, swap(): return lax.ppermute(array, axis, [(i, i ^ flip) for i in range(size)])  50.3 us
    pallas_call x10, Pallas kernels, run(): pl.pallas_call(kernel, out_shape=shapes, in_specs=in_specs, out_specs=[sp...  46.1 us
    ppermute x25, starting transfers between devices, swap(): return lax.ppermute(array, axis, [(i, i ^ flip) for i in range(size)])  39.1 us
    ppermute x4, starting transfers between devices, fetch(): lax.ppermute(array, ('dp', 'row', 'col'), [(holder, me) for me, holder in...  14.2 us
    ppermute x4, waiting for transfers between devices, fetch(): lax.ppermute(array, ('dp', 'row', 'col'), [(holder, me) for me, holder in...  6.25 us
    ppermute x4, starting transfers between devices, give(): lax.ppermute(array, ('dp', 'row', 'col'), [(me, holder) for me, holder in...  5.25 us
  transfers between devices with their start and end apart: 34, of which 16 were waited for; matrix products, arithmetic and copies ran while one was open for 2% of the time, Pallas kernels for 23%

profile of v3, /device:TPU:24, one launch (start us, length us, event | category | flops | bytes accessed | tf_op | source)
XLA Modules:
  0.0 172.4 jit_solution(11150512204296121574)
XLA Ops:
  3.8 4.2 %collective-permute-start = (bf16[192,768]{1,0:T(8,128)(2,1)S(1)}, bf16[192,768]{1,0:T(8,128)(2,1)S(1)}, u32[]{:S(2)}, u32[]{:S(2)}) collective-permute-start(bf16[192,768]{1,0:T(8,128)(2,1)S(1)} %concatenate.12), channel_id=1, source_target_pairs={{2,0},{11,1},{4,2},{13,3},{6,4},{15,5},{0,6},{9,7},{10,8},{3,9},{1... | collective-permute-start | bytes 884744 | tf_op jit(solution)/shard_map/ppermute | solution.py:48
  8.9 6.2 %collective-permute-done.h0 = bf16[192,768]{1,0:T(8,128)(2,1)S(1)} collective-permute-done((bf16[192,768]{1,0:T(8,128)(2,1)S(1)}, bf16[192,768]{1,0:T(8,128)(2,1)S(1)}, u32[]{:S(2)}, u32[]{:S(2)}) %collective-permute-start) | collective-permute-done | bytes 294944 | tf_op jit(solution)/shard_map/ppermute | solution.py:48
  15.1 3.4 %collective-permute-start.2 = (bf16[192,1536]{1,0:T(8,128)(2,1)}, bf16[192,1536]{1,0:T(8,128)(2,1)S(1)}, u32[]{:S(2)}, u32[]{:S(2)}) collective-permute-start(bf16[192,1536]{1,0:T(8,128)(2,1)} %pad_maximum_fusion), channel_id=1, source_target_pairs={{2,0},{11,1},{4,2},{13,3},{6,4},{15,5},{0,6},{9,7},{10,8},{3,9},{1... | collective-permute-start | bytes 1769480 | tf_op jit(solution)/shard_map/ppermute | solution.py:48
  19.4 3.3 %collective-permute-start.4 = (bf16[192,768]{1,0:T(8,128)(2,1)S(1)}, bf16[192,768]{1,0:T(8,128)(2,1)S(1)}, u32[]{:S(2)}, u32[]{:S(2)}) collective-permute-start(bf16[192,768]{1,0:T(8,128)(2,1)S(1)} %collective-permute-done.1.h2), channel_id=1, source_target_pairs={{0,16},{16,0},{1,17},{17,1},{2,18},{18,2},{3,19},{19,3},{4,20},{20... | collective-permute-start | bytes 884744 | tf_op jit(solution)/shard_map/ppermute | solution.py:62
  24.1 2.3 %shard_map.296 = (bf16[624,768]{1,0:T(8,128)(2,1)}, bf16[624,768]{1,0:T(8,128)(2,1)}, bf16[624,768]{1,0:T(8,128)(2,1)}, f32[1,768]{1,0:T(1,128)S(1)}) custom-call(bf16[591,768]{1,0:T(8,128)(2,1)S(1)} %copy-done.7, bf16[591,768]{1,0:T(8,128)(2,1)S(1)} %copy-done.8, f32[1,768]{1,0:T(1,128)S(1)} %reshape.116.gain, f32[1,768]{1,0:T(1,128)S(1)} %reshape.117.shift), custom_call_target="tpu_custom_call" | custom-call | flops 1 | bytes 1 | tf_op jit(solution)/shard_map/pallas_call | solution.py:399
  26.4 5.9 %collective-permute-start.8 = (bf16[192,1536]{1,0:T(8,128)(2,1)}, bf16[192,1536]{1,0:T(8,128)(2,1)}, u32[]{:S(2)}, u32[]{:S(2)}) collective-permute-start(bf16[192,1536]{1,0:T(8,128)(2,1)} %pad_maximum_fusion), channel_id=1, source_target_pairs={{0,0},{9,1},{6,2},{15,3},{4,4},{13,5},{2,6},{11,7},{8,8},{1,9},{14... | collective-permute-start | bytes 1769480 | tf_op jit(solution)/shard_map/ppermute | solution.py:48
  32.3 3.2 %collective-permute-start.7 = (bf16[192,1536]{1,0:T(8,128)(2,1)S(1)}, bf16[192,1536]{1,0:T(8,128)(2,1)S(1)}, u32[]{:S(2)}, u32[]{:S(2)}) collective-permute-start(bf16[192,1536]{1,0:T(8,128)(2,1)S(1)} %collective-permute-done.2.w0), channel_id=1, source_target_pairs={{0,16},{16,0},{1,17},{17,1},{2,18},{18,2},{3,19},{19,3},{4,20},{20... | collective-permute-start | bytes 1769480 | tf_op jit(solution)/shard_map/ppermute | solution.py:62
  35.7 6.1 %shard_map.297 = (bf16[624,768]{1,0:T(8,128)(2,1)}, bf16[624,256]{1,0:T(8,128)(2,1)S(1)}, bf16[9,208,208]{2,1,0:T(8,128)(2,1)}, bf16[624,384]{1,0:T(8,128)(2,1)S(1)}, bf16[624,384]{1,0:T(8,128)(2,1)}) custom-call(s32[2]{0:T(128)S(1)} %pad_add_fusion.ids, bf16[624,768]{1,0:T(8,128)(2,1)} %get-tuple-element.79.first, ...), custom_call_target="tpu_custom_call" | custom-call | flops 1 | bytes 1 | tf_op jit(solution)/shard_map/pallas_call | solution.py:399
  41.8 7.3 %collective-permute-start.6 = (bf16[624,384]{1,0:T(8,128)(2,1)}, bf16[624,384]{1,0:T(8,128)(2,1)S(1)}, u32[]{:S(2)}, u32[]{:S(2)}) collective-permute-start(bf16[624,384]{1,0:T(8,128)(2,1)} %get-tuple-element.83), channel_id=1, source_target_pairs={{0,1},{1,0},{2,3},{3,2},{4,5},{5,4},{6,7},{7,6},{8,9},{9,8},{10,11... | collective-permute-start | bytes 1437704 | tf_op jit(solution)/shard_map/ppermute | solution.py:62
  49.1 1.7 collective-permute-done.6
  50.9 2.2 %collective-permute-start.9 = (bf16[624,384]{1,0:T(8,128)(2,1)S(1)}, bf16[624,384]{1,0:T(8,128)(2,1)S(1)}, u32[]{:S(2)}, u32[]{:S(2)}) collective-permute-start(bf16[624,384]{1,0:T(8,128)(2,1)S(1)} %add.71), channel_id=1, source_target_pairs={{0,2},{1,3},{2,0},{3,1},{4,6},{5,7},{6,4},{7,5},{8,10},{9,11},{10,... | collective-permute-start | bytes 1437704 | tf_op jit(solution)/shard_map/ppermute | solution.py:62
  53.1 11.5 %collective-permute-done.9 = bf16[624,384]{1,0:T(8,128)(2,1)S(1)} collective-permute-done((bf16[624,384]{1,0:T(8,128)(2,1)S(1)}, bf16[624,384]{1,0:T(8,128)(2,1)S(1)}, u32[]{:S(2)}, u32[]{:S(2)}) %collective-permute-start.9) | collective-permute-done | bytes 479264 | tf_op jit(solution)/shard_map/ppermute | solution.py:62
  65.6 1.7 collective-permute-done.11.two.mid_two
  67.3 7.3 %shard_map.298 = (bf16[624,768]{1,0:T(8,128)(2,1)}, bf16[624,768]{1,0:T(8,128)(2,1)}, bf16[624,768]{1,0:T(8,128)(2,1)}, bf16[624,384]{1,0:T(8,128)(2,1)S(1)}, bf...) custom-call(s32[2]{0:T(128)S(1)} %pad_add_fusion.ids, bf16[624,768]{1,0:T(8,128)(2,1)} %get-tuple-element.78.tokens, ...), custom_call_target="tpu_custom_call" | custom-call | flops 1 | bytes 1 | tf_op jit(solution)/shard_map/pallas_call | solution.py:399
  76.9 5.1 %shard_map.299 = (bf16[192,1536]{1,0:T(8,128)(2,1)S(1)}, bf16[192,1536]{1,0:T(8,128)(2,1)S(1)}, bf16[192,1536]{1,0:T(8,128)(2,1)S(1)}, bf16[192,1536]{1,0:T(8,128)(2,1)}) custom-call(s32[2]{0:T(128)S(1)} %pad_add_fusion.ids, bf16[624,768]{1,0:T(8,128)(2,1)} %get-tuple-element.86.cot, bf16[624,768]{1,0:T(8,128)(2,1)} %get-tuple-element.94.hidden, ...), custom_call_target="tpu_custom_call" | custom-call | flops 1 | bytes 1 | tf_op jit(solution)/shard_map/pallas_call | solution.py:399
  82.1 4.3 %shard_map.300 = (bf16[624,384]{1,0:T(8,128)(2,1)S(1)}, bf16[624,384]{1,0:T(8,128)(2,1)S(1)}) custom-call(s32[2]{0:T(128)S(1)} %pad_add_fusion.ids, bf16[624,768]{1,0:T(8,128)(2,1)} %get-tuple-element.94.hidden, bf16[192,1536]{1,0:T(8,128)(2,1)S(1)} %copy-done.6, bf16[192,1536]{1,0:T(8,128)(2,1)} %copy-done.9, bf16[192,1536]{1,0:T(8,128)(2,1)} %collective-permute-done.8.w2, ...), custom_call_target="tpu_custom_call" | custom-call | flops 1 | bytes 1 | tf_op jit(solution)/shard_map/pallas_call | solution.py:399
  88.0 1.8 %collective-permute-done.15 = bf16[624,384]{1,0:T(8,128)(2,1)S(1)} collective-permute-done((bf16[624,384]{1,0:T(8,128)(2,1)S(1)}, bf16[624,384]{1,0:T(8,128)(2,1)S(1)}, u32[]{:S(2)}, u32[]{:S(2)}) %collective-permute-start.15) | collective-permute-done | bytes 479264 | tf_op jit(solution)/shard_map/ppermute | solution.py:62
  92.6 9.6 %shard_map.301 = (bf16[624,768]{1,0:T(8,128)(2,1)}, bf16[624,768]{1,0:T(8,128)(2,1)}, bf16[624,384]{1,0:T(8,128)(2,1)S(1)}, bf16[624,384]{1,0:T(8,128)(2,1)}, f32[4,768]{1,0:T(4,128)S(1)}) custom-call(s32[2]{0:T(128)S(1)} %pad_add_fusion.ids, bf16[624,384]{1,0:T(8,128)(2,1)} %copy-done.11, bf16[624,384]{1,0:T(8,128)(2,1)} %copy-done.12, ...), custom_call_target="tpu_custom_call" | custom-call | flops 1 | bytes 1 | tf_op jit(solution)/shard_map/pallas_call | solution.py:399
  102.2 3.3 %shard_map.302 = (bf16[208,768]{1,0:T(8,128)(2,1)S(1)}, bf16[208,768]{1,0:T(8,128)(2,1)S(1)}, bf16[416,768]{1,0:T(8,128)(2,1)S(1)}) custom-call(s32[2]{0:T(128)S(1)} %pad_add_fusion.ids, bf16[624,768]{1,0:T(8,128)(2,1)} %get-tuple-element.79.first, bf16[624,768]{1,0:T(8,128)(2,1)} %get-tuple-element.102.joined, ...), custom_call_target="tpu_custom_call" | custom-call | flops 1 | bytes 1 | tf_op jit(solution)/shard_map/pallas_call | solution.py:399
  106.5 1.8 %collective-permute-start.22 = (bf16[192,1536]{1,0:T(8,128)(2,1)S(1)}, bf16[192,1536]{1,0:T(8,128)(2,1)S(1)}, u32[]{:S(2)}, u32[]{:S(2)}) collective-permute-start(bf16[192,1536]{1,0:T(8,128)(2,1)S(1)} %add.80), channel_id=1, source_target_pairs={{0,2},{1,11},{2,4},{3,13},{4,6},{5,15},{6,0},{7,9},{8,10},{9,3},{1... | collective-permute-start | bytes 1769480 | tf_op jit(solution)/shard_map/ppermute | solution.py:51
  108.5 6.8 %collective-permute-done.17 = bf16[192,1536]{1,0:T(8,128)(2,1)S(1)} collective-permute-done((bf16[192,1536]{1,0:T(8,128)(2,1)S(1)}, bf16[192,1536]{1,0:T(8,128)(2,1)S(1)}, u32[]{:S(2)}, u32[]{:S(2)}) %collective-permute-start.17) | collective-permute-done | bytes 589856 | tf_op jit(solution)/shard_map/ppermute | solution.py:62
  117.5 4.1 %collective-permute-start.20 = (bf16[624,384]{1,0:T(8,128)(2,1)S(1)}, bf16[624,384]{1,0:T(8,128)(2,1)S(1)}, u32[]{:S(2)}, u32[]{:S(2)}) collective-permute-start(bf16[624,384]{1,0:T(8,128)(2,1)S(1)} %add.78), channel_id=1, source_target_pairs={{0,2},{1,3},{2,0},{3,1},{4,6},{5,7},{6,4},{7,5},{8,10},{9,11},{10,... | collective-permute-start | bytes 1437704 | tf_op jit(solution)/shard_map/ppermute | solution.py:62
  121.6 2.7 %shard_map.303 = bf16[591,768]{1,0:T(8,128)(2,1)} custom-call(s32[2]{0:T(128)S(1)} %pad_add_fusion.ids, bf16[624,384]{1,0:T(8,128)(2,1)S(1)} %add.75.one, bf16[624,384]{1,0:T(8,128)(2,1)S(1)} %collective-permute-done.19.two, bf16[624,768]{1,0:T(8,128)(2,1)} %get-tuple-element.78.tokens, bf16[624,384]{1,0:T(8,128)(2,1)S(1)} %copy-done.1, ...), custom_call_target="tpu_custom_call" | custom-call | flops 1 | bytes 1 | tf_op jit(solution)/shard_map/pallas_call | solution.py:399
  124.3 4.2 %collective-permute-done.23 = bf16[416,768]{1,0:T(8,128)(2,1)S(1)} collective-permute-done((bf16[416,768]{1,0:T(8,128)(2,1)S(1)}, bf16[416,768]{1,0:T(8,128)(2,1)S(1)}, u32[]{:S(2)}, u32[]{:S(2)}) %collective-permute-start.23) | collective-permute-done | bytes 639008 | tf_op jit(solution)/shard_map/ppermute | solution.py:62
  128.6 1.9 %collective-permute-start.27 = (bf16[208,768]{1,0:T(8,128)(2,1)S(1)}, bf16[208,768]{1,0:T(8,128)(2,1)S(1)}, u32[]{:S(2)}, u32[]{:S(2)}) collective-permute-start(bf16[208,768]{1,0:T(8,128)(2,1)S(1)} %slice_add_fusion.1), channel_id=1, source_target_pairs={{0,2},{1,11},{2,4},{3,13},{4,6},{5,15},{6,0},{7,9},{8,10},{9,3},{1... | collective-permute-start | bytes 958472 | tf_op jit(solution)/shard_map/ppermute | solution.py:51
  131.5 2.4 %collective-permute-done.20 = bf16[624,384]{1,0:T(8,128)(2,1)S(1)} collective-permute-done((bf16[624,384]{1,0:T(8,128)(2,1)S(1)}, bf16[624,384]{1,0:T(8,128)(2,1)S(1)}, u32[]{:S(2)}, u32[]{:S(2)}) %collective-permute-start.20) | collective-permute-done | bytes 479264 | tf_op jit(solution)/shard_map/ppermute | solution.py:62
  134.2 11.7 %collective-permute-start.31 = (bf16[192,1536]{1,0:T(8,128)(2,1)S(1)}, bf16[192,1536]{1,0:T(8,128)(2,1)S(1)}, u32[]{:S(2)}, u32[]{:S(2)}) collective-permute-start(bf16[192,1536]{1,0:T(8,128)(2,1)S(1)} %add.83), channel_id=1, source_target_pairs={{0,16},{16,0},{1,17},{17,1},{2,18},{18,2},{3,19},{19,3},{4,20},{20... | collective-permute-start | bytes 1769480 | tf_op jit(solution)/shard_map/ppermute | solution.py:62
  147.8 3.8 %shard_map.304 = (bf16[591,768]{1,0:T(8,128)(2,1)}, f32[2,768]{1,0:T(2,128)S(1)}) custom-call(s32[2]{0:T(128)S(1)} %pad_add_fusion.ids, bf16[624,384]{1,0:T(8,128)(2,1)S(1)} %add.79.one, bf16[320,384]{1,0:T(8,128)(2,1)S(1)} %collective-permute-done.25.upper, bf16[304,384]{1,0:T(8,128)(2,1)S(1)} %collective-permute-done.26.lower, ...), custom_call_target="tpu_custom_call" | custom-call | flops 1 | bytes 1 | tf_op jit(solution)/shard_map/pallas_call | solution.py:399
  152.7 3.6 %collective-permute-done.29 = f32[2,768]{1,0:T(2,128)S(1)} collective-permute-done((f32[2,768]{1,0:T(2,128)S(1)}, f32[2,768]{1,0:T(2,128)S(1)}, u32[]{:S(2)}, u32[]{:S(2)}) %collective-permute-start.29) | collective-permute-done | bytes 6176 | tf_op jit(solution)/shard_map/ppermute | solution.py:62
  156.3 4.5 %collective-permute-done.30 = f32[2,768]{1,0:T(2,128)S(1)} collective-permute-done((f32[2,768]{1,0:T(2,128)S(1)}, f32[2,768]{1,0:T(2,128)S(1)}, u32[]{:S(2)}, u32[]{:S(2)}) %collective-permute-start.30) | collective-permute-done | bytes 6176 | tf_op jit(solution)/shard_map/ppermute | solution.py:62
  160.8 5.4 %collective-permute-done.33.two = bf16[208,768]{1,0:T(8,128)(2,1)S(1)} collective-permute-done((bf16[208,768]{1,0:T(8,128)(2,1)S(1)}, bf16[208,768]{1,0:T(8,128)(2,1)S(1)}, u32[]{:S(2)}, u32[]{:S(2)}) %collective-permute-start.33) | collective-permute-done | bytes 319520 | tf_op jit(solution)/shard_map/ppermute | solution.py:62
  169.5 2.3 %collective-permute-done.32 = f32[2,768]{1,0:T(2,128)S(1)} collective-permute-done((f32[2,768]{1,0:T(2,128)S(1)}, f32[2,768]{1,0:T(2,128)S(1)}, u32[]{:S(2)}, u32[]{:S(2)}) %collective-permute-start.32) | collective-permute-done | bytes 6176 | tf_op jit(solution)/shard_map/ppermute | solution.py:62
  (143 shorter events, 25.3 us)
Async XLA Ops:
  3.1 5.8 %collective-permute-start.1 = (bf16[192,768]{1,0:T(8,128)(2,1)S(1)}, bf16[192,768]{1,0:T(8,128)(2,1)S(1)}, u32[]{:S(2)}, u32[]{:S(2)}) collective-permute-start(bf16[192,768]{1,0:T(8,128)(2,1)S(1)} %concatenate.12), channel_id=1, source_target_pairs={{0,0},{9,1},{6,2},{15,3},{4,4},{13,5},{2,6},{11,7},{8,8},{1,9},{14... | collective-permute-start | bytes 884744 | tf_op jit(solution)/shard_map/ppermute | solution.py:48
  3.8 11.3 %collective-permute-start = (bf16[192,768]{1,0:T(8,128)(2,1)S(1)}, bf16[192,768]{1,0:T(8,128)(2,1)S(1)}, u32[]{:S(2)}, u32[]{:S(2)}) collective-permute-start(bf16[192,768]{1,0:T(8,128)(2,1)S(1)} %concatenate.12), channel_id=1, source_target_pairs={{2,0},{11,1},{4,2},{13,3},{6,4},{15,5},{0,6},{9,7},{10,8},{3,9},{1... | collective-permute-start | bytes 884744 | tf_op jit(solution)/shard_map/ppermute | solution.py:48
  15.1 17.2 %collective-permute-start.2 = (bf16[192,1536]{1,0:T(8,128)(2,1)}, bf16[192,1536]{1,0:T(8,128)(2,1)S(1)}, u32[]{:S(2)}, u32[]{:S(2)}) collective-permute-start(bf16[192,1536]{1,0:T(8,128)(2,1)} %pad_maximum_fusion), channel_id=1, source_target_pairs={{2,0},{11,1},{4,2},{13,3},{6,4},{15,5},{0,6},{9,7},{10,8},{3,9},{1... | collective-permute-start | bytes 1769480 | tf_op jit(solution)/shard_map/ppermute | solution.py:48
  18.6 16.9 %collective-permute-start.5 = (f32[1152]{0:T(1024)S(1)}, f32[1152]{0:T(1024)S(1)}, u32[]{:S(2)}, u32[]{:S(2)}) collective-permute-start(f32[1152]{0:T(1024)S(1)} %concatenate.14), channel_id=1, source_target_pairs={{0,0},{9,1},{6,2},{15,3},{4,4},{13,5},{2,6},{11,7},{8,8},{1,9},{14... | collective-permute-start | bytes 13832 | tf_op jit(solution)/shard_map/ppermute | solution.py:58
  19.4 16.3 %collective-permute-start.4 = (bf16[192,768]{1,0:T(8,128)(2,1)S(1)}, bf16[192,768]{1,0:T(8,128)(2,1)S(1)}, u32[]{:S(2)}, u32[]{:S(2)}) collective-permute-start(bf16[192,768]{1,0:T(8,128)(2,1)S(1)} %collective-permute-done.1.h2), channel_id=1, source_target_pairs={{0,16},{16,0},{1,17},{17,1},{2,18},{18,2},{3,19},{19,3},{4,20},{20... | collective-permute-start | bytes 884744 | tf_op jit(solution)/shard_map/ppermute | solution.py:62
  22.7 13.0 %collective-permute-start.3 = (bf16[192,768]{1,0:T(8,128)(2,1)S(1)}, bf16[192,768]{1,0:T(8,128)(2,1)S(1)}, u32[]{:S(2)}, u32[]{:S(2)}) collective-permute-start(bf16[192,768]{1,0:T(8,128)(2,1)S(1)} %collective-permute-done.h0), channel_id=1, source_target_pairs={{0,16},{16,0},{1,17},{17,1},{2,18},{18,2},{3,19},{19,3},{4,20},{20... | collective-permute-start | bytes 884744 | tf_op jit(solution)/shard_map/ppermute | solution.py:62
  26.4 22.7 %collective-permute-start.8 = (bf16[192,1536]{1,0:T(8,128)(2,1)}, bf16[192,1536]{1,0:T(8,128)(2,1)}, u32[]{:S(2)}, u32[]{:S(2)}) collective-permute-start(bf16[192,1536]{1,0:T(8,128)(2,1)} %pad_maximum_fusion), channel_id=1, source_target_pairs={{0,0},{9,1},{6,2},{15,3},{4,4},{13,5},{2,6},{11,7},{8,8},{1,9},{14... | collective-permute-start | bytes 1769480 | tf_op jit(solution)/shard_map/ppermute | solution.py:48
  32.3 18.6 %collective-permute-start.7 = (bf16[192,1536]{1,0:T(8,128)(2,1)S(1)}, bf16[192,1536]{1,0:T(8,128)(2,1)S(1)}, u32[]{:S(2)}, u32[]{:S(2)}) collective-permute-start(bf16[192,1536]{1,0:T(8,128)(2,1)S(1)} %collective-permute-done.2.w0), channel_id=1, source_target_pairs={{0,16},{16,0},{1,17},{17,1},{2,18},{18,2},{3,19},{19,3},{4,20},{20... | collective-permute-start | bytes 1769480 | tf_op jit(solution)/shard_map/ppermute | solution.py:62
  41.8 9.0 %collective-permute-start.6 = (bf16[624,384]{1,0:T(8,128)(2,1)}, bf16[624,384]{1,0:T(8,128)(2,1)S(1)}, u32[]{:S(2)}, u32[]{:S(2)}) collective-permute-start(bf16[624,384]{1,0:T(8,128)(2,1)} %get-tuple-element.83), channel_id=1, source_target_pairs={{0,1},{1,0},{2,3},{3,2},{4,5},{5,4},{6,7},{7,6},{8,9},{9,8},{10,11... | collective-permute-start | bytes 1437704 | tf_op jit(solution)/shard_map/ppermute | solution.py:62
  49.1 16.4 %collective-permute-start.10 = (bf16[192,1536]{1,0:T(8,128)(2,1)}, bf16[192,1536]{1,0:T(8,128)(2,1)S(1)}, u32[]{:S(2)}, u32[]{:S(2)}) collective-permute-start(bf16[192,1536]{1,0:T(8,128)(2,1)} %collective-permute-done.8.w2), channel_id=1, source_target_pairs={{0,16},{16,0},{1,17},{17,1},{2,18},{18,2},{3,19},{19,3},{4,20},{20... | collective-permute-start | bytes 1769480 | tf_op jit(solution)/shard_map/ppermute | solution.py:62
  50.9 13.7 %collective-permute-start.9 = (bf16[624,384]{1,0:T(8,128)(2,1)S(1)}, bf16[624,384]{1,0:T(8,128)(2,1)S(1)}, u32[]{:S(2)}, u32[]{:S(2)}) collective-permute-start(bf16[624,384]{1,0:T(8,128)(2,1)S(1)} %add.71), channel_id=1, source_target_pairs={{0,2},{1,3},{2,0},{3,1},{4,6},{5,7},{6,4},{7,5},{8,10},{9,11},{10,... | collective-permute-start | bytes 1437704 | tf_op jit(solution)/shard_map/ppermute | solution.py:62
  74.7 1.9 %collective-permute-start.12 = (bf16[624,384]{1,0:T(8,128)(2,1)S(1)}, bf16[624,384]{1,0:T(8,128)(2,1)S(1)}, u32[]{:S(2)}, u32[]{:S(2)}) collective-permute-start(bf16[624,384]{1,0:T(8,128)(2,1)S(1)} %get-tuple-element.89), channel_id=1, source_target_pairs={{0,1},{1,0},{2,3},{3,2},{4,5},{5,4},{6,7},{7,6},{8,9},{9,8},{10,11... | collective-permute-start | bytes 1437704 | tf_op jit(solution)/shard_map/ppermute | solution.py:62
  76.7 13.1 %collective-permute-start.15 = (bf16[624,384]{1,0:T(8,128)(2,1)S(1)}, bf16[624,384]{1,0:T(8,128)(2,1)S(1)}, u32[]{:S(2)}, u32[]{:S(2)}) collective-permute-start(bf16[624,384]{1,0:T(8,128)(2,1)S(1)} %add.73), channel_id=1, source_target_pairs={{0,2},{1,3},{2,0},{3,1},{4,6},{5,7},{6,4},{7,5},{8,10},{9,11},{10,... | collective-permute-start | bytes 1437704 | tf_op jit(solution)/shard_map/ppermute | solution.py:62
  86.4 3.7 %collective-permute-start.13 = (bf16[624,384]{1,0:T(8,128)(2,1)S(1)}, bf16[624,384]{1,0:T(8,128)(2,1)S(1)}, u32[]{:S(2)}, u32[]{:S(2)}) collective-permute-start(bf16[624,384]{1,0:T(8,128)(2,1)S(1)} %get-tuple-element.96), channel_id=1, source_target_pairs={{0,1},{1,0},{2,3},{3,2},{4,5},{5,4},{6,7},{7,6},{8,9},{9,8},{10,11... | collective-permute-start | bytes 1437704 | tf_op jit(solution)/shard_map/ppermute | solution.py:62
  86.5 19.9 %collective-permute-start.21 = (bf16[192,1536]{1,0:T(8,128)(2,1)S(1)}, bf16[192,1536]{1,0:T(8,128)(2,1)S(1)}, u32[]{:S(2)}, u32[]{:S(2)}) collective-permute-start(bf16[192,1536]{1,0:T(8,128)(2,1)S(1)} %get-tuple-element.115), channel_id=1, source_target_pairs={{0,16},{16,0},{1,17},{17,1},{2,18},{18,2},{3,19},{19,3},{4,20},{20... | collective-permute-start | bytes 1769480 | tf_op jit(solution)/shard_map/ppermute | solution.py:62
  89.9 1.9 %collective-permute-start.16 = (bf16[624,384]{1,0:T(8,128)(2,1)S(1)}, bf16[624,384]{1,0:T(8,128)(2,1)S(1)}, u32[]{:S(2)}, u32[]{:S(2)}) collective-permute-start(bf16[624,384]{1,0:T(8,128)(2,1)S(1)} %add.76.one), channel_id=1, source_target_pairs={{0,1},{1,0},{2,3},{3,2},{4,5},{5,4},{6,7},{7,6},{8,9},{9,8},{10,11... | collective-permute-start | bytes 1437704 | tf_op jit(solution)/shard_map/ppermute | solution.py:62
  90.0 25.3 %collective-permute-start.17 = (bf16[192,1536]{1,0:T(8,128)(2,1)S(1)}, bf16[192,1536]{1,0:T(8,128)(2,1)S(1)}, u32[]{:S(2)}, u32[]{:S(2)}) collective-permute-start(bf16[192,1536]{1,0:T(8,128)(2,1)S(1)} %copy-done.24), channel_id=1, source_target_pairs={{0,16},{16,0},{1,17},{17,1},{2,18},{18,2},{3,19},{19,3},{4,20},{20... | collective-permute-start | bytes 1769480 | tf_op jit(solution)/shard_map/ppermute | solution.py:62
  90.2 18.1 %collective-permute-start.14 = (bf16[624,384]{1,0:T(8,128)(2,1)S(1)}, bf16[624,384]{1,0:T(8,128)(2,1)S(1)}, u32[]{:S(2)}, u32[]{:S(2)}) collective-permute-start(bf16[624,384]{1,0:T(8,128)(2,1)S(1)} %add.74), channel_id=1, source_target_pairs={{0,2},{1,3},{2,0},{3,1},{4,6},{5,7},{6,4},{7,5},{8,10},{9,11},{10,... | collective-permute-start | bytes 1437704 | tf_op jit(solution)/shard_map/ppermute | solution.py:62
  105.6 23.0 %collective-permute-start.23 = (bf16[416,768]{1,0:T(8,128)(2,1)S(1)}, bf16[416,768]{1,0:T(8,128)(2,1)S(1)}, u32[]{:S(2)}, u32[]{:S(2)}) collective-permute-start(bf16[416,768]{1,0:T(8,128)(2,1)S(1)} %get-tuple-element.118), channel_id=1, source_target_pairs={{0,16},{16,0},{1,17},{17,1},{2,18},{18,2},{3,19},{19,3},{4,20},{20... | collective-permute-start | bytes 1916936 | tf_op jit(solution)/shard_map/ppermute | solution.py:62
  106.5 17.8 %collective-permute-start.22 = (bf16[192,1536]{1,0:T(8,128)(2,1)S(1)}, bf16[192,1536]{1,0:T(8,128)(2,1)S(1)}, u32[]{:S(2)}, u32[]{:S(2)}) collective-permute-start(bf16[192,1536]{1,0:T(8,128)(2,1)S(1)} %add.80), channel_id=1, source_target_pairs={{0,2},{1,11},{2,4},{3,13},{4,6},{5,15},{6,0},{7,9},{8,10},{9,3},{1... | collective-permute-start | bytes 1769480 | tf_op jit(solution)/shard_map/ppermute | solution.py:51
  115.5 1.9 %collective-permute-start.18 = (bf16[624,384]{1,0:T(8,128)(2,1)S(1)}, bf16[624,384]{1,0:T(8,128)(2,1)S(1)}, u32[]{:S(2)}, u32[]{:S(2)}) collective-permute-start(bf16[624,384]{1,0:T(8,128)(2,1)S(1)} %copy-done.25), channel_id=1, source_target_pairs={{0,1},{1,0},{2,3},{3,2},{4,5},{5,4},{6,7},{7,6},{8,9},{9,8},{10,11... | collective-permute-start | bytes 1437704 | tf_op jit(solution)/shard_map/ppermute | solution.py:62
  115.6 6.1 %collective-permute-start.19 = (bf16[624,384]{1,0:T(8,128)(2,1)S(1)}, bf16[624,384]{1,0:T(8,128)(2,1)S(1)}, u32[]{:S(2)}, u32[]{:S(2)}) collective-permute-start(bf16[624,384]{1,0:T(8,128)(2,1)S(1)} %add.75.one), channel_id=1, source_target_pairs={{0,1},{1,0},{2,3},{3,2},{4,5},{5,4},{6,7},{7,6},{8,9},{9,8},{10,11... | collective-permute-start | bytes 1437704 | tf_op jit(solution)/shard_map/ppermute | solution.py:62
  116.1 18.0 %collective-permute-start.24 = (bf16[192,1536]{1,0:T(8,128)(2,1)S(1)}, bf16[192,1536]{1,0:T(8,128)(2,1)S(1)}, u32[]{:S(2)}, u32[]{:S(2)}) collective-permute-start(bf16[192,1536]{1,0:T(8,128)(2,1)S(1)} %add.77), channel_id=1, source_target_pairs={{0,0},{1,9},{2,6},{3,15},{4,4},{5,13},{6,2},{7,11},{8,8},{9,1},{10... | collective-permute-start | bytes 1769480 | tf_op jit(solution)/shard_map/ppermute | solution.py:51
  117.5 16.4 %collective-permute-start.20 = (bf16[624,384]{1,0:T(8,128)(2,1)S(1)}, bf16[624,384]{1,0:T(8,128)(2,1)S(1)}, u32[]{:S(2)}, u32[]{:S(2)}) collective-permute-start(bf16[624,384]{1,0:T(8,128)(2,1)S(1)} %add.78), channel_id=1, source_target_pairs={{0,2},{1,3},{2,0},{3,1},{4,6},{5,7},{6,4},{7,5},{8,10},{9,11},{10,... | collective-permute-start | bytes 1437704 | tf_op jit(solution)/shard_map/ppermute | solution.py:62
  128.6 23.0 %collective-permute-start.27 = (bf16[208,768]{1,0:T(8,128)(2,1)S(1)}, bf16[208,768]{1,0:T(8,128)(2,1)S(1)}, u32[]{:S(2)}, u32[]{:S(2)}) collective-permute-start(bf16[208,768]{1,0:T(8,128)(2,1)S(1)} %slice_add_fusion.1), channel_id=1, source_target_pairs={{0,2},{1,11},{2,4},{3,13},{4,6},{5,15},{6,0},{7,9},{8,10},{9,3},{1... | collective-permute-start | bytes 958472 | tf_op jit(solution)/shard_map/ppermute | solution.py:51
  130.6 21.0 %collective-permute-start.28 = (bf16[208,768]{1,0:T(8,128)(2,1)S(1)}, bf16[208,768]{1,0:T(8,128)(2,1)S(1)}, u32[]{:S(2)}, u32[]{:S(2)}) collective-permute-start(bf16[208,768]{1,0:T(8,128)(2,1)S(1)} %slice_add_fusion), channel_id=1, source_target_pairs={{0,0},{1,9},{2,6},{3,15},{4,4},{5,13},{6,2},{7,11},{8,8},{9,1},{10... | collective-permute-start | bytes 958472 | tf_op jit(solution)/shard_map/ppermute | solution.py:51
  134.2 33.7 %collective-permute-start.31 = (bf16[192,1536]{1,0:T(8,128)(2,1)S(1)}, bf16[192,1536]{1,0:T(8,128)(2,1)S(1)}, u32[]{:S(2)}, u32[]{:S(2)}) collective-permute-start(bf16[192,1536]{1,0:T(8,128)(2,1)S(1)} %add.83), channel_id=1, source_target_pairs={{0,16},{16,0},{1,17},{17,1},{2,18},{18,2},{3,19},{19,3},{4,20},{20... | collective-permute-start | bytes 1769480 | tf_op jit(solution)/shard_map/ppermute | solution.py:62
  145.9 1.9 %collective-permute-start.25 = (bf16[320,384]{1,0:T(8,128)(2,1)S(1)}, bf16[320,384]{1,0:T(8,128)(2,1)S(1)}, u32[]{:S(2)}, u32[]{:S(2)}) collective-permute-start(bf16[320,384]{1,0:T(8,128)(2,1)S(1)} %slice.50), channel_id=1, source_target_pairs={{0,1},{1,0},{2,3},{3,2},{4,5},{5,4},{6,7},{7,6},{8,9},{9,8},{10,11... | collective-permute-start | bytes 737288 | tf_op jit(solution)/shard_map/ppermute | solution.py:62
  151.7 14.6 %collective-permute-start.33 = (bf16[208,768]{1,0:T(8,128)(2,1)S(1)}, bf16[208,768]{1,0:T(8,128)(2,1)S(1)}, u32[]{:S(2)}, u32[]{:S(2)}) collective-permute-start(bf16[208,768]{1,0:T(8,128)(2,1)S(1)} %add.84.one), channel_id=1, source_target_pairs={{0,16},{16,0},{1,17},{17,1},{2,18},{18,2},{3,19},{19,3},{4,20},{20... | collective-permute-start | bytes 958472 | tf_op jit(solution)/shard_map/ppermute | solution.py:62
  152.7 3.6 %collective-permute-start.29 = (f32[2,768]{1,0:T(2,128)S(1)}, f32[2,768]{1,0:T(2,128)S(1)}, u32[]{:S(2)}, u32[]{:S(2)}) collective-permute-start(f32[2,768]{1,0:T(2,128)S(1)} %get-tuple-element.126), channel_id=1, source_target_pairs={{0,4},{4,0},{8,12},{12,8},{1,5},{5,1},{9,13},{13,9},{2,6},{6,2},{1... | collective-permute-start | bytes 18440 | tf_op jit(solution)/shard_map/ppermute | solution.py:62
  156.3 4.5 %collective-permute-start.30 = (f32[2,768]{1,0:T(2,128)S(1)}, f32[2,768]{1,0:T(2,128)S(1)}, u32[]{:S(2)}, u32[]{:S(2)}) collective-permute-start(f32[2,768]{1,0:T(2,128)S(1)} %add.85), channel_id=1, source_target_pairs={{0,8},{4,12},{8,0},{12,4},{1,9},{5,13},{9,1},{13,5},{2,10},{6,14},... | collective-permute-start | bytes 18440 | tf_op jit(solution)/shard_map/ppermute | solution.py:62
  168.1 3.7 %collective-permute-start.32 = (f32[2,768]{1,0:T(2,128)S(1)}, f32[2,768]{1,0:T(2,128)S(1)}, u32[]{:S(2)}, u32[]{:S(2)}) collective-permute-start(f32[2,768]{1,0:T(2,128)S(1)} %add.86), channel_id=1, source_target_pairs={{0,16},{16,0},{1,17},{17,1},{2,18},{18,2},{3,19},{19,3},{4,20},{20... | collective-permute-start | bytes 18440 | tf_op jit(solution)/shard_map/ppermute | solution.py:62
  (28 other events, 289.4 us)

commit v4 on v3

--- a/solution.py
+++ b/solution.py
@@ -588,7 +588,7 @@
     packed_total = after(packed_given[0], grad_tokens) + packed_given[1]
     own, other = finish(grid, packed_total)
     late = sum_axis(grid, after(late, packed_total), "row", 1)
-    late = sum_axis(grid, after(late, grad_both), "dp", 1)
+    late = sum_axis(grid, late, "dp", 1)
     square, line_of = (query_weight.shape, F32), lambda size: (((size,), F32), 0)
     (
         grad_query,

time: 173 us -> 171 us (0.988)
  the two profiles are of different devices: /device:TPU:24 before, /device:TPU:0 now
where the time goes in v4:
time: 171 us; the launch traced here: 169 us
  starting transfers between devices  61.3 us (36%)
  waiting for transfers between devices  51.4 us (30%)
  Pallas kernels  46.1 us (27%)
  local copies, waits for them, and re-layouts  6.57 us (4%)
  other arithmetic  2.72 us (2%)
    pallas_call x10, Pallas kernels, run(): pl.pallas_call(kernel, out_shape=shapes, in_specs=in_specs, out_specs=[sp...  46.1 us
    ppermute x25, waiting for transfers between devices, swap(): return lax.ppermute(array, axis, [(i, i ^ flip) for i in range(size)])  42.9 us
    ppermute x25, starting transfers between devices, swap(): return lax.ppermute(array, axis, [(i, i ^ flip) for i in range(size)])  40.7 us
    ppermute x4, starting transfers between devices, fetch(): lax.ppermute(array, ('dp', 'row', 'col'), [(holder, me) for me, holder in...  15.7 us
    ppermute x4, waiting for transfers between devices, fetch(): lax.ppermute(array, ('dp', 'row', 'col'), [(holder, me) for me, holder in...  6.61 us
    ppermute x4, starting transfers between devices, give(): lax.ppermute(array, ('dp', 'row', 'col'), [(me, holder) for me, holder in...  4.25 us
  transfers between devices with their start and end apart: 34, of which 17 were waited for; matrix products, arithmetic and copies ran while one was open for 2% of the time, Pallas kernels for 23%

profile of v4, /device:TPU:0, one launch (start us, length us, event | category | flops | bytes accessed | tf_op | source)
XLA Modules:
  0.0 169.3 jit_solution(5031390588170951795)
XLA Ops:
  3.8 5.7 %collective-permute-start = (bf16[192,768]{1,0:T(8,128)(2,1)S(1)}, bf16[192,768]{1,0:T(8,128)(2,1)S(1)}, u32[]{:S(2)}, u32[]{:S(2)}) collective-permute-start(bf16[192,768]{1,0:T(8,128)(2,1)S(1)} %concatenate.12), channel_id=1, source_target_pairs={{2,0},{11,1},{4,2},{13,3},{6,4},{15,5},{0,6},{9,7},{10,8},{3,9},{1... | collective-permute-start | bytes 884744 | tf_op jit(solution)/shard_map/ppermute | solution.py:48
  10.3 6.6 %collective-permute-done.h0 = bf16[192,768]{1,0:T(8,128)(2,1)S(1)} collective-permute-done((bf16[192,768]{1,0:T(8,128)(2,1)S(1)}, bf16[192,768]{1,0:T(8,128)(2,1)S(1)}, u32[]{:S(2)}, u32[]{:S(2)}) %collective-permute-start) | collective-permute-done | bytes 294944 | tf_op jit(solution)/shard_map/ppermute | solution.py:48
  16.9 3.4 %collective-permute-start.2 = (bf16[192,1536]{1,0:T(8,128)(2,1)}, bf16[192,1536]{1,0:T(8,128)(2,1)S(1)}, u32[]{:S(2)}, u32[]{:S(2)}) collective-permute-start(bf16[192,1536]{1,0:T(8,128)(2,1)} %pad_maximum_fusion), channel_id=1, source_target_pairs={{2,0},{11,1},{4,2},{13,3},{6,4},{15,5},{0,6},{9,7},{10,8},{3,9},{1... | collective-permute-start | bytes 1769480 | tf_op jit(solution)/shard_map/ppermute | solution.py:48
  21.2 5.0 %collective-permute-start.4 = (bf16[192,768]{1,0:T(8,128)(2,1)S(1)}, bf16[192,768]{1,0:T(8,128)(2,1)S(1)}, u32[]{:S(2)}, u32[]{:S(2)}) collective-permute-start(bf16[192,768]{1,0:T(8,128)(2,1)S(1)} %collective-permute-done.1.h2), channel_id=1, source_target_pairs={{0,16},{16,0},{1,17},{17,1},{2,18},{18,2},{3,19},{19,3},{4,20},{20... | collective-permute-start | bytes 884744 | tf_op jit(solution)/shard_map/ppermute | solution.py:62
  27.5 2.3 %shard_map.296 = (bf16[624,768]{1,0:T(8,128)(2,1)}, bf16[624,768]{1,0:T(8,128)(2,1)}, bf16[624,768]{1,0:T(8,128)(2,1)}, f32[1,768]{1,0:T(1,128)S(1)}) custom-call(bf16[591,768]{1,0:T(8,128)(2,1)S(1)} %copy-done.7, bf16[591,768]{1,0:T(8,128)(2,1)S(1)} %copy-done.8, f32[1,768]{1,0:T(1,128)S(1)} %reshape.116.gain, f32[1,768]{1,0:T(1,128)S(1)} %reshape.117.shift), custom_call_target="tpu_custom_call" | custom-call | flops 1 | bytes 1 | tf_op jit(solution)/shard_map/pallas_call | solution.py:399
  29.8 5.9 %collective-permute-start.8 = (bf16[192,1536]{1,0:T(8,128)(2,1)}, bf16[192,1536]{1,0:T(8,128)(2,1)}, u32[]{:S(2)}, u32[]{:S(2)}) collective-permute-start(bf16[192,1536]{1,0:T(8,128)(2,1)} %pad_maximum_fusion), channel_id=1, source_target_pairs={{0,0},{9,1},{6,2},{15,3},{4,4},{13,5},{2,6},{11,7},{8,8},{1,9},{14... | collective-permute-start | bytes 1769480 | tf_op jit(solution)/shard_map/ppermute | solution.py:48
  35.7 3.3 %collective-permute-start.7 = (bf16[192,1536]{1,0:T(8,128)(2,1)S(1)}, bf16[192,1536]{1,0:T(8,128)(2,1)S(1)}, u32[]{:S(2)}, u32[]{:S(2)}) collective-permute-start(bf16[192,1536]{1,0:T(8,128)(2,1)S(1)} %collective-permute-done.2.w0), channel_id=1, source_target_pairs={{0,16},{16,0},{1,17},{17,1},{2,18},{18,2},{3,19},{19,3},{4,20},{20... | collective-permute-start | bytes 1769480 | tf_op jit(solution)/shard_map/ppermute | solution.py:62
  39.2 6.1 %shard_map.297 = (bf16[624,768]{1,0:T(8,128)(2,1)}, bf16[624,256]{1,0:T(8,128)(2,1)S(1)}, bf16[9,208,208]{2,1,0:T(8,128)(2,1)}, bf16[624,384]{1,0:T(8,128)(2,1)S(1)}, bf16[624,384]{1,0:T(8,128)(2,1)}) custom-call(s32[2]{0:T(128)S(1)} %pad_add_fusion.ids, bf16[624,768]{1,0:T(8,128)(2,1)} %get-tuple-element.78.first, ...), custom_call_target="tpu_custom_call" | custom-call | flops 1 | bytes 1 | tf_op jit(solution)/shard_map/pallas_call | solution.py:399
  45.2 2.0 %collective-permute-start.6 = (bf16[624,384]{1,0:T(8,128)(2,1)}, bf16[624,384]{1,0:T(8,128)(2,1)S(1)}, u32[]{:S(2)}, u32[]{:S(2)}) collective-permute-start(bf16[624,384]{1,0:T(8,128)(2,1)} %get-tuple-element.82), channel_id=1, source_target_pairs={{0,1},{1,0},{2,3},{3,2},{4,5},{5,4},{6,7},{7,6},{8,9},{9,8},{10,11... | collective-permute-start | bytes 1437704 | tf_op jit(solution)/shard_map/ppermute | solution.py:62
  49.0 2.4 %collective-permute-done.7.w1 = bf16[192,1536]{1,0:T(8,128)(2,1)S(1)} collective-permute-done((bf16[192,1536]{1,0:T(8,128)(2,1)S(1)}, bf16[192,1536]{1,0:T(8,128)(2,1)S(1)}, u32[]{:S(2)}, u32[]{:S(2)}) %collective-permute-start.7) | collective-permute-done | bytes 589856 | tf_op jit(solution)/shard_map/ppermute | solution.py:62
  51.5 5.9 %collective-permute-start.9 = (bf16[624,384]{1,0:T(8,128)(2,1)S(1)}, bf16[624,384]{1,0:T(8,128)(2,1)S(1)}, u32[]{:S(2)}, u32[]{:S(2)}) collective-permute-start(bf16[624,384]{1,0:T(8,128)(2,1)S(1)} %add.71), channel_id=1, source_target_pairs={{0,2},{1,3},{2,0},{3,1},{4,6},{5,7},{6,4},{7,5},{8,10},{9,11},{10,... | collective-permute-start | bytes 1437704 | tf_op jit(solution)/shard_map/ppermute | solution.py:62
  57.4 10.9 %collective-permute-done.9 = bf16[624,384]{1,0:T(8,128)(2,1)S(1)} collective-permute-done((bf16[624,384]{1,0:T(8,128)(2,1)S(1)}, bf16[624,384]{1,0:T(8,128)(2,1)S(1)}, u32[]{:S(2)}, u32[]{:S(2)}) %collective-permute-start.9) | collective-permute-done | bytes 479264 | tf_op jit(solution)/shard_map/ppermute | solution.py:62
  68.6 1.8 %collective-permute-done.11.two.mid_two = bf16[624,384]{1,0:T(8,128)(2,1)S(1)} collective-permute-done((bf16[624,384]{1,0:T(8,128)(2,1)S(1)}, bf16[624,384]{1,0:T(8,128)(2,1)S(1)}, u32[]{:S(2)}, u32[]{:S(2)}) %collective-permute-start.11) | collective-permute-done | bytes 479264 | tf_op jit(solution)/shard_map/ppermute | solution.py:62
  70.3 7.3 %shard_map.298 = (bf16[624,768]{1,0:T(8,128)(2,1)}, bf16[624,768]{1,0:T(8,128)(2,1)}, bf16[624,768]{1,0:T(8,128)(2,1)}, bf16[624,384]{1,0:T(8,128)(2,1)S(1)}, bf...) custom-call(s32[2]{0:T(128)S(1)} %pad_add_fusion.ids, bf16[624,768]{1,0:T(8,128)(2,1)} %get-tuple-element.77.tokens, ...), custom_call_target="tpu_custom_call" | custom-call | flops 1 | bytes 1 | tf_op jit(solution)/shard_map/pallas_call | solution.py:399
  80.5 5.1 %shard_map.299 = (bf16[192,1536]{1,0:T(8,128)(2,1)S(1)}, bf16[192,1536]{1,0:T(8,128)(2,1)S(1)}, bf16[192,1536]{1,0:T(8,128)(2,1)S(1)}, bf16[192,1536]{1,0:T(8,128)(2,1)}) custom-call(s32[2]{0:T(128)S(1)} %pad_add_fusion.ids, bf16[624,768]{1,0:T(8,128)(2,1)} %get-tuple-element.85.cot, bf16[624,768]{1,0:T(8,128)(2,1)} %get-tuple-element.93.hidden, ...), custom_call_target="tpu_custom_call" | custom-call | flops 1 | bytes 1 | tf_op jit(solution)/shard_map/pallas_call | solution.py:399
  85.6 4.3 %shard_map.300 = (bf16[624,384]{1,0:T(8,128)(2,1)S(1)}, bf16[624,384]{1,0:T(8,128)(2,1)S(1)}) custom-call(s32[2]{0:T(128)S(1)} %pad_add_fusion.ids, bf16[624,768]{1,0:T(8,128)(2,1)} %get-tuple-element.93.hidden, bf16[192,1536]{1,0:T(8,128)(2,1)S(1)} %copy-done.6, bf16[192,1536]{1,0:T(8,128)(2,1)} %copy-done.9, bf16[192,1536]{1,0:T(8,128)(2,1)} %collective-permute-done.8.w2, ...), custom_call_target="tpu_custom_call" | custom-call | flops 1 | bytes 1 | tf_op jit(solution)/shard_map/pallas_call | solution.py:399
  90.9 1.9 %collective-permute-done.15 = bf16[624,384]{1,0:T(8,128)(2,1)S(1)} collective-permute-done((bf16[624,384]{1,0:T(8,128)(2,1)S(1)}, bf16[624,384]{1,0:T(8,128)(2,1)S(1)}, u32[]{:S(2)}, u32[]{:S(2)}) %collective-permute-start.15) | collective-permute-done | bytes 479264 | tf_op jit(solution)/shard_map/ppermute | solution.py:62
  95.6 9.6 %shard_map.301 = (bf16[624,768]{1,0:T(8,128)(2,1)}, bf16[624,768]{1,0:T(8,128)(2,1)}, bf16[624,384]{1,0:T(8,128)(2,1)S(1)}, bf16[624,384]{1,0:T(8,128)(2,1)}, f32[4,768]{1,0:T(4,128)S(1)}) custom-call(s32[2]{0:T(128)S(1)} %pad_add_fusion.ids, bf16[624,384]{1,0:T(8,128)(2,1)} %copy-done.11, bf16[624,384]{1,0:T(8,128)(2,1)} %copy-done.12, ...), custom_call_target="tpu_custom_call" | custom-call | flops 1 | bytes 1 | tf_op jit(solution)/shard_map/pallas_call | solution.py:399
  105.2 3.3 %shard_map.302 = (bf16[208,768]{1,0:T(8,128)(2,1)S(1)}, bf16[208,768]{1,0:T(8,128)(2,1)S(1)}, bf16[416,768]{1,0:T(8,128)(2,1)S(1)}) custom-call(s32[2]{0:T(128)S(1)} %pad_add_fusion.ids, bf16[624,768]{1,0:T(8,128)(2,1)} %get-tuple-element.78.first, bf16[624,768]{1,0:T(8,128)(2,1)} %get-tuple-element.101.joined, ...), custom_call_target="tpu_custom_call" | custom-call | flops 1 | bytes 1 | tf_op jit(solution)/shard_map/pallas_call | solution.py:399
  111.5 7.4 %collective-permute-done.17 = bf16[192,1536]{1,0:T(8,128)(2,1)S(1)} collective-permute-done((bf16[192,1536]{1,0:T(8,128)(2,1)S(1)}, bf16[192,1536]{1,0:T(8,128)(2,1)S(1)}, u32[]{:S(2)}, u32[]{:S(2)}) %collective-permute-start.17) | collective-permute-done | bytes 589856 | tf_op jit(solution)/shard_map/ppermute | solution.py:62
  121.1 6.6 %collective-permute-start.20 = (bf16[624,384]{1,0:T(8,128)(2,1)S(1)}, bf16[624,384]{1,0:T(8,128)(2,1)S(1)}, u32[]{:S(2)}, u32[]{:S(2)}) collective-permute-start(bf16[624,384]{1,0:T(8,128)(2,1)S(1)} %add.78), channel_id=1, source_target_pairs={{0,2},{1,3},{2,0},{3,1},{4,6},{5,7},{6,4},{7,5},{8,10},{9,11},{10,... | collective-permute-start | bytes 1437704 | tf_op jit(solution)/shard_map/ppermute | solution.py:62
  127.7 2.7 %shard_map.303 = bf16[591,768]{1,0:T(8,128)(2,1)} custom-call(s32[2]{0:T(128)S(1)} %pad_add_fusion.ids, bf16[624,384]{1,0:T(8,128)(2,1)S(1)} %add.75.one, bf16[624,384]{1,0:T(8,128)(2,1)S(1)} %collective-permute-done.19.two, bf16[624,768]{1,0:T(8,128)(2,1)} %get-tuple-element.77.tokens, bf16[624,384]{1,0:T(8,128)(2,1)S(1)} %copy-done.1, ...), custom_call_target="tpu_custom_call" | custom-call | flops 1 | bytes 1 | tf_op jit(solution)/shard_map/pallas_call | solution.py:399
  130.4 1.7 %collective-permute-done.23 = bf16[416,768]{1,0:T(8,128)(2,1)S(1)} collective-permute-done((bf16[416,768]{1,0:T(8,128)(2,1)S(1)}, bf16[416,768]{1,0:T(8,128)(2,1)S(1)}, u32[]{:S(2)}, u32[]{:S(2)}) %collective-permute-start.23) | collective-permute-done | bytes 639008 | tf_op jit(solution)/shard_map/ppermute | solution.py:62
  134.5 3.7 %collective-permute-done.20 = bf16[624,384]{1,0:T(8,128)(2,1)S(1)} collective-permute-done((bf16[624,384]{1,0:T(8,128)(2,1)S(1)}, bf16[624,384]{1,0:T(8,128)(2,1)S(1)}, u32[]{:S(2)}, u32[]{:S(2)}) %collective-permute-start.20) | collective-permute-done | bytes 479264 | tf_op jit(solution)/shard_map/ppermute | solution.py:62
  138.5 1.9 %collective-permute-start.33 = (bf16[192,1536]{1,0:T(8,128)(2,1)S(1)}, bf16[192,1536]{1,0:T(8,128)(2,1)S(1)}, u32[]{:S(2)}, u32[]{:S(2)}) collective-permute-start(bf16[192,1536]{1,0:T(8,128)(2,1)S(1)} %add.83), channel_id=1, source_target_pairs={{0,16},{16,0},{1,17},{17,1},{2,18},{18,2},{3,19},{19,3},{4,20},{20... | collective-permute-start | bytes 1769480 | tf_op jit(solution)/shard_map/ppermute | solution.py:62
  142.3 3.8 %shard_map.304 = (bf16[591,768]{1,0:T(8,128)(2,1)}, f32[2,768]{1,0:T(2,128)S(1)}) custom-call(s32[2]{0:T(128)S(1)} %pad_add_fusion.ids, bf16[624,384]{1,0:T(8,128)(2,1)S(1)} %add.79.one, bf16[320,384]{1,0:T(8,128)(2,1)S(1)} %collective-permute-done.25.upper, bf16[304,384]{1,0:T(8,128)(2,1)S(1)} %collective-permute-done.26.lower, ...), custom_call_target="tpu_custom_call" | custom-call | flops 1 | bytes 1 | tf_op jit(solution)/shard_map/pallas_call | solution.py:399
  146.1 1.9 %collective-permute-done.27 = bf16[208,768]{1,0:T(8,128)(2,1)S(1)} collective-permute-done((bf16[208,768]{1,0:T(8,128)(2,1)S(1)}, bf16[208,768]{1,0:T(8,128)(2,1)S(1)}, u32[]{:S(2)}, u32[]{:S(2)}) %collective-permute-start.27) | collective-permute-done | bytes 319520 | tf_op jit(solution)/shard_map/ppermute | solution.py:51
  148.0 6.0 %collective-permute-start.32 = (bf16[208,768]{1,0:T(8,128)(2,1)S(1)}, bf16[208,768]{1,0:T(8,128)(2,1)S(1)}, u32[]{:S(2)}, u32[]{:S(2)}) collective-permute-start(bf16[208,768]{1,0:T(8,128)(2,1)S(1)} %add.84.one), channel_id=1, source_target_pairs={{0,16},{16,0},{1,17},{17,1},{2,18},{18,2},{3,19},{19,3},{4,20},{20... | collective-permute-start | bytes 958472 | tf_op jit(solution)/shard_map/ppermute | solution.py:62
  154.1 3.6 %collective-permute-done.29 = f32[2,768]{1,0:T(2,128)S(1)} collective-permute-done((f32[2,768]{1,0:T(2,128)S(1)}, f32[2,768]{1,0:T(2,128)S(1)}, u32[]{:S(2)}, u32[]{:S(2)}) %collective-permute-start.29) | collective-permute-done | bytes 6176 | tf_op jit(solution)/shard_map/ppermute | solution.py:62
  157.7 2.2 %collective-permute-start.30 = (f32[2,768]{1,0:T(2,128)S(1)}, f32[2,768]{1,0:T(2,128)S(1)}, u32[]{:S(2)}, u32[]{:S(2)}) collective-permute-start(f32[2,768]{1,0:T(2,128)S(1)} %add.85), channel_id=1, source_target_pairs={{0,8},{4,12},{8,0},{12,4},{1,9},{5,13},{9,1},{13,5},{2,10},{6,14},... | collective-permute-start | bytes 18440 | tf_op jit(solution)/shard_map/ppermute | solution.py:62
  159.9 2.3 %collective-permute-done.30 = f32[2,768]{1,0:T(2,128)S(1)} collective-permute-done((f32[2,768]{1,0:T(2,128)S(1)}, f32[2,768]{1,0:T(2,128)S(1)}, u32[]{:S(2)}, u32[]{:S(2)}) %collective-permute-start.30) | collective-permute-done | bytes 6176 | tf_op jit(solution)/shard_map/ppermute | solution.py:62
  162.6 3.2 %collective-permute-done.31 = f32[2,768]{1,0:T(2,128)S(1)} collective-permute-done((f32[2,768]{1,0:T(2,128)S(1)}, f32[2,768]{1,0:T(2,128)S(1)}, u32[]{:S(2)}, u32[]{:S(2)}) %collective-permute-start.31) | collective-permute-done | bytes 6176 | tf_op jit(solution)/shard_map/ppermute | solution.py:62
  (143 shorter events, 28.4 us)
Async XLA Ops:
  3.1 7.2 %collective-permute-start.1 = (bf16[192,768]{1,0:T(8,128)(2,1)S(1)}, bf16[192,768]{1,0:T(8,128)(2,1)S(1)}, u32[]{:S(2)}, u32[]{:S(2)}) collective-permute-start(bf16[192,768]{1,0:T(8,128)(2,1)S(1)} %concatenate.12), channel_id=1, source_target_pairs={{0,0},{9,1},{6,2},{15,3},{4,4},{13,5},{2,6},{11,7},{8,8},{1,9},{14... | collective-permute-start | bytes 884744 | tf_op jit(solution)/shard_map/ppermute | solution.py:48
  3.8 13.1 %collective-permute-start = (bf16[192,768]{1,0:T(8,128)(2,1)S(1)}, bf16[192,768]{1,0:T(8,128)(2,1)S(1)}, u32[]{:S(2)}, u32[]{:S(2)}) collective-permute-start(bf16[192,768]{1,0:T(8,128)(2,1)S(1)} %concatenate.12), channel_id=1, source_target_pairs={{2,0},{11,1},{4,2},{13,3},{6,4},{15,5},{0,6},{9,7},{10,8},{3,9},{1... | collective-permute-start | bytes 884744 | tf_op jit(solution)/shard_map/ppermute | solution.py:48
  16.9 18.8 %collective-permute-start.2 = (bf16[192,1536]{1,0:T(8,128)(2,1)}, bf16[192,1536]{1,0:T(8,128)(2,1)S(1)}, u32[]{:S(2)}, u32[]{:S(2)}) collective-permute-start(bf16[192,1536]{1,0:T(8,128)(2,1)} %pad_maximum_fusion), channel_id=1, source_target_pairs={{2,0},{11,1},{4,2},{13,3},{6,4},{15,5},{0,6},{9,7},{10,8},{3,9},{1... | collective-permute-start | bytes 1769480 | tf_op jit(solution)/shard_map/ppermute | solution.py:48
  20.4 18.6 %collective-permute-start.5 = (f32[1152]{0:T(1024)S(1)}, f32[1152]{0:T(1024)S(1)}, u32[]{:S(2)}, u32[]{:S(2)}) collective-permute-start(f32[1152]{0:T(1024)S(1)} %concatenate.14), channel_id=1, source_target_pairs={{0,0},{9,1},{6,2},{15,3},{4,4},{13,5},{2,6},{11,7},{8,8},{1,9},{14... | collective-permute-start | bytes 13832 | tf_op jit(solution)/shard_map/ppermute | solution.py:58
  21.2 18.0 %collective-permute-start.4 = (bf16[192,768]{1,0:T(8,128)(2,1)S(1)}, bf16[192,768]{1,0:T(8,128)(2,1)S(1)}, u32[]{:S(2)}, u32[]{:S(2)}) collective-permute-start(bf16[192,768]{1,0:T(8,128)(2,1)S(1)} %collective-permute-done.1.h2), channel_id=1, source_target_pairs={{0,16},{16,0},{1,17},{17,1},{2,18},{18,2},{3,19},{19,3},{4,20},{20... | collective-permute-start | bytes 884744 | tf_op jit(solution)/shard_map/ppermute | solution.py:62
  26.1 13.0 %collective-permute-start.3 = (bf16[192,768]{1,0:T(8,128)(2,1)S(1)}, bf16[192,768]{1,0:T(8,128)(2,1)S(1)}, u32[]{:S(2)}, u32[]{:S(2)}) collective-permute-start(bf16[192,768]{1,0:T(8,128)(2,1)S(1)} %collective-permute-done.h0), channel_id=1, source_target_pairs={{0,16},{16,0},{1,17},{17,1},{2,18},{18,2},{3,19},{19,3},{4,20},{20... | collective-permute-start | bytes 884744 | tf_op jit(solution)/shard_map/ppermute | solution.py:62
  29.8 17.4 %collective-permute-start.8 = (bf16[192,1536]{1,0:T(8,128)(2,1)}, bf16[192,1536]{1,0:T(8,128)(2,1)}, u32[]{:S(2)}, u32[]{:S(2)}) collective-permute-start(bf16[192,1536]{1,0:T(8,128)(2,1)} %pad_maximum_fusion), channel_id=1, source_target_pairs={{0,0},{9,1},{6,2},{15,3},{4,4},{13,5},{2,6},{11,7},{8,8},{1,9},{14... | collective-permute-start | bytes 1769480 | tf_op jit(solution)/shard_map/ppermute | solution.py:48
  35.7 15.7 %collective-permute-start.7 = (bf16[192,1536]{1,0:T(8,128)(2,1)S(1)}, bf16[192,1536]{1,0:T(8,128)(2,1)S(1)}, u32[]{:S(2)}, u32[]{:S(2)}) collective-permute-start(bf16[192,1536]{1,0:T(8,128)(2,1)S(1)} %collective-permute-done.2.w0), channel_id=1, source_target_pairs={{0,16},{16,0},{1,17},{17,1},{2,18},{18,2},{3,19},{19,3},{4,20},{20... | collective-permute-start | bytes 1769480 | tf_op jit(solution)/shard_map/ppermute | solution.py:62
  45.2 3.6 %collective-permute-start.6 = (bf16[624,384]{1,0:T(8,128)(2,1)}, bf16[624,384]{1,0:T(8,128)(2,1)S(1)}, u32[]{:S(2)}, u32[]{:S(2)}) collective-permute-start(bf16[624,384]{1,0:T(8,128)(2,1)} %get-tuple-element.82), channel_id=1, source_target_pairs={{0,1},{1,0},{2,3},{3,2},{4,5},{5,4},{6,7},{7,6},{8,9},{9,8},{10,11... | collective-permute-start | bytes 1437704 | tf_op jit(solution)/shard_map/ppermute | solution.py:62
  47.2 21.2 %collective-permute-start.10 = (bf16[192,1536]{1,0:T(8,128)(2,1)}, bf16[192,1536]{1,0:T(8,128)(2,1)S(1)}, u32[]{:S(2)}, u32[]{:S(2)}) collective-permute-start(bf16[192,1536]{1,0:T(8,128)(2,1)} %collective-permute-done.8.w2), channel_id=1, source_target_pairs={{0,16},{16,0},{1,17},{17,1},{2,18},{18,2},{3,19},{19,3},{4,20},{20... | collective-permute-start | bytes 1769480 | tf_op jit(solution)/shard_map/ppermute | solution.py:62
  51.5 16.8 %collective-permute-start.9 = (bf16[624,384]{1,0:T(8,128)(2,1)S(1)}, bf16[624,384]{1,0:T(8,128)(2,1)S(1)}, u32[]{:S(2)}, u32[]{:S(2)}) collective-permute-start(bf16[624,384]{1,0:T(8,128)(2,1)S(1)} %add.71), channel_id=1, source_target_pairs={{0,2},{1,3},{2,0},{3,1},{4,6},{5,7},{6,4},{7,5},{8,10},{9,11},{10,... | collective-permute-start | bytes 1437704 | tf_op jit(solution)/shard_map/ppermute | solution.py:62
  68.4 1.9 %collective-permute-start.11 = (bf16[624,384]{1,0:T(8,128)(2,1)S(1)}, bf16[624,384]{1,0:T(8,128)(2,1)S(1)}, u32[]{:S(2)}, u32[]{:S(2)}) collective-permute-start(bf16[624,384]{1,0:T(8,128)(2,1)S(1)} %add.72.one.mid_one), channel_id=1, source_target_pairs={{0,1},{1,0},{2,3},{3,2},{4,5},{5,4},{6,7},{7,6},{8,9},{9,8},{10,11... | collective-permute-start | bytes 1437704 | tf_op jit(solution)/shard_map/ppermute | solution.py:62
  77.7 1.9 %collective-permute-start.12 = (bf16[624,384]{1,0:T(8,128)(2,1)S(1)}, bf16[624,384]{1,0:T(8,128)(2,1)S(1)}, u32[]{:S(2)}, u32[]{:S(2)}) collective-permute-start(bf16[624,384]{1,0:T(8,128)(2,1)S(1)} %get-tuple-element.88), channel_id=1, source_target_pairs={{0,1},{1,0},{2,3},{3,2},{4,5},{5,4},{6,7},{7,6},{8,9},{9,8},{10,11... | collective-permute-start | bytes 1437704 | tf_op jit(solution)/shard_map/ppermute | solution.py:62
  79.7 13.1 %collective-permute-start.15 = (bf16[624,384]{1,0:T(8,128)(2,1)S(1)}, bf16[624,384]{1,0:T(8,128)(2,1)S(1)}, u32[]{:S(2)}, u32[]{:S(2)}) collective-permute-start(bf16[624,384]{1,0:T(8,128)(2,1)S(1)} %add.73), channel_id=1, source_target_pairs={{0,2},{1,3},{2,0},{3,1},{4,6},{5,7},{6,4},{7,5},{8,10},{9,11},{10,... | collective-permute-start | bytes 1437704 | tf_op jit(solution)/shard_map/ppermute | solution.py:62
  90.0 3.2 %collective-permute-start.13 = (bf16[624,384]{1,0:T(8,128)(2,1)S(1)}, bf16[624,384]{1,0:T(8,128)(2,1)S(1)}, u32[]{:S(2)}, u32[]{:S(2)}) collective-permute-start(bf16[624,384]{1,0:T(8,128)(2,1)S(1)} %get-tuple-element.95), channel_id=1, source_target_pairs={{0,1},{1,0},{2,3},{3,2},{4,5},{5,4},{6,7},{7,6},{8,9},{9,8},{10,11... | collective-permute-start | bytes 1437704 | tf_op jit(solution)/shard_map/ppermute | solution.py:62
  90.1 19.8 %collective-permute-start.21 = (bf16[192,1536]{1,0:T(8,128)(2,1)S(1)}, bf16[192,1536]{1,0:T(8,128)(2,1)S(1)}, u32[]{:S(2)}, u32[]{:S(2)}) collective-permute-start(bf16[192,1536]{1,0:T(8,128)(2,1)S(1)} %get-tuple-element.114), channel_id=1, source_target_pairs={{0,16},{16,0},{1,17},{17,1},{2,18},{18,2},{3,19},{19,3},{4,20},{20... | collective-permute-start | bytes 1769480 | tf_op jit(solution)/shard_map/ppermute | solution.py:62
  92.9 1.9 %collective-permute-start.16 = (bf16[624,384]{1,0:T(8,128)(2,1)S(1)}, bf16[624,384]{1,0:T(8,128)(2,1)S(1)}, u32[]{:S(2)}, u32[]{:S(2)}) collective-permute-start(bf16[624,384]{1,0:T(8,128)(2,1)S(1)} %add.76.one), channel_id=1, source_target_pairs={{0,1},{1,0},{2,3},{3,2},{4,5},{5,4},{6,7},{7,6},{8,9},{9,8},{10,11... | collective-permute-start | bytes 1437704 | tf_op jit(solution)/shard_map/ppermute | solution.py:62
  93.0 25.9 %collective-permute-start.17 = (bf16[192,1536]{1,0:T(8,128)(2,1)S(1)}, bf16[192,1536]{1,0:T(8,128)(2,1)S(1)}, u32[]{:S(2)}, u32[]{:S(2)}) collective-permute-start(bf16[192,1536]{1,0:T(8,128)(2,1)S(1)} %copy-done.24), channel_id=1, source_target_pairs={{0,16},{16,0},{1,17},{17,1},{2,18},{18,2},{3,19},{19,3},{4,20},{20... | collective-permute-start | bytes 1769480 | tf_op jit(solution)/shard_map/ppermute | solution.py:62
  93.3 18.0 %collective-permute-start.14 = (bf16[624,384]{1,0:T(8,128)(2,1)S(1)}, bf16[624,384]{1,0:T(8,128)(2,1)S(1)}, u32[]{:S(2)}, u32[]{:S(2)}) collective-permute-start(bf16[624,384]{1,0:T(8,128)(2,1)S(1)} %add.74), channel_id=1, source_target_pairs={{0,2},{1,3},{2,0},{3,1},{4,6},{5,7},{6,4},{7,5},{8,10},{9,11},{10,... | collective-permute-start | bytes 1437704 | tf_op jit(solution)/shard_map/ppermute | solution.py:62
  108.6 23.6 %collective-permute-start.23 = (bf16[416,768]{1,0:T(8,128)(2,1)S(1)}, bf16[416,768]{1,0:T(8,128)(2,1)S(1)}, u32[]{:S(2)}, u32[]{:S(2)}) collective-permute-start(bf16[416,768]{1,0:T(8,128)(2,1)S(1)} %get-tuple-element.117), channel_id=1, source_target_pairs={{0,16},{16,0},{1,17},{17,1},{2,18},{18,2},{3,19},{19,3},{4,20},{20... | collective-permute-start | bytes 1916936 | tf_op jit(solution)/shard_map/ppermute | solution.py:62
  110.0 20.4 %collective-permute-start.22 = (bf16[192,1536]{1,0:T(8,128)(2,1)S(1)}, bf16[192,1536]{1,0:T(8,128)(2,1)S(1)}, u32[]{:S(2)}, u32[]{:S(2)}) collective-permute-start(bf16[192,1536]{1,0:T(8,128)(2,1)S(1)} %add.80), channel_id=1, source_target_pairs={{0,2},{1,11},{2,4},{3,13},{4,6},{5,15},{6,0},{7,9},{8,10},{9,3},{1... | collective-permute-start | bytes 1769480 | tf_op jit(solution)/shard_map/ppermute | solution.py:51
  119.1 8.6 %collective-permute-start.19 = (bf16[624,384]{1,0:T(8,128)(2,1)S(1)}, bf16[624,384]{1,0:T(8,128)(2,1)S(1)}, u32[]{:S(2)}, u32[]{:S(2)}) collective-permute-start(bf16[624,384]{1,0:T(8,128)(2,1)S(1)} %add.75.one), channel_id=1, source_target_pairs={{0,1},{1,0},{2,3},{3,2},{4,5},{5,4},{6,7},{7,6},{8,9},{9,8},{10,11... | collective-permute-start | bytes 1437704 | tf_op jit(solution)/shard_map/ppermute | solution.py:62
  119.6 18.7 %collective-permute-start.24 = (bf16[192,1536]{1,0:T(8,128)(2,1)S(1)}, bf16[192,1536]{1,0:T(8,128)(2,1)S(1)}, u32[]{:S(2)}, u32[]{:S(2)}) collective-permute-start(bf16[192,1536]{1,0:T(8,128)(2,1)S(1)} %add.77), channel_id=1, source_target_pairs={{0,0},{1,9},{2,6},{3,15},{4,4},{5,13},{6,2},{7,11},{8,8},{9,1},{10... | collective-permute-start | bytes 1769480 | tf_op jit(solution)/shard_map/ppermute | solution.py:51
  121.1 17.1 %collective-permute-start.20 = (bf16[624,384]{1,0:T(8,128)(2,1)S(1)}, bf16[624,384]{1,0:T(8,128)(2,1)S(1)}, u32[]{:S(2)}, u32[]{:S(2)}) collective-permute-start(bf16[624,384]{1,0:T(8,128)(2,1)S(1)} %add.78), channel_id=1, source_target_pairs={{0,2},{1,3},{2,0},{3,1},{4,6},{5,7},{6,4},{7,5},{8,10},{9,11},{10,... | collective-permute-start | bytes 1437704 | tf_op jit(solution)/shard_map/ppermute | solution.py:62
  132.2 15.8 %collective-permute-start.27 = (bf16[208,768]{1,0:T(8,128)(2,1)S(1)}, bf16[208,768]{1,0:T(8,128)(2,1)S(1)}, u32[]{:S(2)}, u32[]{:S(2)}) collective-permute-start(bf16[208,768]{1,0:T(8,128)(2,1)S(1)} %slice_add_fusion.1), channel_id=1, source_target_pairs={{0,2},{1,11},{2,4},{3,13},{4,6},{5,15},{6,0},{7,9},{8,10},{9,3},{1... | collective-permute-start | bytes 958472 | tf_op jit(solution)/shard_map/ppermute | solution.py:51
  133.6 14.3 %collective-permute-start.28 = (bf16[208,768]{1,0:T(8,128)(2,1)S(1)}, bf16[208,768]{1,0:T(8,128)(2,1)S(1)}, u32[]{:S(2)}, u32[]{:S(2)}) collective-permute-start(bf16[208,768]{1,0:T(8,128)(2,1)S(1)} %slice_add_fusion), channel_id=1, source_target_pairs={{0,0},{1,9},{2,6},{3,15},{4,4},{5,13},{6,2},{7,11},{8,8},{9,1},{10... | collective-permute-start | bytes 958472 | tf_op jit(solution)/shard_map/ppermute | solution.py:51
  138.5 29.6 %collective-permute-start.33 = (bf16[192,1536]{1,0:T(8,128)(2,1)S(1)}, bf16[192,1536]{1,0:T(8,128)(2,1)S(1)}, u32[]{:S(2)}, u32[]{:S(2)}) collective-permute-start(bf16[192,1536]{1,0:T(8,128)(2,1)S(1)} %add.83), channel_id=1, source_target_pairs={{0,16},{16,0},{1,17},{17,1},{2,18},{18,2},{3,19},{19,3},{4,20},{20... | collective-permute-start | bytes 1769480 | tf_op jit(solution)/shard_map/ppermute | solution.py:62
  140.4 1.9 %collective-permute-start.25 = (bf16[320,384]{1,0:T(8,128)(2,1)S(1)}, bf16[320,384]{1,0:T(8,128)(2,1)S(1)}, u32[]{:S(2)}, u32[]{:S(2)}) collective-permute-start(bf16[320,384]{1,0:T(8,128)(2,1)S(1)} %slice.50), channel_id=1, source_target_pairs={{0,1},{1,0},{2,3},{3,2},{4,5},{5,4},{6,7},{7,6},{8,9},{9,8},{10,11... | collective-permute-start | bytes 737288 | tf_op jit(solution)/shard_map/ppermute | solution.py:62
  148.0 18.4 %collective-permute-start.32 = (bf16[208,768]{1,0:T(8,128)(2,1)S(1)}, bf16[208,768]{1,0:T(8,128)(2,1)S(1)}, u32[]{:S(2)}, u32[]{:S(2)}) collective-permute-start(bf16[208,768]{1,0:T(8,128)(2,1)S(1)} %add.84.one), channel_id=1, source_target_pairs={{0,16},{16,0},{1,17},{17,1},{2,18},{18,2},{3,19},{19,3},{4,20},{20... | collective-permute-start | bytes 958472 | tf_op jit(solution)/shard_map/ppermute | solution.py:62
  154.0 3.6 %collective-permute-start.29 = (f32[2,768]{1,0:T(2,128)S(1)}, f32[2,768]{1,0:T(2,128)S(1)}, u32[]{:S(2)}, u32[]{:S(2)}) collective-permute-start(f32[2,768]{1,0:T(2,128)S(1)} %get-tuple-element.125), channel_id=1, source_target_pairs={{0,4},{4,0},{8,12},{12,8},{1,5},{5,1},{9,13},{13,9},{2,6},{6,2},{1... | collective-permute-start | bytes 18440 | tf_op jit(solution)/shard_map/ppermute | solution.py:62
  157.7 4.5 %collective-permute-start.30 = (f32[2,768]{1,0:T(2,128)S(1)}, f32[2,768]{1,0:T(2,128)S(1)}, u32[]{:S(2)}, u32[]{:S(2)}) collective-permute-start(f32[2,768]{1,0:T(2,128)S(1)} %add.85), channel_id=1, source_target_pairs={{0,8},{4,12},{8,0},{12,4},{1,9},{5,13},{9,1},{13,5},{2,10},{6,14},... | collective-permute-start | bytes 18440 | tf_op jit(solution)/shard_map/ppermute | solution.py:62
  162.2 3.6 %collective-permute-start.31 = (f32[2,768]{1,0:T(2,128)S(1)}, f32[2,768]{1,0:T(2,128)S(1)}, u32[]{:S(2)}, u32[]{:S(2)}) collective-permute-start(f32[2,768]{1,0:T(2,128)S(1)} %add.86), channel_id=1, source_target_pairs={{0,16},{16,0},{1,17},{17,1},{2,18},{18,2},{3,19},{19,3},{4,20},{20... | collective-permute-start | bytes 18440 | tf_op jit(solution)/shard_map/ppermute | solution.py:62
  (28 other events, 313.7 us)

commit v5 on v4

--- a/solution.py
+++ b/solution.py
@@ -449,7 +449,6 @@
     biases = grid.fetch_own(jnp.concatenate([query_bias, value_bias, expand_bias]))
     p_pieces = gather_block(grid, packed)
     w_pieces = gather_block(grid, after(both, p_pieces[0], p_pieces[2]))
-    p_pieces[0] = after(p_pieces[0], w_pieces[0])
     q_bias, v_bias, e_bias = biases[:wide], biases[wide : 2 * wide], biases[2 * wide :]
     nothing = jnp.zeros_like(q_bias)
     joined_bias = pack(q_bias, nothing, v_bias, nothing)
@@ -484,7 +483,7 @@
         images,
         weights_scratch + [pltpu.SemaphoreType.DMA((4,))],
     )
-    _, one = sum_two(grid, mine, away, (w_pieces[1], w_pieces[2]))
+    _, one = sum_two(grid, mine, away, (w_pieces[1],))
     two = grid.swap(after(one, w_pieces[3]), "col", 1)
     mid_one, mid_two = one, two
     second_in, hidden, grad_pre, mine, away, mlp_sums = run(

time: 171 us -> 169 us (0.988)
  no operation moved by 1% of the time
where the time goes in v5:
time: 169 us; the launch traced here: 167 us
  starting transfers between devices  61.1 us (36%)
  waiting for transfers between devices  49.7 us (29%)
  Pallas kernels  46.1 us (27%)
  local copies, waits for them, and re-layouts  6.57 us (4%)
  other arithmetic  2.72 us (2%)
    pallas_call x10, Pallas kernels, run(): pl.pallas_call(kernel, out_shape=shapes, in_specs=in_specs, out_specs=[sp...  46.1 us
    ppermute x25, waiting for transfers between devices, swap(): return lax.ppermute(array, axis, [(i, i ^ flip) for i in range(size)])  42.9 us
    ppermute x25, starting transfers between devices, swap(): return lax.ppermute(array, axis, [(i, i ^ flip) for i in range(size)])  39.4 us
    ppermute x4, starting transfers between devices, fetch(): lax.ppermute(array, ('dp', 'row', 'col'), [(holder, me) for me, holder in...  16.4 us
    ppermute x4, waiting for transfers between devices, fetch(): lax.ppermute(array, ('dp', 'row', 'col'), [(holder, me) for me, holder in...  4.98 us
    ppermute x4, starting transfers between devices, give(): lax.ppermute(array, ('dp', 'row', 'col'), [(me, holder) for me, holder in...  4.64 us
  transfers between devices with their start and end apart: 34, of which 17 were waited for; matrix products, arithmetic and copies ran while one was open for 2% of the time, Pallas kernels for 23%

profile of v5, /device:TPU:0, one launch (start us, length us, event | category | flops | bytes accessed | tf_op | source)
XLA Modules:
  0.0 167.5 jit_solution(8189273752680752585)
XLA Ops:
  3.1 4.0 %collective-permute-start = (bf16[192,768]{1,0:T(8,128)(2,1)S(1)}, bf16[192,768]{1,0:T(8,128)(2,1)S(1)}, u32[]{:S(2)}, u32[]{:S(2)}) collective-permute-start(bf16[192,768]{1,0:T(8,128)(2,1)S(1)} %concatenate.12), channel_id=1, source_target_pairs={{2,0},{11,1},{4,2},{13,3},{6,4},{15,5},{0,6},{9,7},{10,8},{3,9},{1... | collective-permute-start | bytes 884744 | tf_op jit(solution)/shard_map/ppermute | solution.py:48
  8.6 5.0 %collective-permute-done.h0 = bf16[192,768]{1,0:T(8,128)(2,1)S(1)} collective-permute-done((bf16[192,768]{1,0:T(8,128)(2,1)S(1)}, bf16[192,768]{1,0:T(8,128)(2,1)S(1)}, u32[]{:S(2)}, u32[]{:S(2)}) %collective-permute-start) | collective-permute-done | bytes 294944 | tf_op jit(solution)/shard_map/ppermute | solution.py:48
  13.6 5.8 %collective-permute-start.6 = (bf16[192,1536]{1,0:T(8,128)(2,1)}, bf16[192,1536]{1,0:T(8,128)(2,1)S(1)}, u32[]{:S(2)}, u32[]{:S(2)}) collective-permute-start(bf16[192,1536]{1,0:T(8,128)(2,1)} %pad_maximum_fusion), channel_id=1, source_target_pairs={{2,0},{11,1},{4,2},{13,3},{6,4},{15,5},{0,6},{9,7},{10,8},{3,9},{1... | collective-permute-start | bytes 1769480 | tf_op jit(solution)/shard_map/ppermute | solution.py:48
  20.3 4.1 %collective-permute-start.1 = (bf16[192,768]{1,0:T(8,128)(2,1)S(1)}, bf16[192,768]{1,0:T(8,128)(2,1)S(1)}, u32[]{:S(2)}, u32[]{:S(2)}) collective-permute-start(bf16[192,768]{1,0:T(8,128)(2,1)S(1)} %collective-permute-done.h0), channel_id=1, source_target_pairs={{0,16},{16,0},{1,17},{17,1},{2,18},{18,2},{3,19},{19,3},{4,20},{20... | collective-permute-start | bytes 884744 | tf_op jit(solution)/shard_map/ppermute | solution.py:62
  25.8 2.3 %shard_map.296 = (bf16[624,768]{1,0:T(8,128)(2,1)}, bf16[624,768]{1,0:T(8,128)(2,1)}, bf16[624,768]{1,0:T(8,128)(2,1)}, f32[1,768]{1,0:T(1,128)S(1)}) custom-call(bf16[591,768]{1,0:T(8,128)(2,1)S(1)} %copy-done.7, bf16[591,768]{1,0:T(8,128)(2,1)S(1)} %copy-done.8, f32[1,768]{1,0:T(1,128)S(1)} %reshape.116.gain, f32[1,768]{1,0:T(1,128)S(1)} %reshape.117.shift), custom_call_target="tpu_custom_call" | custom-call | flops 1 | bytes 1 | tf_op jit(solution)/shard_map/pallas_call | solution.py:399
  28.0 5.9 %collective-permute-start.9 = (bf16[192,1536]{1,0:T(8,128)(2,1)}, bf16[192,1536]{1,0:T(8,128)(2,1)}, u32[]{:S(2)}, u32[]{:S(2)}) collective-permute-start(bf16[192,1536]{1,0:T(8,128)(2,1)} %pad_maximum_fusion), channel_id=1, source_target_pairs={{0,0},{9,1},{6,2},{15,3},{4,4},{13,5},{2,6},{11,7},{8,8},{1,9},{14... | collective-permute-start | bytes 1769480 | tf_op jit(solution)/shard_map/ppermute | solution.py:48
  34.0 3.3 %collective-permute-start.7 = (bf16[192,1536]{1,0:T(8,128)(2,1)S(1)}, bf16[192,1536]{1,0:T(8,128)(2,1)S(1)}, u32[]{:S(2)}, u32[]{:S(2)}) collective-permute-start(bf16[192,1536]{1,0:T(8,128)(2,1)S(1)} %collective-permute-done.6.w0), channel_id=1, source_target_pairs={{0,16},{16,0},{1,17},{17,1},{2,18},{18,2},{3,19},{19,3},{4,20},{20... | collective-permute-start | bytes 1769480 | tf_op jit(solution)/shard_map/ppermute | solution.py:62
  37.4 6.1 %shard_map.297 = (bf16[624,768]{1,0:T(8,128)(2,1)}, bf16[624,256]{1,0:T(8,128)(2,1)S(1)}, bf16[9,208,208]{2,1,0:T(8,128)(2,1)}, bf16[624,384]{1,0:T(8,128)(2,1)S(1)}, bf16[624,384]{1,0:T(8,128)(2,1)}) custom-call(s32[2]{0:T(128)S(1)} %pad_add_fusion.ids, bf16[624,768]{1,0:T(8,128)(2,1)} %get-tuple-element.77.first, ...), custom_call_target="tpu_custom_call" | custom-call | flops 1 | bytes 1 | tf_op jit(solution)/shard_map/pallas_call | solution.py:399
  43.5 1.9 %collective-permute-start.5 = (bf16[624,384]{1,0:T(8,128)(2,1)}, bf16[624,384]{1,0:T(8,128)(2,1)S(1)}, u32[]{:S(2)}, u32[]{:S(2)}) collective-permute-start(bf16[624,384]{1,0:T(8,128)(2,1)} %get-tuple-element.79), channel_id=1, source_target_pairs={{0,1},{1,0},{2,3},{3,2},{4,5},{5,4},{6,7},{7,6},{8,9},{9,8},{10,11... | collective-permute-start | bytes 1437704 | tf_op jit(solution)/shard_map/ppermute | solution.py:62
  47.2 2.6 %collective-permute-done.7.w1 = bf16[192,1536]{1,0:T(8,128)(2,1)S(1)} collective-permute-done((bf16[192,1536]{1,0:T(8,128)(2,1)S(1)}, bf16[192,1536]{1,0:T(8,128)(2,1)S(1)}, u32[]{:S(2)}, u32[]{:S(2)}) %collective-permute-start.7) | collective-permute-done | bytes 589856 | tf_op jit(solution)/shard_map/ppermute | solution.py:62
  49.8 5.8 %collective-permute-start.8 = (bf16[624,384]{1,0:T(8,128)(2,1)S(1)}, bf16[624,384]{1,0:T(8,128)(2,1)S(1)}, u32[]{:S(2)}, u32[]{:S(2)}) collective-permute-start(bf16[624,384]{1,0:T(8,128)(2,1)S(1)} %add.71), channel_id=1, source_target_pairs={{0,2},{1,3},{2,0},{3,1},{4,6},{5,7},{6,4},{7,5},{8,10},{9,11},{10,... | collective-permute-start | bytes 1437704 | tf_op jit(solution)/shard_map/ppermute | solution.py:62
  55.6 11.0 %collective-permute-done.8 = bf16[624,384]{1,0:T(8,128)(2,1)S(1)} collective-permute-done((bf16[624,384]{1,0:T(8,128)(2,1)S(1)}, bf16[624,384]{1,0:T(8,128)(2,1)S(1)}, u32[]{:S(2)}, u32[]{:S(2)}) %collective-permute-start.8) | collective-permute-done | bytes 479264 | tf_op jit(solution)/shard_map/ppermute | solution.py:62
  66.9 1.8 %collective-permute-done.11.two.mid_two = bf16[624,384]{1,0:T(8,128)(2,1)S(1)} collective-permute-done((bf16[624,384]{1,0:T(8,128)(2,1)S(1)}, bf16[624,384]{1,0:T(8,128)(2,1)S(1)}, u32[]{:S(2)}, u32[]{:S(2)}) %collective-permute-start.11) | collective-permute-done | bytes 479264 | tf_op jit(solution)/shard_map/ppermute | solution.py:62
  68.7 7.3 %shard_map.298 = (bf16[624,768]{1,0:T(8,128)(2,1)}, bf16[624,768]{1,0:T(8,128)(2,1)}, bf16[624,768]{1,0:T(8,128)(2,1)}, bf16[624,384]{1,0:T(8,128)(2,1)S(1)}, bf...) custom-call(s32[2]{0:T(128)S(1)} %pad_add_fusion.ids, bf16[624,768]{1,0:T(8,128)(2,1)} %get-tuple-element.76.tokens, ...), custom_call_target="tpu_custom_call" | custom-call | flops 1 | bytes 1 | tf_op jit(solution)/shard_map/pallas_call | solution.py:399
  76.3 1.6 collective-permute-done.12
  78.6 5.1 %shard_map.299 = (bf16[192,1536]{1,0:T(8,128)(2,1)S(1)}, bf16[192,1536]{1,0:T(8,128)(2,1)S(1)}, bf16[192,1536]{1,0:T(8,128)(2,1)S(1)}, bf16[192,1536]{1,0:T(8,128)(2,1)}) custom-call(s32[2]{0:T(128)S(1)} %pad_add_fusion.ids, bf16[624,768]{1,0:T(8,128)(2,1)} %get-tuple-element.83.cot, bf16[624,768]{1,0:T(8,128)(2,1)} %get-tuple-element.91.hidden, ...), custom_call_target="tpu_custom_call" | custom-call | flops 1 | bytes 1 | tf_op jit(solution)/shard_map/pallas_call | solution.py:399
  83.8 4.3 %shard_map.300 = (bf16[624,384]{1,0:T(8,128)(2,1)S(1)}, bf16[624,384]{1,0:T(8,128)(2,1)S(1)}) custom-call(s32[2]{0:T(128)S(1)} %pad_add_fusion.ids, bf16[624,768]{1,0:T(8,128)(2,1)} %get-tuple-element.91.hidden, bf16[192,1536]{1,0:T(8,128)(2,1)S(1)} %copy-done.6, bf16[192,1536]{1,0:T(8,128)(2,1)} %copy-done.9, bf16[192,1536]{1,0:T(8,128)(2,1)} %collective-permute-done.9.w2, ...), custom_call_target="tpu_custom_call" | custom-call | flops 1 | bytes 1 | tf_op jit(solution)/shard_map/pallas_call | solution.py:399
  89.0 2.1 %collective-permute-done.15 = bf16[624,384]{1,0:T(8,128)(2,1)S(1)} collective-permute-done((bf16[624,384]{1,0:T(8,128)(2,1)S(1)}, bf16[624,384]{1,0:T(8,128)(2,1)S(1)}, u32[]{:S(2)}, u32[]{:S(2)}) %collective-permute-start.15) | collective-permute-done | bytes 479264 | tf_op jit(solution)/shard_map/ppermute | solution.py:62
  93.9 9.6 %shard_map.301 = (bf16[624,768]{1,0:T(8,128)(2,1)}, bf16[624,768]{1,0:T(8,128)(2,1)}, bf16[624,384]{1,0:T(8,128)(2,1)S(1)}, bf16[624,384]{1,0:T(8,128)(2,1)}, f32[4,768]{1,0:T(4,128)S(1)}) custom-call(s32[2]{0:T(128)S(1)} %pad_add_fusion.ids, bf16[624,384]{1,0:T(8,128)(2,1)} %copy-done.11, bf16[624,384]{1,0:T(8,128)(2,1)} %copy-done.12, ...), custom_call_target="tpu_custom_call" | custom-call | flops 1 | bytes 1 | tf_op jit(solution)/shard_map/pallas_call | solution.py:399
  103.6 3.3 %shard_map.302 = (bf16[208,768]{1,0:T(8,128)(2,1)S(1)}, bf16[208,768]{1,0:T(8,128)(2,1)S(1)}, bf16[416,768]{1,0:T(8,128)(2,1)S(1)}) custom-call(s32[2]{0:T(128)S(1)} %pad_add_fusion.ids, bf16[624,768]{1,0:T(8,128)(2,1)} %get-tuple-element.77.first, bf16[624,768]{1,0:T(8,128)(2,1)} %get-tuple-element.99.joined, bf16[624,768]{1,0:T(8,128)(2,1)} %get-tuple-element.100.grad_mid, ...), custom_call_target="tpu_custom_call" | custom-call | flops 1 | bytes 1 | tf_op jit(solution)/shard_map/pallas_call | solution.py:399
  109.8 7.2 %collective-permute-done.17 = bf16[192,1536]{1,0:T(8,128)(2,1)S(1)} collective-permute-done((bf16[192,1536]{1,0:T(8,128)(2,1)S(1)}, bf16[192,1536]{1,0:T(8,128)(2,1)S(1)}, u32[]{:S(2)}, u32[]{:S(2)}) %collective-permute-start.17) | collective-permute-done | bytes 589856 | tf_op jit(solution)/shard_map/ppermute | solution.py:62
  119.2 6.7 %collective-permute-start.20 = (bf16[624,384]{1,0:T(8,128)(2,1)S(1)}, bf16[624,384]{1,0:T(8,128)(2,1)S(1)}, u32[]{:S(2)}, u32[]{:S(2)}) collective-permute-start(bf16[624,384]{1,0:T(8,128)(2,1)S(1)} %add.78), channel_id=1, source_target_pairs={{0,2},{1,3},{2,0},{3,1},{4,6},{5,7},{6,4},{7,5},{8,10},{9,11},{10,... | collective-permute-start | bytes 1437704 | tf_op jit(solution)/shard_map/ppermute | solution.py:62
  126.0 2.7 %shard_map.303 = bf16[591,768]{1,0:T(8,128)(2,1)} custom-call(s32[2]{0:T(128)S(1)} %pad_add_fusion.ids, bf16[624,384]{1,0:T(8,128)(2,1)S(1)} %add.75.one, bf16[624,384]{1,0:T(8,128)(2,1)S(1)} %collective-permute-done.19.two, bf16[624,768]{1,0:T(8,128)(2,1)} %get-tuple-element.76.tokens, bf16[624,384]{1,0:T(8,128)(2,1)S(1)} %copy-done.1, ...), custom_call_target="tpu_custom_call" | custom-call | flops 1 | bytes 1 | tf_op jit(solution)/shard_map/pallas_call | solution.py:399
  132.8 3.4 %collective-permute-done.20 = bf16[624,384]{1,0:T(8,128)(2,1)S(1)} collective-permute-done((bf16[624,384]{1,0:T(8,128)(2,1)S(1)}, bf16[624,384]{1,0:T(8,128)(2,1)S(1)}, u32[]{:S(2)}, u32[]{:S(2)}) %collective-permute-start.20) | collective-permute-done | bytes 479264 | tf_op jit(solution)/shard_map/ppermute | solution.py:62
  136.5 2.1 %collective-permute-start.33 = (bf16[192,1536]{1,0:T(8,128)(2,1)S(1)}, bf16[192,1536]{1,0:T(8,128)(2,1)S(1)}, u32[]{:S(2)}, u32[]{:S(2)}) collective-permute-start(bf16[192,1536]{1,0:T(8,128)(2,1)S(1)} %add.83), channel_id=1, source_target_pairs={{0,16},{16,0},{1,17},{17,1},{2,18},{18,2},{3,19},{19,3},{4,20},{20... | collective-permute-start | bytes 1769480 | tf_op jit(solution)/shard_map/ppermute | solution.py:62
  140.5 3.8 %shard_map.304 = (bf16[591,768]{1,0:T(8,128)(2,1)}, f32[2,768]{1,0:T(2,128)S(1)}) custom-call(s32[2]{0:T(128)S(1)} %pad_add_fusion.ids, bf16[624,384]{1,0:T(8,128)(2,1)S(1)} %add.79.one, bf16[320,384]{1,0:T(8,128)(2,1)S(1)} %collective-permute-done.25.upper, bf16[304,384]{1,0:T(8,128)(2,1)S(1)} %collective-permute-done.26.lower, ...), custom_call_target="tpu_custom_call" | custom-call | flops 1 | bytes 1 | tf_op jit(solution)/shard_map/pallas_call | solution.py:399
  144.2 1.9 %collective-permute-done.27 = bf16[208,768]{1,0:T(8,128)(2,1)S(1)} collective-permute-done((bf16[208,768]{1,0:T(8,128)(2,1)S(1)}, bf16[208,768]{1,0:T(8,128)(2,1)S(1)}, u32[]{:S(2)}, u32[]{:S(2)}) %collective-permute-start.27) | collective-permute-done | bytes 319520 | tf_op jit(solution)/shard_map/ppermute | solution.py:51
  146.2 5.9 %collective-permute-start.32 = (bf16[208,768]{1,0:T(8,128)(2,1)S(1)}, bf16[208,768]{1,0:T(8,128)(2,1)S(1)}, u32[]{:S(2)}, u32[]{:S(2)}) collective-permute-start(bf16[208,768]{1,0:T(8,128)(2,1)S(1)} %add.84.one), channel_id=1, source_target_pairs={{0,16},{16,0},{1,17},{17,1},{2,18},{18,2},{3,19},{19,3},{4,20},{20... | collective-permute-start | bytes 958472 | tf_op jit(solution)/shard_map/ppermute | solution.py:62
  152.2 3.6 %collective-permute-done.29 = f32[2,768]{1,0:T(2,128)S(1)} collective-permute-done((f32[2,768]{1,0:T(2,128)S(1)}, f32[2,768]{1,0:T(2,128)S(1)}, u32[]{:S(2)}, u32[]{:S(2)}) %collective-permute-start.29) | collective-permute-done | bytes 6176 | tf_op jit(solution)/shard_map/ppermute | solution.py:62
  155.8 2.4 %collective-permute-start.30 = (f32[2,768]{1,0:T(2,128)S(1)}, f32[2,768]{1,0:T(2,128)S(1)}, u32[]{:S(2)}, u32[]{:S(2)}) collective-permute-start(f32[2,768]{1,0:T(2,128)S(1)} %add.85), channel_id=1, source_target_pairs={{0,8},{4,12},{8,0},{12,4},{1,9},{5,13},{9,1},{13,5},{2,10},{6,14},... | collective-permute-start | bytes 18440 | tf_op jit(solution)/shard_map/ppermute | solution.py:62
  158.2 2.2 %collective-permute-done.30 = f32[2,768]{1,0:T(2,128)S(1)} collective-permute-done((f32[2,768]{1,0:T(2,128)S(1)}, f32[2,768]{1,0:T(2,128)S(1)}, u32[]{:S(2)}, u32[]{:S(2)}) %collective-permute-start.30) | collective-permute-done | bytes 6176 | tf_op jit(solution)/shard_map/ppermute | solution.py:62
  160.9 3.1 %collective-permute-done.31 = f32[2,768]{1,0:T(2,128)S(1)} collective-permute-done((f32[2,768]{1,0:T(2,128)S(1)}, f32[2,768]{1,0:T(2,128)S(1)}, u32[]{:S(2)}, u32[]{:S(2)}) %collective-permute-start.31) | collective-permute-done | bytes 6176 | tf_op jit(solution)/shard_map/ppermute | solution.py:62
  (143 shorter events, 28.5 us)
Async XLA Ops:
  3.1 10.5 %collective-permute-start = (bf16[192,768]{1,0:T(8,128)(2,1)S(1)}, bf16[192,768]{1,0:T(8,128)(2,1)S(1)}, u32[]{:S(2)}, u32[]{:S(2)}) collective-permute-start(bf16[192,768]{1,0:T(8,128)(2,1)S(1)} %concatenate.12), channel_id=1, source_target_pairs={{2,0},{11,1},{4,2},{13,3},{6,4},{15,5},{0,6},{9,7},{10,8},{3,9},{1... | collective-permute-start | bytes 884744 | tf_op jit(solution)/shard_map/ppermute | solution.py:48
  7.1 6.5 %collective-permute-start.2 = (bf16[192,768]{1,0:T(8,128)(2,1)S(1)}, bf16[192,768]{1,0:T(8,128)(2,1)S(1)}, u32[]{:S(2)}, u32[]{:S(2)}) collective-permute-start(bf16[192,768]{1,0:T(8,128)(2,1)S(1)} %concatenate.12), channel_id=1, source_target_pairs={{0,0},{9,1},{6,2},{15,3},{4,4},{13,5},{2,6},{11,7},{8,8},{1,9},{14... | collective-permute-start | bytes 884744 | tf_op jit(solution)/shard_map/ppermute | solution.py:48
  13.6 20.4 %collective-permute-start.6 = (bf16[192,1536]{1,0:T(8,128)(2,1)}, bf16[192,1536]{1,0:T(8,128)(2,1)S(1)}, u32[]{:S(2)}, u32[]{:S(2)}) collective-permute-start(bf16[192,1536]{1,0:T(8,128)(2,1)} %pad_maximum_fusion), channel_id=1, source_target_pairs={{2,0},{11,1},{4,2},{13,3},{6,4},{15,5},{0,6},{9,7},{10,8},{3,9},{1... | collective-permute-start | bytes 1769480 | tf_op jit(solution)/shard_map/ppermute | solution.py:48
  19.5 17.7 %collective-permute-start.4 = (f32[1152]{0:T(1024)S(1)}, f32[1152]{0:T(1024)S(1)}, u32[]{:S(2)}, u32[]{:S(2)}) collective-permute-start(f32[1152]{0:T(1024)S(1)} %concatenate.13), channel_id=1, source_target_pairs={{0,0},{9,1},{6,2},{15,3},{4,4},{13,5},{2,6},{11,7},{8,8},{1,9},{14... | collective-permute-start | bytes 13832 | tf_op jit(solution)/shard_map/ppermute | solution.py:58
  20.3 17.1 %collective-permute-start.1 = (bf16[192,768]{1,0:T(8,128)(2,1)S(1)}, bf16[192,768]{1,0:T(8,128)(2,1)S(1)}, u32[]{:S(2)}, u32[]{:S(2)}) collective-permute-start(bf16[192,768]{1,0:T(8,128)(2,1)S(1)} %collective-permute-done.h0), channel_id=1, source_target_pairs={{0,16},{16,0},{1,17},{17,1},{2,18},{18,2},{3,19},{19,3},{4,20},{20... | collective-permute-start | bytes 884744 | tf_op jit(solution)/shard_map/ppermute | solution.py:62
  24.4 13.0 %collective-permute-start.3 = (bf16[192,768]{1,0:T(8,128)(2,1)S(1)}, bf16[192,768]{1,0:T(8,128)(2,1)S(1)}, u32[]{:S(2)}, u32[]{:S(2)}) collective-permute-start(bf16[192,768]{1,0:T(8,128)(2,1)S(1)} %collective-permute-done.2.h2), channel_id=1, source_target_pairs={{0,16},{16,0},{1,17},{17,1},{2,18},{18,2},{3,19},{19,3},{4,20},{20... | collective-permute-start | bytes 884744 | tf_op jit(solution)/shard_map/ppermute | solution.py:62
  28.0 17.4 %collective-permute-start.9 = (bf16[192,1536]{1,0:T(8,128)(2,1)}, bf16[192,1536]{1,0:T(8,128)(2,1)}, u32[]{:S(2)}, u32[]{:S(2)}) collective-permute-start(bf16[192,1536]{1,0:T(8,128)(2,1)} %pad_maximum_fusion), channel_id=1, source_target_pairs={{0,0},{9,1},{6,2},{15,3},{4,4},{13,5},{2,6},{11,7},{8,8},{1,9},{14... | collective-permute-start | bytes 1769480 | tf_op jit(solution)/shard_map/ppermute | solution.py:48
  34.0 15.8 %collective-permute-start.7 = (bf16[192,1536]{1,0:T(8,128)(2,1)S(1)}, bf16[192,1536]{1,0:T(8,128)(2,1)S(1)}, u32[]{:S(2)}, u32[]{:S(2)}) collective-permute-start(bf16[192,1536]{1,0:T(8,128)(2,1)S(1)} %collective-permute-done.6.w0), channel_id=1, source_target_pairs={{0,16},{16,0},{1,17},{17,1},{2,18},{18,2},{3,19},{19,3},{4,20},{20... | collective-permute-start | bytes 1769480 | tf_op jit(solution)/shard_map/ppermute | solution.py:62
  43.5 3.6 %collective-permute-start.5 = (bf16[624,384]{1,0:T(8,128)(2,1)}, bf16[624,384]{1,0:T(8,128)(2,1)S(1)}, u32[]{:S(2)}, u32[]{:S(2)}) collective-permute-start(bf16[624,384]{1,0:T(8,128)(2,1)} %get-tuple-element.79), channel_id=1, source_target_pairs={{0,1},{1,0},{2,3},{3,2},{4,5},{5,4},{6,7},{7,6},{8,9},{9,8},{10,11... | collective-permute-start | bytes 1437704 | tf_op jit(solution)/shard_map/ppermute | solution.py:62
  45.4 21.3 %collective-permute-start.10 = (bf16[192,1536]{1,0:T(8,128)(2,1)}, bf16[192,1536]{1,0:T(8,128)(2,1)S(1)}, u32[]{:S(2)}, u32[]{:S(2)}) collective-permute-start(bf16[192,1536]{1,0:T(8,128)(2,1)} %collective-permute-done.9.w2), channel_id=1, source_target_pairs={{0,16},{16,0},{1,17},{17,1},{2,18},{18,2},{3,19},{19,3},{4,20},{20... | collective-permute-start | bytes 1769480 | tf_op jit(solution)/shard_map/ppermute | solution.py:62
  49.8 16.8 %collective-permute-start.8 = (bf16[624,384]{1,0:T(8,128)(2,1)S(1)}, bf16[624,384]{1,0:T(8,128)(2,1)S(1)}, u32[]{:S(2)}, u32[]{:S(2)}) collective-permute-start(bf16[624,384]{1,0:T(8,128)(2,1)S(1)} %add.71), channel_id=1, source_target_pairs={{0,2},{1,3},{2,0},{3,1},{4,6},{5,7},{6,4},{7,5},{8,10},{9,11},{10,... | collective-permute-start | bytes 1437704 | tf_op jit(solution)/shard_map/ppermute | solution.py:62
  66.8 1.9 %collective-permute-start.11 = (bf16[624,384]{1,0:T(8,128)(2,1)S(1)}, bf16[624,384]{1,0:T(8,128)(2,1)S(1)}, u32[]{:S(2)}, u32[]{:S(2)}) collective-permute-start(bf16[624,384]{1,0:T(8,128)(2,1)S(1)} %add.72.one.mid_one), channel_id=1, source_target_pairs={{0,1},{1,0},{2,3},{3,2},{4,5},{5,4},{6,7},{7,6},{8,9},{9,8},{10,11... | collective-permute-start | bytes 1437704 | tf_op jit(solution)/shard_map/ppermute | solution.py:62
  76.0 1.9 %collective-permute-start.12 = (bf16[624,384]{1,0:T(8,128)(2,1)S(1)}, bf16[624,384]{1,0:T(8,128)(2,1)S(1)}, u32[]{:S(2)}, u32[]{:S(2)}) collective-permute-start(bf16[624,384]{1,0:T(8,128)(2,1)S(1)} %get-tuple-element.86), channel_id=1, source_target_pairs={{0,1},{1,0},{2,3},{3,2},{4,5},{5,4},{6,7},{7,6},{8,9},{9,8},{10,11... | collective-permute-start | bytes 1437704 | tf_op jit(solution)/shard_map/ppermute | solution.py:62
  78.0 13.1 %collective-permute-start.15 = (bf16[624,384]{1,0:T(8,128)(2,1)S(1)}, bf16[624,384]{1,0:T(8,128)(2,1)S(1)}, u32[]{:S(2)}, u32[]{:S(2)}) collective-permute-start(bf16[624,384]{1,0:T(8,128)(2,1)S(1)} %add.73), channel_id=1, source_target_pairs={{0,2},{1,3},{2,0},{3,1},{4,6},{5,7},{6,4},{7,5},{8,10},{9,11},{10,... | collective-permute-start | bytes 1437704 | tf_op jit(solution)/shard_map/ppermute | solution.py:62
  88.1 3.3 %collective-permute-start.13 = (bf16[624,384]{1,0:T(8,128)(2,1)S(1)}, bf16[624,384]{1,0:T(8,128)(2,1)S(1)}, u32[]{:S(2)}, u32[]{:S(2)}) collective-permute-start(bf16[624,384]{1,0:T(8,128)(2,1)S(1)} %get-tuple-element.93), channel_id=1, source_target_pairs={{0,1},{1,0},{2,3},{3,2},{4,5},{5,4},{6,7},{7,6},{8,9},{9,8},{10,11... | collective-permute-start | bytes 1437704 | tf_op jit(solution)/shard_map/ppermute | solution.py:62
  88.2 19.8 %collective-permute-start.21 = (bf16[192,1536]{1,0:T(8,128)(2,1)S(1)}, bf16[192,1536]{1,0:T(8,128)(2,1)S(1)}, u32[]{:S(2)}, u32[]{:S(2)}) collective-permute-start(bf16[192,1536]{1,0:T(8,128)(2,1)S(1)} %get-tuple-element.112), channel_id=1, source_target_pairs={{0,16},{16,0},{1,17},{17,1},{2,18},{18,2},{3,19},{19,3},{4,20},{20... | collective-permute-start | bytes 1769480 | tf_op jit(solution)/shard_map/ppermute | solution.py:62
  91.2 1.9 %collective-permute-start.16 = (bf16[624,384]{1,0:T(8,128)(2,1)S(1)}, bf16[624,384]{1,0:T(8,128)(2,1)S(1)}, u32[]{:S(2)}, u32[]{:S(2)}) collective-permute-start(bf16[624,384]{1,0:T(8,128)(2,1)S(1)} %add.76.one), channel_id=1, source_target_pairs={{0,1},{1,0},{2,3},{3,2},{4,5},{5,4},{6,7},{7,6},{8,9},{9,8},{10,11... | collective-permute-start | bytes 1437704 | tf_op jit(solution)/shard_map/ppermute | solution.py:62
  91.3 25.7 %collective-permute-start.17 = (bf16[192,1536]{1,0:T(8,128)(2,1)S(1)}, bf16[192,1536]{1,0:T(8,128)(2,1)S(1)}, u32[]{:S(2)}, u32[]{:S(2)}) collective-permute-start(bf16[192,1536]{1,0:T(8,128)(2,1)S(1)} %copy-done.24), channel_id=1, source_target_pairs={{0,16},{16,0},{1,17},{17,1},{2,18},{18,2},{3,19},{19,3},{4,20},{20... | collective-permute-start | bytes 1769480 | tf_op jit(solution)/shard_map/ppermute | solution.py:62
  91.6 18.1 %collective-permute-start.14 = (bf16[624,384]{1,0:T(8,128)(2,1)S(1)}, bf16[624,384]{1,0:T(8,128)(2,1)S(1)}, u32[]{:S(2)}, u32[]{:S(2)}) collective-permute-start(bf16[624,384]{1,0:T(8,128)(2,1)S(1)} %add.74), channel_id=1, source_target_pairs={{0,2},{1,3},{2,0},{3,1},{4,6},{5,7},{6,4},{7,5},{8,10},{9,11},{10,... | collective-permute-start | bytes 1437704 | tf_op jit(solution)/shard_map/ppermute | solution.py:62
  106.9 23.4 %collective-permute-start.23 = (bf16[416,768]{1,0:T(8,128)(2,1)S(1)}, bf16[416,768]{1,0:T(8,128)(2,1)S(1)}, u32[]{:S(2)}, u32[]{:S(2)}) collective-permute-start(bf16[416,768]{1,0:T(8,128)(2,1)S(1)} %get-tuple-element.115), channel_id=1, source_target_pairs={{0,16},{16,0},{1,17},{17,1},{2,18},{18,2},{3,19},{19,3},{4,20},{20... | collective-permute-start | bytes 1916936 | tf_op jit(solution)/shard_map/ppermute | solution.py:62
  108.1 20.5 %collective-permute-start.22 = (bf16[192,1536]{1,0:T(8,128)(2,1)S(1)}, bf16[192,1536]{1,0:T(8,128)(2,1)S(1)}, u32[]{:S(2)}, u32[]{:S(2)}) collective-permute-start(bf16[192,1536]{1,0:T(8,128)(2,1)S(1)} %add.80), channel_id=1, source_target_pairs={{0,2},{1,11},{2,4},{3,13},{4,6},{5,15},{6,0},{7,9},{8,10},{9,3},{1... | collective-permute-start | bytes 1769480 | tf_op jit(solution)/shard_map/ppermute | solution.py:51
  117.3 8.7 %collective-permute-start.19 = (bf16[624,384]{1,0:T(8,128)(2,1)S(1)}, bf16[624,384]{1,0:T(8,128)(2,1)S(1)}, u32[]{:S(2)}, u32[]{:S(2)}) collective-permute-start(bf16[624,384]{1,0:T(8,128)(2,1)S(1)} %add.75.one), channel_id=1, source_target_pairs={{0,1},{1,0},{2,3},{3,2},{4,5},{5,4},{6,7},{7,6},{8,9},{9,8},{10,11... | collective-permute-start | bytes 1437704 | tf_op jit(solution)/shard_map/ppermute | solution.py:62
  117.8 18.5 %collective-permute-start.24 = (bf16[192,1536]{1,0:T(8,128)(2,1)S(1)}, bf16[192,1536]{1,0:T(8,128)(2,1)S(1)}, u32[]{:S(2)}, u32[]{:S(2)}) collective-permute-start(bf16[192,1536]{1,0:T(8,128)(2,1)S(1)} %add.77), channel_id=1, source_target_pairs={{0,0},{1,9},{2,6},{3,15},{4,4},{5,13},{6,2},{7,11},{8,8},{9,1},{10... | collective-permute-start | bytes 1769480 | tf_op jit(solution)/shard_map/ppermute | solution.py:51
  119.2 16.9 %collective-permute-start.20 = (bf16[624,384]{1,0:T(8,128)(2,1)S(1)}, bf16[624,384]{1,0:T(8,128)(2,1)S(1)}, u32[]{:S(2)}, u32[]{:S(2)}) collective-permute-start(bf16[624,384]{1,0:T(8,128)(2,1)S(1)} %add.78), channel_id=1, source_target_pairs={{0,2},{1,3},{2,0},{3,1},{4,6},{5,7},{6,4},{7,5},{8,10},{9,11},{10,... | collective-permute-start | bytes 1437704 | tf_op jit(solution)/shard_map/ppermute | solution.py:62
  130.3 15.8 %collective-permute-start.27 = (bf16[208,768]{1,0:T(8,128)(2,1)S(1)}, bf16[208,768]{1,0:T(8,128)(2,1)S(1)}, u32[]{:S(2)}, u32[]{:S(2)}) collective-permute-start(bf16[208,768]{1,0:T(8,128)(2,1)S(1)} %slice_add_fusion.1), channel_id=1, source_target_pairs={{0,2},{1,11},{2,4},{3,13},{4,6},{5,15},{6,0},{7,9},{8,10},{9,3},{1... | collective-permute-start | bytes 958472 | tf_op jit(solution)/shard_map/ppermute | solution.py:51
  131.9 14.2 %collective-permute-start.28 = (bf16[208,768]{1,0:T(8,128)(2,1)S(1)}, bf16[208,768]{1,0:T(8,128)(2,1)S(1)}, u32[]{:S(2)}, u32[]{:S(2)}) collective-permute-start(bf16[208,768]{1,0:T(8,128)(2,1)S(1)} %slice_add_fusion), channel_id=1, source_target_pairs={{0,0},{1,9},{2,6},{3,15},{4,4},{5,13},{6,2},{7,11},{8,8},{9,1},{10... | collective-permute-start | bytes 958472 | tf_op jit(solution)/shard_map/ppermute | solution.py:51
  136.5 29.7 %collective-permute-start.33 = (bf16[192,1536]{1,0:T(8,128)(2,1)S(1)}, bf16[192,1536]{1,0:T(8,128)(2,1)S(1)}, u32[]{:S(2)}, u32[]{:S(2)}) collective-permute-start(bf16[192,1536]{1,0:T(8,128)(2,1)S(1)} %add.83), channel_id=1, source_target_pairs={{0,16},{16,0},{1,17},{17,1},{2,18},{18,2},{3,19},{19,3},{4,20},{20... | collective-permute-start | bytes 1769480 | tf_op jit(solution)/shard_map/ppermute | solution.py:62
  138.6 1.9 %collective-permute-start.25 = (bf16[320,384]{1,0:T(8,128)(2,1)S(1)}, bf16[320,384]{1,0:T(8,128)(2,1)S(1)}, u32[]{:S(2)}, u32[]{:S(2)}) collective-permute-start(bf16[320,384]{1,0:T(8,128)(2,1)S(1)} %slice.50), channel_id=1, source_target_pairs={{0,1},{1,0},{2,3},{3,2},{4,5},{5,4},{6,7},{7,6},{8,9},{9,8},{10,11... | collective-permute-start | bytes 737288 | tf_op jit(solution)/shard_map/ppermute | solution.py:62
  146.2 18.4 %collective-permute-start.32 = (bf16[208,768]{1,0:T(8,128)(2,1)S(1)}, bf16[208,768]{1,0:T(8,128)(2,1)S(1)}, u32[]{:S(2)}, u32[]{:S(2)}) collective-permute-start(bf16[208,768]{1,0:T(8,128)(2,1)S(1)} %add.84.one), channel_id=1, source_target_pairs={{0,16},{16,0},{1,17},{17,1},{2,18},{18,2},{3,19},{19,3},{4,20},{20... | collective-permute-start | bytes 958472 | tf_op jit(solution)/shard_map/ppermute | solution.py:62
  152.2 3.6 %collective-permute-start.29 = (f32[2,768]{1,0:T(2,128)S(1)}, f32[2,768]{1,0:T(2,128)S(1)}, u32[]{:S(2)}, u32[]{:S(2)}) collective-permute-start(f32[2,768]{1,0:T(2,128)S(1)} %get-tuple-element.123), channel_id=1, source_target_pairs={{0,4},{4,0},{8,12},{12,8},{1,5},{5,1},{9,13},{13,9},{2,6},{6,2},{1... | collective-permute-start | bytes 18440 | tf_op jit(solution)/shard_map/ppermute | solution.py:62
  155.8 4.5 %collective-permute-start.30 = (f32[2,768]{1,0:T(2,128)S(1)}, f32[2,768]{1,0:T(2,128)S(1)}, u32[]{:S(2)}, u32[]{:S(2)}) collective-permute-start(f32[2,768]{1,0:T(2,128)S(1)} %add.85), channel_id=1, source_target_pairs={{0,8},{4,12},{8,0},{12,4},{1,9},{5,13},{9,1},{13,5},{2,10},{6,14},... | collective-permute-start | bytes 18440 | tf_op jit(solution)/shard_map/ppermute | solution.py:62
  160.3 3.6 %collective-permute-start.31 = (f32[2,768]{1,0:T(2,128)S(1)}, f32[2,768]{1,0:T(2,128)S(1)}, u32[]{:S(2)}, u32[]{:S(2)}) collective-permute-start(f32[2,768]{1,0:T(2,128)S(1)} %add.86), channel_id=1, source_target_pairs={{0,16},{16,0},{1,17},{17,1},{2,18},{18,2},{3,19},{19,3},{4,20},{20... | collective-permute-start | bytes 18440 | tf_op jit(solution)/shard_map/ppermute | solution.py:62
  (28 other events, 301.8 us)
